TPU v7x, 128 devices: a whole 4x4x4 slice. The times are simulated.
128 devices in a mesh: tp: 4 (over z_lo, core), cp: 32 (over x, z_hi, y).
Axes of the slice: x: 4, y: 4, z: 4 (z_hi: 2, z_lo: 2; z = z_hi * 2 + z_lo), core: 2. Of those that a mesh axis runs over, the one named last changes fastest.
Arguments:
- grad_out: bfloat16 [4, 4096, 4096], P('tp', 'cp'), may hold values from -6 to 6
- expert_ids: int32 [4, 4096, 8], P('tp', 'cp'), may hold values from 0 to 127, all different within a row; in each aligned block of 128 rows (0 to 127, 128 to 255, ..., all dimensions but the last counted through in order) at most 10 rows name the same one
- route_prob: bfloat16 [4, 4096, 8], P('tp', 'cp'), may hold values from 0.049804688 to 0.5
- attn_out: bfloat16 [16384, 4096], P('cp', 'tp'), may hold values from -0.046875 to 0.046875
- w_down: bfloat16 [128, 768, 4096], P(('tp', 'cp')), may hold values from -0.09375 to 0.09375
- hidden_saved: bfloat16 [128, 1280, 768], P(('tp', 'cp')), may hold values from -0.21875 to 0.21875
Outputs:
- grad_prob: float32 [4, 4096, 8], P('tp', 'cp')
- grad_hidden: bfloat16 [128, 1280, 768], P(('tp', 'cp'))
- grad_down: bfloat16 [128, 768, 4096], P(('tp', 'cp'))
- grad_oproj: bfloat16 [4096, 4096], P('cp', 'tp')
Inputs may be any that keep to these rules, and one draw needn't show every extreme that they name: `expert_ids`: within each device's block of 128 tokens, no expert is named by more than 10 routes, and in every draw some expert is named by exactly 10; every expert is named somewhere.
All inputs are finite; a program needn't handle non-finite values.
Results may differ from a plain program's by a relative error of at most 0.0049.
Values may be sent and summed in bfloat16 or wider, within the bound.
No kernel may reach another device: no remote copies, remote signals or barrier semaphores. Data moves between devices by JAX's collectives and lax.ppermute only.
A program may use at most 192 MiB of HBM per device.

v0:
```python
import jax
import jax.numpy as jnp
from jax import lax
from jax.sharding import PartitionSpec as P


def local(grad_out, expert_ids, route_prob, attn_out, w_down, hidden_saved):
    tp_count = lax.axis_size("tp")
    cp_count = lax.axis_size("cp")
    n_experts = tp_count * cp_count
    slot_count = hidden_saved.shape[1]
    capacity = slot_count // n_experts
    local_rows = grad_out[0]
    token_count = local_rows.shape[0]
    width = local_rows.shape[1]
    top_count = expert_ids.shape[2]
    route_ids = expert_ids[0].reshape(-1)
    onehot = (route_ids[:, None] == jnp.arange(n_experts, dtype=jnp.int32)[None, :]).astype(
        jnp.int32
    )
    position = jnp.sum((jnp.cumsum(onehot, axis=0) - 1) * onehot, axis=1)
    target = route_ids * capacity + position
    token_of = jnp.arange(token_count * top_count, dtype=jnp.int32) // top_count
    send_rows = (
        jnp.zeros((n_experts * capacity, width), jnp.bfloat16).at[target].set(local_rows[token_of])
    )
    send_prob = (
        jnp.zeros((n_experts * capacity,), jnp.bfloat16).at[target].set(route_prob[0].reshape(-1))
    )
    got_rows, got_prob = (
        lax.all_to_all(
            send_rows.reshape(n_experts, capacity, width),
            ("tp", "cp"),
            split_axis=0,
            concat_axis=0,
            tiled=True,
        ),
        lax.all_to_all(
            send_prob.reshape(n_experts, capacity),
            ("tp", "cp"),
            split_axis=0,
            concat_axis=0,
            tiled=True,
        ),
    )
    routed = got_rows.reshape(slot_count, width)
    weight = got_prob.reshape(slot_count).astype(jnp.float32)[:, None]
    expert_weight = w_down[0]
    saved = hidden_saved[0]
    proj = lax.dot_general(
        routed, expert_weight, (((1,), (1,)), ((), ())), preferred_element_type=jnp.float32
    )
    grad_hid = (weight * proj).astype(jnp.bfloat16)
    prob_part = jnp.sum(proj * saved.astype(jnp.float32), axis=1)
    weighted = (weight * routed.astype(jnp.float32)).astype(jnp.bfloat16)
    grad_w = lax.dot_general(
        saved, weighted, (((0,), (0,)), ((), ())), preferred_element_type=jnp.float32
    ).astype(jnp.bfloat16)
    returned = lax.all_to_all(
        prob_part.reshape(n_experts, capacity),
        ("tp", "cp"),
        split_axis=0,
        concat_axis=0,
        tiled=True,
    )
    grad_prob = returned.reshape(-1)[target].reshape(1, token_count, top_count)
    gathered = lax.all_gather(grad_out, "tp", axis=0, tiled=True).reshape(-1, width)
    grad_oproj = lax.psum_scatter(
        lax.dot_general(
            gathered, attn_out, (((0,), (0,)), ((), ())), preferred_element_type=jnp.float32
        ),
        "cp",
        scatter_dimension=0,
        tiled=True,
    ).astype(jnp.bfloat16)
    return (grad_prob, grad_hid[None], grad_w[None], grad_oproj)


def solution(mesh):
    in_specs = (
        P("tp", "cp", None),
        P("tp", "cp", None),
        P("tp", "cp", None),
        P("cp", "tp"),
        P(("tp", "cp"), None, None),
        P(("tp", "cp"), None, None),
    )
    out_specs = (
        P("tp", "cp", None),
        P(("tp", "cp"), None, None),
        P(("tp", "cp"), None, None),
        P("cp", "tp"),
    )
    return jax.shard_map(local, mesh=mesh, in_specs=in_specs, out_specs=out_specs, check_vma=False)
```

profile of v0, /device:TPU:1, one launch (start us, length us, event | category | flops | bytes accessed | tf_op | source)
XLA Modules:
  0.0 673.5 jit_solution(8308457495964636281)
XLA Ops:
  7.2 0.0 copy-start
  7.2 0.0 all-gather.2.cloned.1.call-start
  7.2 0.7 all-gather.2.cloned.1.call-update
  7.9 0.0 reduce-scatter.2.cloned.1.call-start
  8.0 52.0 %all-gather.2.cloned.1.call-done = bf16[4,128,4096]{2,1,0:T(8,128)(2,1)} async-done(((bf16[1,128,4096]{2,1,0:T(8,128)(2,1)}), bf16[4,128,4096]{2,1,0:T(8,128)(2,1)}) %all-gather.2.cloned.1.call-update) | async-done | bytes 4194320 | tf_op jit(solution)/shard_map/all_gather | solution.py:67
  60.0 10.4 %fusion.15 = f32[4096,1024]{1,0:T(8,128)} fusion(bf16[512,4096]{1,0:T(8,128)(2,1)} %bitcast.42, bf16[512,1024]{1,0:T(8,128)(2,1)S(1)} %copy-done), kind=kOutput, calls=%fused_computation.36 | convolution fusion | flops 4294967296 | bytes 22020096 | tf_op jit(solution)/shard_map/dot_general | solution.py:69
  70.3 0.0 reduce-scatter.2.cloned.1.call-update
  70.4 0.7 copy-done.4
  71.0 0.1 copy.24
  71.1 0.1 eq.29
  71.2 0.1 eq.25
  71.3 0.1 copy.26
  71.4 0.2 fusion.8
  71.7 0.1 copy.27
  71.8 0.1 copy.23
  71.9 0.1 mul.41
  72.0 0.1 copy.30
  72.1 0.1 reshape.176
  72.3 0.4 fusion.7
  72.6 7.6 %scatter_custom_fusion.1 = bf16[1280]{0:T(1024)(128)(2,1)S(1)} fusion(s32[1024]{0:T(1024)S(1)} %bitcast.38, bf16[1024]{0:T(1024)(128)(2,1)S(1)} %reshape.176, bf16[]{:T(256)} %constant.27.clone.1), kind=kCustom, calls=%fused_computation.32 | custom fusion | bytes 2562 | tf_op jit(solution)/shard_map/scatter | solution.py:28
  80.2 0.8 all_to_all.20
  81.0 8.7 %all-to-all-start.2 = ((bf16[128,1,10]{2,1,0:T(2,128)(2,1)}), bf16[128,1,10]{2,1,0:T(2,128)(2,1)S(1)}, u32[]{:S(2)}, u32[]{:S(2)}) async-start(bf16[128,1,10]{2,1,0:T(2,128)(2,1)} %all_to_all.20), calls=%async_computation.2 | async-start | bytes 131072 | tf_op jit(solution)/shard_map/all_to_all | solution.py:38
  89.8 7.8 %gather_fusion = bf16[1024,4096]{1,0:T(8,128)(2,1)} fusion(bf16[128,4096]{1,0:T(8,128)(2,1)S(1)} %bitcast.35, s32[1024]{0:T(1024)S(1)} %broadcast_clamp_fusion.1), kind=kCustom, calls=%fused_computation | custom fusion | bytes 16781312 | tf_op jit(solution)/shard_map/gather | solution.py:25
  97.5 18.9 %scatter_custom_fusion = bf16[1280,4096]{1,0:T(8,128)(2,1)} fusion(s32[1024]{0:T(1024)S(1)} %bitcast.39, bf16[1024,4096]{1,0:T(8,128)(2,1)} %gather_fusion, bf16[]{:T(256)} %constant.27.clone.1), kind=kCustom, calls=%fused_computation.9 | custom fusion | bytes 10486272 | tf_op jit(solution)/shard_map/scatter | solution.py:25
  116.4 15.3 %reshape.141 = bf16[128,10,4096]{2,1,0:T(8,128)(2,1)} reshape(bf16[1280,4096]{1,0:T(8,128)(2,1)} %scatter_custom_fusion) | data formatting | bytes 20971520 | tf_op jit(solution)/shard_map/reshape | solution.py:32
  131.7 0.0 all-to-all-done.2
  131.7 10.6 %all-to-all-start = ((bf16[128,10,4096]{2,1,0:T(8,128)(2,1)}), bf16[128,10,4096]{2,1,0:T(8,128)(2,1)}, u32[]{:S(2)}, u32[]{:S(2)}) async-start(bf16[128,10,4096]{2,1,0:T(8,128)(2,1)} %reshape.141), calls=%async_computation | async-start | bytes 33554432 | tf_op jit(solution)/shard_map/all_to_all | solution.py:31
  142.3 2.3 copy.28
  144.5 0.2 convert_reduce_fusion
  144.7 0.1 reshape.146
  144.8 0.1 convert_element_type.59
  144.9 383.0 %all-to-all-done = bf16[128,10,4096]{2,1,0:T(8,128)(2,1)} async-done(((bf16[128,10,4096]{2,1,0:T(8,128)(2,1)}), bf16[128,10,4096]{2,1,0:T(8,128)(2,1)}, u32[]{:S(2)}, u32[]{:S(2)}) %all-to-all-start) | async-done | bytes 10485792 | tf_op jit(solution)/shard_map/all_to_all | solution.py:31
  528.0 16.6 %reshape.142 = bf16[1280,4096]{1,0:T(8,128)(2,1)} reshape(bf16[128,10,4096]{2,1,0:T(8,128)(2,1)} %all-to-all-done) | data formatting | bytes 20971520 | tf_op jit(solution)/shard_map/reshape | solution.py:46
  544.5 14.8 %fusion.5 = (bf16[1,1280,768]{1,2,0:T(8,128)(2,1)}, f32[1280]{0:T(1024)S(1)}) fusion(f32[1280]{0:T(1024)S(1)} %reshape.146, bf16[1,1280,768]{1,2,0:T(8,128)(2,1)} %copy.28, bf16[1280,4096]{1,0:T(8,128)(2,1)} %reshape.142, bf16[1,768,4096]{2,1,0:T(8,128)(2,1)} %param.10), kind=kOutput, calls=%fused_computation.13 | convolution fusion | flops 8057977856 | bytes 20719616 | tf_op jit(solution)/shard_map/dot_general | solution.py:50
  559.3 0.8 all_to_all.16
  560.1 37.1 %all-to-all-start.1 = ((f32[128,1,10]{2,1,0:T(1,128)}), f32[128,1,10]{2,1,0:T(1,128)S(1)}, u32[]{:S(2)}, u32[]{:S(2)}) async-start(f32[128,1,10]{2,1,0:T(1,128)} %bitcast.9), calls=%async_computation.1 | async-start | bytes 131072 | tf_op jit(solution)/shard_map/all_to_all | solution.py:59
  597.2 15.3 %multiply_convert_fusion = bf16[128,10,4096]{2,1,0:T(8,128)(2,1)} fusion(bf16[128,10,4096]{2,1,0:T(8,128)(2,1)} %all-to-all-done, f32[128,10]{1,0:T(8,128)S(1)} %bitcast.36), kind=kLoop, calls=%fused_computation.4 | loop fusion | flops 15728640 | bytes 20976640 | tf_op jit(solution)/shard_map/convert_element_type | solution.py:55
  612.5 16.5 %convert_element_type.55 = bf16[1280,4096]{1,0:T(8,128)(2,1)} reshape(bf16[128,10,4096]{2,1,0:T(8,128)(2,1)} %multiply_convert_fusion) | data formatting | bytes 20971520 | tf_op jit(solution)/shard_map/convert_element_type | solution.py:55
  629.0 14.9 %fusion.2 = bf16[1,768,4096]{1,2,0:T(8,128)(2,1)} fusion(bf16[1280,4096]{1,0:T(8,128)(2,1)} %convert_element_type.55, bf16[1,1280,768]{2,1,0:T(8,128)(2,1)S(1)} %copy-done.3), kind=kOutput, calls=%fused_computation.8 | convolution fusion | flops 8056209408 | bytes 18743296 | tf_op jit(solution)/shard_map/dot_general | solution.py:56
  643.9 4.0 copy.33
  647.9 8.6 %copy.34 = bf16[1,768,4096]{2,1,0:T(8,128)(2,1)} copy(bf16[1,768,4096]{1,2,0:T(8,128)(2,1)} %fusion.2) | data formatting | bytes 12582912
  656.5 0.5 broadcast.139
  657.1 0.8 reduce.7
  657.9 0.1 reshape.143
  658.0 6.2 gather_fusion.1
  664.2 0.1 reshape.144
  664.3 0.7 copy.32
  664.9 1.8 convert_element_type.58
  (21 shorter events, 0.1 us)
Async XLA Ops:
  7.2 52.8 %copy-start = (bf16[512,1024]{1,0:T(8,128)(2,1)S(1)}, bf16[512,1024]{1,0:T(8,128)(2,1)}, u32[]{:S(2)}) copy-start(bf16[512,1024]{1,0:T(8,128)(2,1)} %param.9) | copy-start | bytes 3145732
  7.2 52.8 %all-gather.2.cloned.1.call-start = ((), (), s32[]{:S(2)}) async-start(), calls=%async_computation.4 | async-start | bytes 5242880 | tf_op jit(solution)/shard_map/all_gather | solution.py:67
  7.9 657.0 %reduce-scatter.2.cloned.1.call-start = ((), (), s32[]{:S(2)}) async-start(), calls=%async_computation.5 | async-start | bytes 17301504 | tf_op jit(solution)/shard_map/reduce_scatter | solution.py:68
  70.3 0.7 copy-start.4
  70.3 1.7 copy-start.5
  70.3 19.4 %copy-start.2 = (bf16[1,128,4096]{2,1,0:T(8,128)(2,1)S(1)}, bf16[1,128,4096]{2,1,0:T(8,128)(2,1)}, u32[]{:S(2)}) copy-start(bf16[1,128,4096]{2,1,0:T(8,128)(2,1)} %param.6) | copy-start | bytes 3145732
  81.0 50.6 %all-to-all-start.2 = ((bf16[128,1,10]{2,1,0:T(2,128)(2,1)}), bf16[128,1,10]{2,1,0:T(2,128)(2,1)S(1)}, u32[]{:S(2)}, u32[]{:S(2)}) async-start(bf16[128,1,10]{2,1,0:T(2,128)(2,1)} %all_to_all.20), calls=%async_computation.2 | async-start | bytes 131072 | tf_op jit(solution)/shard_map/all_to_all | solution.py:38
  131.7 10.6 %copy-start.3 = (bf16[1,1280,768]{2,1,0:T(8,128)(2,1)S(1)}, bf16[1,1280,768]{2,1,0:T(8,128)(2,1)}, u32[]{:S(2)}) copy-start(bf16[1,1280,768]{2,1,0:T(8,128)(2,1)} %param.11) | copy-start | bytes 5898244
  131.7 396.3 %all-to-all-start = ((bf16[128,10,4096]{2,1,0:T(8,128)(2,1)}), bf16[128,10,4096]{2,1,0:T(8,128)(2,1)}, u32[]{:S(2)}, u32[]{:S(2)}) async-start(bf16[128,10,4096]{2,1,0:T(8,128)(2,1)} %reshape.141), calls=%async_computation | async-start | bytes 33554432 | tf_op jit(solution)/shard_map/all_to_all | solution.py:31
  560.1 96.5 %all-to-all-start.1 = ((f32[128,1,10]{2,1,0:T(1,128)}), f32[128,1,10]{2,1,0:T(1,128)S(1)}, u32[]{:S(2)}, u32[]{:S(2)}) async-start(f32[128,1,10]{2,1,0:T(1,128)} %bitcast.9), calls=%async_computation.1 | async-start | bytes 131072 | tf_op jit(solution)/shard_map/all_to_all | solution.py:59
  643.9 22.8 %copy-start.1 = (bf16[512,1024]{1,0:T(8,128)(2,1)S(1)}, bf16[512,1024]{1,0:T(8,128)(2,1)}, u32[]{:S(2)}) copy-start(bf16[512,1024]{1,0:T(8,128)(2,1)} %param.9) | copy-start | bytes 3145732
Sparse Core Ops, SparseCore 0:
  9.7 50.2 all-gather.1
  70.5 461.0 reduce-scatter.1
where the time goes:
time: 675 us; the launch traced here: 674 us
  waiting for transfers between devices  436 us (65%)
  local copies, waits for them, and re-layouts  108 us (16%)
  starting transfers between devices  56.5 us (8%)
  matrix products  40 us (6%)
  other arithmetic  18.8 us (3%)
  between operations  14.2 us (2%)
    all_to_all x1, waiting for transfers between devices, local(): lax.all_to_all(send_rows.reshape(n_experts, capacity, width), ('tp', 'cp'...  383 us
    all_gather x1, waiting for transfers between devices, local(): lax.all_gather(grad_out, 'tp', axis=0, tiled=True).reshape(-1, width)  52 us
    all_to_all x1, starting transfers between devices, local(): lax.all_to_all(prob_part.reshape(n_experts, capacity), ('tp', 'cp'), spli...  37.1 us
    scatter x1, local copies, waits for them, and re-layouts, local(): jnp.zeros((n_experts * capacity, width), jnp.bfloat16).at[target]  18.9 us
    reshape x1, local copies, waits for them, and re-layouts, local(): routed = got_rows.reshape(slot_count, width)  16.6 us
    convert_element_type x1, local copies, waits for them, and re-layouts, local(): weighted = (weight * routed.astype(jnp.float32)).astype(jnp.bfloat16)  16.5 us
    unnamed x18, local copies, waits for them, and re-layouts  16.5 us
    convert_element_type x1, other arithmetic, local(): weighted = (weight * routed.astype(jnp.float32)).astype(jnp.bfloat16)  15.3 us
  transfers between devices with their start and end apart: 5, of which 2 were waited for; matrix products, arithmetic and copies ran while one was open for 23% of the time, Pallas kernels for 0%

commit v1 on v0

v1 whole, which is shorter than its diff:
```python
import jax
import jax.numpy as jnp
from jax import lax
from jax.experimental import pallas as pl
from jax.experimental.pallas import tpu as pltpu
from jax.sharding import Mesh
from jax.sharding import PartitionSpec as P

TP = ("zlo", "core")
CP = ("x", "zhi", "y")
ALL = TP + CP
PEERS = ("zlo", "core", "x", "zhi")
CHUNKS = 2
TILE = 512
VMEM = 56 * 1024 * 1024
BF = jnp.bfloat16
F32 = jnp.float32


def params():
    return pltpu.CompilerParams(vmem_limit_bytes=VMEM)


def upper(n):
    return (
        lax.broadcasted_iota(jnp.int32, (n, n), 0) < lax.broadcasted_iota(jnp.int32, (n, n), 1)
    ).astype(BF)


def ranks(member):
    count = jnp.dot(member.astype(BF), upper(member.shape[1]), preferred_element_type=F32)
    return jnp.where(member, count, -1.0)


def place_kernel(y_ref, ids_ref, s_ref):
    y = y_ref[0]
    rows, cols = s_ref.shape
    peers = rows // 40
    expert = lax.broadcasted_iota(jnp.int32, (peers, 128), 0) * 4 + y
    parts = []
    for k in range(4):
        member = ids_ref[k, 0:1, :] == expert
        for i in range(1, 8):
            member = member | (ids_ref[k, i : i + 1, :] == expert)
        parts.append(ranks(member).astype(BF))
    table = jnp.concatenate(parts, axis=1)
    row = lax.broadcasted_iota(jnp.int32, (rows, peers), 0)
    pick = (lax.shift_right_logical(row * 6554, 18) == lax.broadcasted_iota(jnp.int32, (rows, peers), 1)).astype(BF)
    spread = jnp.dot(pick, table, preferred_element_type=F32)
    row = lax.broadcasted_iota(jnp.int32, (rows, cols), 0)
    tenth = lax.shift_right_logical(row * 6554, 16)
    rank = (row - tenth * 10).astype(F32)
    block = lax.shift_right_logical(lax.broadcasted_iota(jnp.int32, (rows, cols), 1), 7)
    origin = jnp.where(block == 0, 0, jnp.where(block == 1, 3, jnp.where(block == 2, 1, 2)))
    here = (tenth & 3) == ((origin + y) & 3)
    s_ref[...] = jnp.where(here & (spread == rank), 1.0, 0.0).astype(BF)


def place(y, ids4, rows):
    return pl.pallas_call(
        place_kernel,
        out_shape=jax.ShapeDtypeStruct((rows, 512), BF),
        in_specs=[
            pl.BlockSpec(memory_space=pltpu.SMEM),
            pl.BlockSpec(memory_space=pltpu.VMEM),
        ],
        out_specs=pl.BlockSpec(memory_space=pltpu.VMEM),
        compiler_params=params(),
        cost_estimate=pl.CostEstimate(flops=10**8, bytes_accessed=2 * 10**6, transcendentals=0),
    )(y, ids4)


def dispatch_kernel(s_ref, g0, g1, g2, g3, g4, o_ref):
    g = jnp.concatenate([g0[...], g1[...], g2[...], g3[...], g4[...]], axis=0)
    o_ref[...] = jnp.dot(s_ref[...], g, preferred_element_type=F32).astype(BF)


def dispatch(s, blocks):
    rows = s.shape[0]
    width = blocks[0].shape[1]
    return pl.pallas_call(
        dispatch_kernel,
        out_shape=jax.ShapeDtypeStruct((rows, width), BF),
        grid=(width // TILE,),
        in_specs=[pl.BlockSpec(s.shape, lambda i: (0, 0))]
        + [pl.BlockSpec((b.shape[0], TILE), lambda i: (0, i)) for b in blocks],
        out_specs=pl.BlockSpec((rows, TILE), lambda i: (0, i)),
        compiler_params=params(),
        cost_estimate=pl.CostEstimate(
            flops=2 * rows * 512 * width, bytes_accessed=2 * rows * width, transcendentals=0
        ),
    )(s, *blocks)


def select_kernel(y_ref, *refs):
    o_ref = refs[-1]
    y = y_ref[0]
    for ref, shift, start in zip(refs[:-1], (0, 3, 1, 2, 2), (0, 0, 0, 0, 64)):
        at = pl.multiple_of(((y + shift) & 3) * 128 + start, 64)
        o_ref[pl.ds(at, ref.shape[0]), :] = ref[...]


def select(y, blocks):
    width = blocks[0].shape[1]
    n = width // 512
    return pl.pallas_call(
        select_kernel,
        out_shape=jax.ShapeDtypeStruct((512, n * 128), BF),
        grid_spec=pltpu.PrefetchScalarGridSpec(
            num_scalar_prefetch=1,
            grid=(n,),
            in_specs=[
                pl.BlockSpec((b.shape[0], 128), lambda i, y_ref: (0, i * 4 + y_ref[0])) for b in blocks
            ],
            out_specs=pl.BlockSpec((512, 128), lambda i, y_ref: (0, i)),
        ),
        compiler_params=params(),
        cost_estimate=pl.CostEstimate(flops=0, bytes_accessed=4 * 512 * n * 128, transcendentals=0),
    )(y, *blocks)


def expert_kernel(first, last, *refs):
    if first:
        routed_ref, w_ref, ht_ref, wt_ref = refs[:4]
        outs = refs[4:]
    else:
        routed_ref, w_ref, ht_ref, wt_ref, before_ref, h_ref = refs[:6]
        outs = refs[7:]
    step = pl.program_id(0)
    if last:
        down_ref, hid_ref, part_ref, proj_ref = outs
    else:
        down_ref, proj_ref = outs
    routed = routed_ref[...]
    term = lax.dot_general(
        routed, w_ref[...], (((1,), (1,)), ((), ())), preferred_element_type=F32
    )

    @pl.when(step == 0)
    def _():
        if first:
            proj_ref[...] = term
        else:
            proj_ref[...] = before_ref[...] + term

    @pl.when(step > 0)
    def _():
        proj_ref[...] += term

    weighted = (wt_ref[...] * routed.astype(F32)).astype(BF)
    down_ref[...] = jnp.dot(ht_ref[...], weighted, preferred_element_type=F32).astype(BF)
    if last:

        @pl.when(step == pl.num_programs(0) - 1)
        def _():
            proj = proj_ref[...]
            hid_ref[...] = (wt_ref[...] * proj).astype(BF)
            part_ref[...] = jnp.sum(proj * h_ref[...].astype(F32), axis=1, keepdims=True)


def expert(chunk, n_chunks, routed, w, hidden_t, weight, proj, hidden, down):
    rows, width = routed.shape
    hid, full = w.shape
    first, last = chunk == 0, chunk == n_chunks - 1
    steps = width // TILE
    base = chunk * steps
    in_specs = [
        pl.BlockSpec((rows, TILE), lambda i: (0, i)),
        pl.BlockSpec((hid, TILE), lambda i: (0, base + i)),
        pl.BlockSpec((hid, rows), lambda i: (0, 0)),
        pl.BlockSpec((rows, 1), lambda i: (0, 0)),
    ]
    args = [routed, w, hidden_t, weight]
    aliases = {}
    if not first:
        in_specs += [
            pl.BlockSpec((rows, hid), lambda i: (0, 0)),
            pl.BlockSpec((rows, hid), lambda i: (0, 0)),
            pl.BlockSpec(memory_space=pl.ANY),
        ]
        args += [proj, hidden, down]
        aliases = {6: 0}
    out_shape = [jax.ShapeDtypeStruct((hid, full), BF)]
    out_specs = [pl.BlockSpec((hid, TILE), lambda i: (0, base + i))]
    scratch = []
    whole = lambda i: (0, 0)
    if last:
        out_shape += [jax.ShapeDtypeStruct((rows, hid), BF), jax.ShapeDtypeStruct((rows, 1), F32)]
        out_specs += [pl.BlockSpec((rows, hid), whole), pl.BlockSpec((rows, 1), whole)]
        scratch = [pltpu.VMEM((rows, hid), F32)]
    else:
        out_shape += [jax.ShapeDtypeStruct((rows, hid), F32)]
        out_specs += [pl.BlockSpec((rows, hid), whole)]

    def kernel(*refs):
        expert_kernel(first, last, *refs)

    return pl.pallas_call(
        kernel,
        out_shape=out_shape,
        grid=(steps,),
        in_specs=in_specs,
        out_specs=out_specs,
        scratch_shapes=scratch,
        input_output_aliases=aliases,
        compiler_params=params(),
        cost_estimate=pl.CostEstimate(
            flops=4 * rows * hid * width, bytes_accessed=2 * (rows + 2 * hid) * width, transcendentals=0
        ),
    )(*args)


def ring(x, shift):
    return lax.ppermute(x, "y", [(i, (i + shift) % 4) for i in range(4)])


def ring_gather(x):
    half = x.shape[0] // 2
    before, after = ring(x, 1), ring(x, -1)
    return [x, before, after, ring(before[:half], 1), ring(after[half:], -1)]


def local(grad_out, expert_ids, route_prob, attn_out, w_down, hidden_saved):
    n_experts = lax.axis_size(ALL)
    slots = hidden_saved.shape[1]
    cap = slots // n_experts
    g = grad_out[0]
    tokens, width = g.shape
    y = lax.axis_index("y").reshape(1)
    chunk = width // CHUNKS
    ids = expert_ids[0].T
    blocks = [ring_gather(g[:, i * chunk : (i + 1) * chunk]) for i in range(CHUNKS)]
    ids4 = jnp.stack([ids, ring(ids, 1), ring(ids, -1), ring(ids, 2)])
    spread = place(y, ids4, slots)
    named = ids[:, None, :] == jnp.arange(n_experts, dtype=jnp.int32)[None, :, None]
    rank = ranks(jnp.any(named, axis=0))
    prob = jnp.sum(jnp.where(named, route_prob[0].T[:, None, :].astype(F32), 0.0), axis=0)
    at = rank[:, None, :] == jnp.arange(cap, dtype=jnp.int32).astype(F32)[None, :, None]
    send_prob = jnp.sum(jnp.where(at, prob[:, None, :], 0.0), axis=2)
    got_prob = lax.all_to_all(
        send_prob.reshape(n_experts, 1, cap), ALL, split_axis=0, concat_axis=0, tiled=True
    )
    weight = got_prob.reshape(slots, 1)
    hidden = hidden_saved[0]
    hidden_t = hidden.T
    w = w_down[0]
    routed = []
    for part in blocks:
        rows = dispatch(spread, part)
        sent = lax.all_to_all(
            rows.reshape(n_experts // 4, 4 * cap, chunk), PEERS, split_axis=0, concat_axis=0, tiled=True
        )
        routed.append(sent.reshape(slots, chunk))
    proj = down = None
    for i in range(CHUNKS):
        out = expert(i, CHUNKS, routed[i], w, hidden_t, weight, proj, hidden, down)
        down, proj = out[0], out[-1]
    _, grad_hid, part = out
    returned = lax.all_to_all(
        part.reshape(n_experts, 1, cap), ALL, split_axis=0, concat_axis=0, tiled=True
    ).reshape(n_experts, cap)
    value = jnp.sum(jnp.where(at, returned[:, :, None], 0.0), axis=1)
    grad_prob = jnp.sum(jnp.where(named, value[None], 0.0), axis=1).T[None]

    features = jnp.concatenate([select(y, part) for part in blocks], axis=1)
    features = lax.all_gather(features, TP, axis=0, tiled=False)
    context = lax.all_gather(attn_out, "y", axis=0, tiled=False)
    context = context.reshape(4, 4, tokens, -1).transpose(1, 0, 2, 3).reshape(16 * tokens, -1)
    partial = lax.dot_general(
        features.reshape(16 * tokens, -1), context, (((0,), (0,)), ((), ())), preferred_element_type=F32
    )
    grad_oproj = lax.psum_scatter(partial, ("x", "zhi"), scatter_dimension=0, tiled=True).astype(BF)
    return (grad_prob, grad_hid[None], down[None], grad_oproj)


def solution(mesh):
    fine = Mesh(mesh.devices.reshape(2, 2, 4, 2, 4), ALL)
    in_specs = (
        P(TP, CP, None),
        P(TP, CP, None),
        P(TP, CP, None),
        P(CP, TP),
        P(ALL, None, None),
        P(ALL, None, None),
    )
    out_specs = (
        P(TP, CP, None),
        P(ALL, None, None),
        P(ALL, None, None),
        P(CP, TP),
    )
    return jax.shard_map(local, mesh=fine, in_specs=in_specs, out_specs=out_specs, check_vma=False)
```

time: 675 us -> 352 us (0.52)
  waiting for transfers between devices: 436 us -> 187 us
  local copies, waits for them, and re-layouts: 108 us -> 13.3 us
  Pallas kernels: 0 us -> 55.6 us
  matrix products: 40 us -> 10.1 us
  blocking collectives: 0 us -> 17.4 us
  starting transfers between devices: 56.5 us -> 44.8 us
  other arithmetic: 18.8 us -> 8.18 us
    all_to_all x3, waiting for transfers between devices: 383 us -> 60.2 us  [the longest x2 60.2 us: local(): lax.all_to_all(rows.reshape(n_experts // 4, 4 * cap, chunk), PEERS, split...]
    pallas_call x0 -> x7, Pallas kernels: none -> 55.6 us  [the longest x2 33.1 us: expert(): pl.pallas_call(kernel, out_shape=out_shape, grid=(steps,), in_specs=in_sp...]
    ppermute x0 -> x11, waiting for transfers between devices: none -> 42.7 us  [ring(): return lax.ppermute(x, 'y', [(i, (i + shift) % 4) for i in range(4)])]
    reshape x4 -> x3, local copies, waits for them, and re-layouts: 32 us -> 1.94 us  [the longest x1 1.06 us: local(): weight = got_prob.reshape(slots, 1)]
    dot_general x3 -> x2, matrix products: 40 us -> 10.1 us  [the longest x1 9.98 us: local(): lax.dot_general(features.reshape(16 * tokens, -1), context, (((0,), (0,))...]
    all_to_all x3, starting transfers between devices: 56.4 us -> 29.7 us  [the longest x1 16.8 us: local(): lax.all_to_all(send_prob.reshape(n_experts, 1, cap), ALL, split_axis=0, c...]
    scatter x2 -> x0, local copies, waits for them, and re-layouts: 26.5 us -> none  [the longest x1 18.9 us: local(): jnp.zeros((n_experts * capacity, width), jnp.bfloat16).at[target]]
    all_gather x1 -> x2, waiting for transfers between devices: 52 us -> 78.1 us  [the longest x1 78 us: local(): features = lax.all_gather(features, TP, axis=0, tiled=False)]
  transfers between devices with their start and end apart: 5 -> 17, of which waited for: 2 -> 9; matrix products, arithmetic and copies ran while one was open for 23% -> 9% of each run, Pallas kernels for 0% -> 16%
where the time goes in v1:
time: 352 us; the launch traced here: 350 us
  waiting for transfers between devices  187 us (53%)
  Pallas kernels  55.6 us (16%)
  starting transfers between devices  44.8 us (13%)
  blocking collectives  17.4 us (5%)
  between operations  13.9 us (4%)
  local copies, waits for them, and re-layouts  13.3 us (4%)
  matrix products  10.1 us (3%)
  other arithmetic  8.18 us (2%)
    all_gather x1, waiting for transfers between devices, local(): features = lax.all_gather(features, TP, axis=0, tiled=False)  78 us
    all_to_all x2, waiting for transfers between devices, local(): lax.all_to_all(rows.reshape(n_experts // 4, 4 * cap, chunk), PEERS, split...  60.2 us
    ppermute x11, waiting for transfers between devices, ring(): return lax.ppermute(x, 'y', [(i, (i + shift) % 4) for i in range(4)])  42.7 us
    pallas_call x2, Pallas kernels, expert(): pl.pallas_call(kernel, out_shape=out_shape, grid=(steps,), in_specs=in_sp...  33.1 us
    all_to_all x1, blocking collectives, local(): lax.all_to_all(part.reshape(n_experts, 1, cap), ALL, split_axis=0, concat...  17.4 us
    all_to_all x1, starting transfers between devices, local(): lax.all_to_all(send_prob.reshape(n_experts, 1, cap), ALL, split_axis=0, c...  16.8 us
    ppermute x11, starting transfers between devices, ring(): return lax.ppermute(x, 'y', [(i, (i + shift) % 4) for i in range(4)])  14.9 us
    pallas_call x2, Pallas kernels, dispatch(): pl.pallas_call(dispatch_kernel, out_shape=jax.ShapeDtypeStruct((rows, wid...  13.8 us
  transfers between devices with their start and end apart: 17, of which 9 were waited for; matrix products, arithmetic and copies ran while one was open for 9% of the time, Pallas kernels for 16%

profile of v1, /device:TPU:1, one launch (start us, length us, event | category | flops | bytes accessed | tf_op | source)
XLA Modules:
  0.0 350.5 jit_solution(14530842948897784724)
XLA Ops:
  7.2 0.7 all-gather.7.cloned.1.call-update
  7.9 1.3 fusion.3
  9.2 3.6 %collective-permute-start.8 = (bf16[128,2048]{1,0:T(8,128)(2,1)S(1)}, bf16[128,2048]{1,0:T(8,128)(2,1)S(1)}, u32[]{:S(2)}, u32[]{:S(2)}) collective-permute-start(bf16[128,2048]{1,0:T(8,128)(2,1)S(1)} %get-tuple-element.14.g0.refs_0_), channel_id=1, source_target_pairs={{0,3},{1,0},{2,1},{3,2},{4,7},{5,4},{6,5},{7,6},{8,11},{9,8},{10,9... | collective-permute-start | bytes 1572872 | tf_op jit(solution)/shard_map/ppermute | solution.py:214
  12.9 2.7 collective-permute-start.4
  15.6 7.9 %collective-permute-done.8.g2.refs_2_ = bf16[128,2048]{1,0:T(8,128)(2,1)S(1)} collective-permute-done((bf16[128,2048]{1,0:T(8,128)(2,1)S(1)}, bf16[128,2048]{1,0:T(8,128)(2,1)S(1)}, u32[]{:S(2)}, u32[]{:S(2)}) %collective-permute-start.8) | collective-permute-done | bytes 524320 | tf_op jit(solution)/shard_map/ppermute | solution.py:214
  23.5 3.5 collective-permute-start.10
  27.0 0.8 slice.28
  27.7 17.0 %collective-permute-done.4.g2.refs_2_ = bf16[128,2048]{1,0:T(8,128)(2,1)S(1)} collective-permute-done((bf16[128,2048]{1,0:T(8,128)(2,1)S(1)}, bf16[128,2048]{1,0:T(8,128)(2,1)S(1)}, u32[]{:S(2)}, u32[]{:S(2)}) %collective-permute-start.4) | collective-permute-done | bytes 524320 | tf_op jit(solution)/shard_map/ppermute | solution.py:214
  44.7 0.8 slice.26
  45.5 3.5 %collective-permute-start.6 = (bf16[64,2048]{1,0:T(8,128)(2,1)}, bf16[64,2048]{1,0:T(8,128)(2,1)}, u32[]{:S(2)}, u32[]{:S(2)}) collective-permute-start(bf16[64,2048]{1,0:T(8,128)(2,1)} %slice.26), channel_id=1, source_target_pairs={{0,3},{1,0},{2,1},{3,2},{4,7},{5,4},{6,5},{7,6},{8,11},{9,8},{10,9... | collective-permute-start | bytes 786440 | tf_op jit(solution)/shard_map/ppermute | solution.py:214
  49.0 0.8 slice.25
  49.8 6.2 %collective-permute-done.10.g4.refs_4_ = bf16[64,2048]{1,0:T(8,128)(2,1)} collective-permute-done((bf16[64,2048]{1,0:T(8,128)(2,1)S(1)}, bf16[64,2048]{1,0:T(8,128)(2,1)}, u32[]{:S(2)}, u32[]{:S(2)}) %collective-permute-start.10) | collective-permute-done | bytes 262176 | tf_op jit(solution)/shard_map/ppermute | solution.py:214
  55.9 3.5 collective-permute-done.9.g3.refs_3_
  59.5 3.0 shard_map.98
  62.5 4.8 %collective-permute-done.6.g4.refs_4_ = bf16[64,2048]{1,0:T(8,128)(2,1)} collective-permute-done((bf16[64,2048]{1,0:T(8,128)(2,1)}, bf16[64,2048]{1,0:T(8,128)(2,1)}, u32[]{:S(2)}, u32[]{:S(2)}) %collective-permute-start.6) | collective-permute-done | bytes 262176 | tf_op jit(solution)/shard_map/ppermute | solution.py:214
  67.3 3.4 collective-permute-done.5.g3.refs_3_
  70.7 3.0 shard_map.99
  73.7 2.3 pad_maximum_fusion
  76.0 0.1 collective-permute-start.1
  76.1 1.4 collective-permute-start
  77.7 0.1 convolution_select_fusion
  77.8 0.3 fusion
  78.2 0.7 copy.28
  78.9 16.8 %all-to-all-start.1 = ((f32[128,1,10]{2,1,0:T(1,128)}), f32[128,1,10]{2,1,0:T(1,128)S(1)}, u32[]{:S(2)}, u32[]{:S(2)}) async-start(f32[128,1,10]{2,1,0:T(1,128)} %copy.28), calls=%async_computation.1 | async-start | bytes 131072 | tf_op jit(solution)/shard_map/all_to_all | solution.py:240
  95.8 0.6 pad_add_fusion.ids_ref
  96.4 2.6 shard_map.93.s_ref
  99.0 6.9 %shard_map.95 = bf16[1280,2048]{1,0:T(8,128)(2,1)} custom-call(bf16[1280,512]{1,0:T(8,128)(2,1)} %shard_map.93.s_ref, bf16[128,2048]{1,0:T(8,128)(2,1)} %copy-done.1, bf16[128,2048]{1,0:T(8,128)(2,1)} %copy-done.6, bf16[128,2048]{1,0:T(8,128)(2,1)} %copy-done.5, bf16[64,2048]{1,0:T(8,128)(2,1)} %collective-permute-done.9.g3.refs_3_, ...), custom_call_target="tpu_custom_call" | custom-call | flops 2684354560 | bytes 5242880 | tf_op jit(solution)/shard_map/pallas_call | solution.py:81
  105.9 7.9 %all-to-all-start.2 = ((bf16[32,40,2048]{2,1,0:T(8,128)(2,1)}), bf16[32,40,2048]{2,1,0:T(8,128)(2,1)}, u32[]{:S(2)}, u32[]{:S(2)}) async-start(bf16[32,40,2048]{2,1,0:T(8,128)(2,1)} %bitcast.38), calls=%async_computation.2 | async-start | bytes 10485760 | tf_op jit(solution)/shard_map/all_to_all | solution.py:250
  113.8 0.2 reduce-scatter.2.cloned.1.call-start
  114.0 4.9 %copy.35 = bf16[4,4,128,1024]{3,2,1,0:T(8,128)(2,1)} copy(bf16[4,4,128,1024]{3,2,0,1:T(8,128)(2,1)} %bitcast.40) | data formatting | bytes 8388608 | tf_op jit(solution)/shard_map/transpose | solution.py:268
  118.9 78.0 %all-gather.5.cloned.1.call-done = bf16[2048,1024]{1,0:T(8,128)(2,1)} async-done(((bf16[512,1024]{1,0:T(8,128)(2,1)}), bf16[2048,1024]{1,0:T(8,128)(2,1)}) %all-gather.5.cloned.1.call-update) | async-done | bytes 4194320 | tf_op jit(solution)/shard_map/all_gather | solution.py:266
  196.9 10.0 %fusion.4 = f32[1024,1024]{1,0:T(8,128)} fusion(bf16[2048,1024]{1,0:T(8,128)(2,1)} %all-gather.5.cloned.1.call-done, bf16[2048,1024]{1,0:T(8,128)(2,1)} %bitcast.41), kind=kOutput, calls=%fused_computation.15 | convolution fusion | flops 4294967296 | bytes 12582912 | tf_op jit(solution)/shard_map/dot_general | solution.py:269
  206.9 6.9 %shard_map.94 = bf16[1280,2048]{1,0:T(8,128)(2,1)} custom-call(bf16[1280,512]{1,0:T(8,128)(2,1)} %shard_map.93.s_ref, bf16[128,2048]{1,0:T(8,128)(2,1)} %copy-done, bf16[128,2048]{1,0:T(8,128)(2,1)} %copy-done.4, bf16[128,2048]{1,0:T(8,128)(2,1)} %copy-done.3, bf16[64,2048]{1,0:T(8,128)(2,1)} %collective-permute-done.5.g3.refs_3_, ...), custom_call_target="tpu_custom_call" | custom-call | flops 2684354560 | bytes 5242880 | tf_op jit(solution)/shard_map/pallas_call | solution.py:81
  213.9 5.0 %all-to-all-start = ((bf16[32,40,2048]{2,1,0:T(8,128)(2,1)}), bf16[32,40,2048]{2,1,0:T(8,128)(2,1)}, u32[]{:S(2)}, u32[]{:S(2)}) async-start(bf16[32,40,2048]{2,1,0:T(8,128)(2,1)} %bitcast.39), calls=%async_computation | async-start | bytes 10485760 | tf_op jit(solution)/shard_map/all_to_all | solution.py:250
  218.9 2.3 copy.31.refs_2_
  221.2 0.5 broadcast.9
  221.8 0.8 reduce.4
  222.6 1.1 reshape.70.refs_3_
  223.6 14.8 %shard_map.96 = (bf16[768,4096]{1,0:T(8,128)(2,1)}, f32[1280,768]{1,0:T(8,128)}) custom-call(bf16[1280,2048]{1,0:T(8,128)(2,1)} %bitcast.18.refs_0_, bf16[768,4096]{1,0:T(8,128)(2,1)} %bitcast.59, bf16[768,1280]{1,0:T(8,128)(2,1)} %copy.31.refs_2_, f32[1280,1]{1,0:T(8,128)} %reshape.70.refs_3_), custom_call_target="tpu_custom_call" | custom-call | flops 8053063680 | bytes 11534336 | tf_op jit(solution)/shard_map/pallas_call | solution.py:198
  238.4 60.2 %all-to-all-done = bf16[32,40,2048]{2,1,0:T(8,128)(2,1)} async-done(((bf16[32,40,2048]{2,1,0:T(8,128)(2,1)}), bf16[32,40,2048]{2,1,0:T(8,128)(2,1)}, u32[]{:S(2)}, u32[]{:S(2)}) %all-to-all-start) | async-done | bytes 5242912 | tf_op jit(solution)/shard_map/all_to_all | solution.py:250
  298.6 18.3 %shard_map.97 = (bf16[768,4096]{1,0:T(8,128)(2,1)}, bf16[1280,768]{1,0:T(8,128)(2,1)}, f32[1280,1]{1,0:T(8,128)}) custom-call(bf16[1280,2048]{1,0:T(8,128)(2,1)} %bitcast.10.refs_0_, bf16[768,4096]{1,0:T(8,128)(2,1)} %bitcast.60, bf16[768,1280]{1,0:T(8,128)(2,1)} %copy.31.refs_2_, f32[1280,1]{1,0:T(8,128)} %reshape.70.refs_3_, ...), custom_call_target="tpu_custom_call", output_to_operand_aliasing={{0}: (6, {})} | custom-call | flops 8053063680 | bytes 11534336 | tf_op jit(solution)/shard_map/pallas_call | solution.py:198
  316.9 1.3 reduce.1
  318.3 0.1 reshape.61
  318.4 17.4 %all_to_all.20 = f32[128,1,10]{2,1,0:T(1,128)S(1)} all-to-all(f32[128,1,10]{2,1,0:T(1,128)S(1)} %bitcast.45), channel_id=1, replica_groups=mesh['zlo'=2,'core'=2,'x'=4,'zhi'=2,'y'=4] {'zlo','core','x','zhi','y'}, dimensions={0} | all-to-all | bytes 10240 | tf_op jit(solution)/shard_map/all_to_all | solution.py:259
  335.9 0.3 fusion.1
  336.1 0.7 select_reduce_fusion
  336.8 5.4 %reduce-scatter.2.cloned.1.call-done = f32[128,1024]{1,0:T(8,128)} async-done(((f32[1024,1024]{1,0:T(8,128)}), f32[128,1024]{1,0:T(8,128)}) %reduce-scatter.2.cloned.1.call-update) | async-done | bytes 524304 | tf_op jit(solution)/shard_map/reduce_scatter | solution.py:272
  342.2 1.8 convert_element_type.26
  (41 shorter events, 0.4 us)
Async XLA Ops:
  7.2 106.9 %all-gather.7.cloned.1.call-start = ((), (), s32[]{:S(2)}) async-start(), calls=%async_computation.7 | async-start | bytes 5242880 | tf_op jit(solution)/shard_map/all_gather | solution.py:267
  7.9 189.0 %all-gather.5.cloned.1.call-start = ((), (), s32[]{:S(2)}) async-start(), calls=%async_computation.6 | async-start | bytes 5242880 | tf_op jit(solution)/shard_map/all_gather | solution.py:266
  9.2 50.2 %copy-start.1 = (bf16[128,2048]{1,0:T(8,128)(2,1)}, bf16[128,2048]{1,0:T(8,128)(2,1)S(1)}, u32[]{:S(2)}) copy-start(bf16[128,2048]{1,0:T(8,128)(2,1)S(1)} %get-tuple-element.14.g0.refs_0_) | copy-start | bytes 1572868
  9.2 61.4 %copy-start = (bf16[128,2048]{1,0:T(8,128)(2,1)}, bf16[128,2048]{1,0:T(8,128)(2,1)S(1)}, u32[]{:S(2)}) copy-start(bf16[128,2048]{1,0:T(8,128)(2,1)S(1)} %get-tuple-element.15.g0.refs_0_) | copy-start | bytes 1572868
  9.2 14.2 %collective-permute-start.8 = (bf16[128,2048]{1,0:T(8,128)(2,1)S(1)}, bf16[128,2048]{1,0:T(8,128)(2,1)S(1)}, u32[]{:S(2)}, u32[]{:S(2)}) collective-permute-start(bf16[128,2048]{1,0:T(8,128)(2,1)S(1)} %get-tuple-element.14.g0.refs_0_), channel_id=1, source_target_pairs={{0,3},{1,0},{2,1},{3,2},{4,7},{5,4},{6,5},{7,6},{8,11},{9,8},{10,9... | collective-permute-start | bytes 1572872 | tf_op jit(solution)/shard_map/ppermute | solution.py:214
  12.9 14.1 %collective-permute-start.7 = (bf16[128,2048]{1,0:T(8,128)(2,1)S(1)}, bf16[128,2048]{1,0:T(8,128)(2,1)S(1)}, u32[]{:S(2)}, u32[]{:S(2)}) collective-permute-start(bf16[128,2048]{1,0:T(8,128)(2,1)S(1)} %get-tuple-element.14.g0.refs_0_), channel_id=1, source_target_pairs={{0,1},{1,2},{2,3},{3,0},{4,5},{5,6},{6,7},{7,4},{8,9},{9,10},{10,1... | collective-permute-start | bytes 1572872 | tf_op jit(solution)/shard_map/ppermute | solution.py:214
  12.9 31.8 %collective-permute-start.4 = (bf16[128,2048]{1,0:T(8,128)(2,1)S(1)}, bf16[128,2048]{1,0:T(8,128)(2,1)S(1)}, u32[]{:S(2)}, u32[]{:S(2)}) collective-permute-start(bf16[128,2048]{1,0:T(8,128)(2,1)S(1)} %get-tuple-element.15.g0.refs_0_), channel_id=1, source_target_pairs={{0,3},{1,0},{2,1},{3,2},{4,7},{5,4},{6,5},{7,6},{8,11},{9,8},{10,9... | collective-permute-start | bytes 1572872 | tf_op jit(solution)/shard_map/ppermute | solution.py:214
  15.5 33.4 %collective-permute-start.3 = (bf16[128,2048]{1,0:T(8,128)(2,1)S(1)}, bf16[128,2048]{1,0:T(8,128)(2,1)S(1)}, u32[]{:S(2)}, u32[]{:S(2)}) collective-permute-start(bf16[128,2048]{1,0:T(8,128)(2,1)S(1)} %get-tuple-element.15.g0.refs_0_), channel_id=1, source_target_pairs={{0,1},{1,2},{2,3},{3,0},{4,5},{5,6},{6,7},{7,4},{8,9},{9,10},{10,1... | collective-permute-start | bytes 1572872 | tf_op jit(solution)/shard_map/ppermute | solution.py:214
  23.5 36.0 %copy-start.5 = (bf16[128,2048]{1,0:T(8,128)(2,1)}, bf16[128,2048]{1,0:T(8,128)(2,1)S(1)}, u32[]{:S(2)}) copy-start(bf16[128,2048]{1,0:T(8,128)(2,1)S(1)} %collective-permute-done.8.g2.refs_2_) | copy-start | bytes 1572868
  23.5 32.5 %collective-permute-start.10 = (bf16[64,2048]{1,0:T(8,128)(2,1)S(1)}, bf16[64,2048]{1,0:T(8,128)(2,1)}, u32[]{:S(2)}, u32[]{:S(2)}) collective-permute-start(bf16[64,2048]{1,0:T(8,128)(2,1)S(1)} %slice.29), channel_id=1, source_target_pairs={{0,3},{1,0},{2,1},{3,2},{4,7},{5,4},{6,5},{7,6},{8,11},{9,8},{10,9... | collective-permute-start | bytes 786440 | tf_op jit(solution)/shard_map/ppermute | solution.py:214
  27.0 32.5 %copy-start.6 = (bf16[128,2048]{1,0:T(8,128)(2,1)}, bf16[128,2048]{1,0:T(8,128)(2,1)S(1)}, u32[]{:S(2)}) copy-start(bf16[128,2048]{1,0:T(8,128)(2,1)S(1)} %collective-permute-done.7.g1.refs_1_) | copy-start | bytes 1572868
  27.7 31.7 %collective-permute-start.9 = (bf16[64,2048]{1,0:T(8,128)(2,1)}, bf16[64,2048]{1,0:T(8,128)(2,1)}, u32[]{:S(2)}, u32[]{:S(2)}) collective-permute-start(bf16[64,2048]{1,0:T(8,128)(2,1)} %slice.28), channel_id=1, source_target_pairs={{0,1},{1,2},{2,3},{3,0},{4,5},{5,6},{6,7},{7,4},{8,9},{9,10},{10,1... | collective-permute-start | bytes 786440 | tf_op jit(solution)/shard_map/ppermute | solution.py:214
  44.7 26.0 %copy-start.3 = (bf16[128,2048]{1,0:T(8,128)(2,1)}, bf16[128,2048]{1,0:T(8,128)(2,1)S(1)}, u32[]{:S(2)}) copy-start(bf16[128,2048]{1,0:T(8,128)(2,1)S(1)} %collective-permute-done.4.g2.refs_2_) | copy-start | bytes 1572868
  45.5 21.8 %collective-permute-start.6 = (bf16[64,2048]{1,0:T(8,128)(2,1)}, bf16[64,2048]{1,0:T(8,128)(2,1)}, u32[]{:S(2)}, u32[]{:S(2)}) collective-permute-start(bf16[64,2048]{1,0:T(8,128)(2,1)} %slice.26), channel_id=1, source_target_pairs={{0,3},{1,0},{2,1},{3,2},{4,7},{5,4},{6,5},{7,6},{8,11},{9,8},{10,9... | collective-permute-start | bytes 786440 | tf_op jit(solution)/shard_map/ppermute | solution.py:214
  49.0 21.7 %copy-start.4 = (bf16[128,2048]{1,0:T(8,128)(2,1)}, bf16[128,2048]{1,0:T(8,128)(2,1)S(1)}, u32[]{:S(2)}) copy-start(bf16[128,2048]{1,0:T(8,128)(2,1)S(1)} %collective-permute-done.3.g1.refs_1_) | copy-start | bytes 1572868
  49.8 20.9 %collective-permute-start.5 = (bf16[64,2048]{1,0:T(8,128)(2,1)}, bf16[64,2048]{1,0:T(8,128)(2,1)}, u32[]{:S(2)}, u32[]{:S(2)}) collective-permute-start(bf16[64,2048]{1,0:T(8,128)(2,1)} %slice.25), channel_id=1, source_target_pairs={{0,1},{1,2},{2,3},{3,0},{4,5},{5,6},{6,7},{7,4},{8,9},{9,10},{10,1... | collective-permute-start | bytes 786440 | tf_op jit(solution)/shard_map/ppermute | solution.py:214
  59.4 16.6 %copy-start.7 = (s32[1,128,8]{1,2,0:T(8,128)S(1)}, s32[1,128,8]{1,2,0:T(8,128)}, u32[]{:S(2)}) copy-start(s32[1,128,8]{1,2,0:T(8,128)} %param.7) | copy-start | bytes 12292
  59.4 18.2 %copy-start.8 = (bf16[1,128,8]{1,2,0:T(8,128)(2,1)S(1)}, bf16[1,128,8]{1,2,0:T(8,128)(2,1)}, u32[]{:S(2)}) copy-start(bf16[1,128,8]{1,2,0:T(8,128)(2,1)} %param.8) | copy-start | bytes 6148
  76.0 19.7 %collective-permute-start.1 = (s32[8,128]{1,0:T(8,128)S(1)}, s32[8,128]{1,0:T(8,128)S(1)}, u32[]{:S(2)}, u32[]{:S(2)}) collective-permute-start(s32[8,128]{1,0:T(8,128)S(1)} %bitcast.47), channel_id=1, source_target_pairs={{0,3},{1,0},{2,1},{3,2},{4,7},{5,4},{6,5},{7,6},{8,11},{9,8},{10,9... | collective-permute-start | bytes 12296 | tf_op jit(solution)/shard_map/ppermute | solution.py:214
  76.1 19.6 %collective-permute-start = (s32[8,128]{1,0:T(8,128)S(1)}, s32[8,128]{1,0:T(8,128)S(1)}, u32[]{:S(2)}, u32[]{:S(2)}) collective-permute-start(s32[8,128]{1,0:T(8,128)S(1)} %bitcast.48), channel_id=1, source_target_pairs={{0,1},{1,2},{2,3},{3,0},{4,5},{5,6},{6,7},{7,4},{8,9},{9,10},{10,1... | collective-permute-start | bytes 12296 | tf_op jit(solution)/shard_map/ppermute | solution.py:214
  77.5 18.2 %collective-permute-start.2 = (s32[8,128]{1,0:T(8,128)S(1)}, s32[8,128]{1,0:T(8,128)S(1)}, u32[]{:S(2)}, u32[]{:S(2)}) collective-permute-start(s32[8,128]{1,0:T(8,128)S(1)} %bitcast.49), channel_id=1, source_target_pairs={{0,2},{1,3},{2,0},{3,1},{4,6},{5,7},{6,4},{7,5},{8,10},{9,11},{10,... | collective-permute-start | bytes 12296 | tf_op jit(solution)/shard_map/ppermute | solution.py:214
  78.9 27.0 %all-to-all-start.1 = ((f32[128,1,10]{2,1,0:T(1,128)}), f32[128,1,10]{2,1,0:T(1,128)S(1)}, u32[]{:S(2)}, u32[]{:S(2)}) async-start(f32[128,1,10]{2,1,0:T(1,128)} %copy.28), calls=%async_computation.1 | async-start | bytes 131072 | tf_op jit(solution)/shard_map/all_to_all | solution.py:240
  105.9 108.0 %all-to-all-start.2 = ((bf16[32,40,2048]{2,1,0:T(8,128)(2,1)}), bf16[32,40,2048]{2,1,0:T(8,128)(2,1)}, u32[]{:S(2)}, u32[]{:S(2)}) async-start(bf16[32,40,2048]{2,1,0:T(8,128)(2,1)} %bitcast.38), calls=%async_computation.2 | async-start | bytes 10485760 | tf_op jit(solution)/shard_map/all_to_all | solution.py:250
  113.8 228.4 %reduce-scatter.2.cloned.1.call-start = ((), (), s32[]{:S(2)}) async-start(), calls=%async_computation.5 | async-start | bytes 4718592 | tf_op jit(solution)/shard_map/reduce_scatter | solution.py:272
  213.9 5.0 %copy-start.2 = (bf16[1,1280,768]{2,1,0:T(8,128)(2,1)S(1)}, bf16[1,1280,768]{2,1,0:T(8,128)(2,1)}, u32[]{:S(2)}) copy-start(bf16[1,1280,768]{2,1,0:T(8,128)(2,1)} %param.11) | copy-start | bytes 5898244
  213.9 84.7 %all-to-all-start = ((bf16[32,40,2048]{2,1,0:T(8,128)(2,1)}), bf16[32,40,2048]{2,1,0:T(8,128)(2,1)}, u32[]{:S(2)}, u32[]{:S(2)}) async-start(bf16[32,40,2048]{2,1,0:T(8,128)(2,1)} %bitcast.39), calls=%async_computation | async-start | bytes 10485760 | tf_op jit(solution)/shard_map/all_to_all | solution.py:250
Sparse Core Ops, SparseCore 0:
  9.7 74.8 all-gather.6
  86.2 110.6 all-gather.4
  207.0 135.0 reduce-scatter.1

commit v2 on v1

v2 whole, which is shorter than its diff:
```python
import jax
import jax.numpy as jnp
from jax import lax
from jax.experimental import pallas as pl
from jax.experimental.pallas import tpu as pltpu
from jax.sharding import Mesh
from jax.sharding import PartitionSpec as P

TP = ("zlo", "core")
CP = ("x", "zhi", "y")
ALL = TP + CP
PEERS = ("zlo", "core", "x", "zhi")
CHUNKS = ((2560, 1536), (0, 2560))
TILE = 512
WIDE = 512
VMEM = 56 * 1024 * 1024
BF = jnp.bfloat16
F32 = jnp.float32


def params():
    return pltpu.CompilerParams(vmem_limit_bytes=VMEM)


def cost(flops, moved):
    return pl.CostEstimate(flops=flops, bytes_accessed=moved, transcendentals=0)


def upper(n):
    return (
        lax.broadcasted_iota(jnp.int32, (n, n), 0) < lax.broadcasted_iota(jnp.int32, (n, n), 1)
    ).astype(BF)


def ranks(member):
    count = jnp.dot(member.astype(BF), upper(member.shape[1]), preferred_element_type=F32)
    return jnp.where(member, count, -1.0)


def place_kernel(y_ref, *refs):
    s_ref = refs[-1]
    y = y_ref[0]
    rows, cols = s_ref.shape
    peers = rows // 40
    expert = (lax.broadcasted_iota(jnp.int32, (peers, 128), 0) * 4 + y).astype(F32)
    parts = []
    for ref in refs[:-1]:
        named = ref[...].astype(F32)
        member = named[0:1, :] == expert
        for i in range(1, 8):
            member = member | (named[i : i + 1, :] == expert)
        parts.append(ranks(member).astype(BF))
    table = jnp.concatenate(parts, axis=1)
    row = lax.broadcasted_iota(jnp.int32, (rows, peers), 0)
    peer = lax.broadcasted_iota(jnp.int32, (rows, peers), 1)
    pick = (lax.shift_right_logical(row * 6554, 18) == peer).astype(BF)
    spread = jnp.dot(pick, table, preferred_element_type=F32)
    row = lax.broadcasted_iota(jnp.int32, (rows, cols), 0)
    tenth = lax.shift_right_logical(row * 6554, 16)
    rank = (row - tenth * 10).astype(F32)
    block = lax.shift_right_logical(lax.broadcasted_iota(jnp.int32, (rows, cols), 1), 7)
    origin = jnp.where(block == 0, 0, jnp.where(block == 1, 3, jnp.where(block == 2, 1, 2)))
    here = (tenth & 3) == ((origin + y) & 3)
    s_ref[...] = jnp.where(here & (spread == rank), 1.0, 0.0).astype(BF)


def place(y, blocks, rows):
    last = blocks[0].shape[1] // 128 - 1
    return pl.pallas_call(
        place_kernel,
        out_shape=jax.ShapeDtypeStruct((rows, 512), BF),
        grid=(1,),
        in_specs=[pl.BlockSpec(memory_space=pltpu.SMEM)]
        + [pl.BlockSpec((16, 128), lambda i: (0, last)) for _ in blocks],
        out_specs=pl.BlockSpec((rows, 512), lambda i: (0, 0)),
        compiler_params=params(),
        cost_estimate=cost(10**8, 2 * 10**6),
    )(y, *blocks)


def dispatch_kernel(s_ref, g0, g1, g2, g3, o_ref):
    g = jnp.concatenate([g0[...], g1[...], g2[...], g3[...]], axis=0)
    o_ref[...] = jnp.dot(s_ref[...], g, preferred_element_type=F32).astype(BF)


def dispatch(s, blocks, width):
    rows = s.shape[0]
    return pl.pallas_call(
        dispatch_kernel,
        out_shape=jax.ShapeDtypeStruct((rows, width), BF),
        grid=(width // TILE,),
        in_specs=[pl.BlockSpec(s.shape, lambda i: (0, 0))]
        + [pl.BlockSpec((128, TILE), lambda i: (0, i)) for _ in blocks],
        out_specs=pl.BlockSpec((rows, TILE), lambda i: (0, i)),
        compiler_params=params(),
        cost_estimate=cost(2 * rows * 512 * width, 2 * rows * width),
    )(s, *blocks)


def select_kernel(y_ref, *refs):
    out = refs[-1]
    col = 0
    for first, (_, width) in ((4, CHUNKS[1]), (0, CHUNKS[0])):
        for i in range(width // 512):
            at = pl.multiple_of(i * 512 + y_ref[0] * 128, 128)
            for k in range(4):
                out[k * 128 : (k + 1) * 128, col : col + 128] = refs[first + k][:, pl.ds(at, 128)]
            col += 128


def select(y, low, high, width):
    moved = 8 * 128 * width
    return pl.pallas_call(
        select_kernel,
        out_shape=jax.ShapeDtypeStruct((512, width // 4), BF),
        in_specs=[pl.BlockSpec(memory_space=pltpu.SMEM)]
        + [pl.BlockSpec(memory_space=pltpu.VMEM)] * 8,
        out_specs=pl.BlockSpec(memory_space=pltpu.VMEM),
        compiler_params=params(),
        cost_estimate=cost(0, moved),
    )(y, *low, *high)


def quarter_kernel(y_ref, g_ref, *outs):
    for out, shift in zip(outs, (0, 1, 3, 2)):
        y = (y_ref[0] + shift) & 3
        for i in range(g_ref.shape[1] // 512):
            at = pl.multiple_of(i * 512 + y * 128, 128)
            out[:, i * 128 : (i + 1) * 128] = g_ref[:, pl.ds(at, 128)]


def quarters(y, g):
    return pl.pallas_call(
        quarter_kernel,
        out_shape=[jax.ShapeDtypeStruct((128, g.shape[1] // 4), BF)] * 4,
        in_specs=[pl.BlockSpec(memory_space=pltpu.SMEM), pl.BlockSpec(memory_space=pltpu.VMEM)],
        out_specs=[pl.BlockSpec(memory_space=pltpu.VMEM)] * 4,
        compiler_params=params(),
        cost_estimate=cost(0, 4 * g.shape[0] * g.shape[1]),
    )(y, g)


def outer_kernel(t_ref, *refs):
    features, contexts, (o_ref, ft, at) = refs[:4], refs[4:9], refs[9:]

    @pl.when(pl.program_id(0) == 0)
    def _():
        for i, f in enumerate(features):
            ft[:, i * 512 : (i + 1) * 512] = f[...].T

    for i in range(4):
        who = t_ref[0] ^ i
        start = pl.multiple_of(who * 128, 128)
        for k in range(3):
            at[(i * 4 + k) * 128 : (i * 4 + k + 1) * 128, :] = contexts[k][pl.ds(start, 128), :]
        start = pl.multiple_of((who & 1) * 128, 128)
        at[(i * 4 + 3) * 128 : (i * 4 + 4) * 128, :] = jnp.where(
            who < 2, contexts[3][pl.ds(start, 128), :], contexts[4][pl.ds(start, 128), :]
        )
    o_ref[...] = jnp.dot(ft[...], at[...], preferred_element_type=F32).astype(BF)


def outer(t, features, contexts):
    n, wide = features[0].shape[1], contexts[0].shape[1]
    return pl.pallas_call(
        outer_kernel,
        out_shape=jax.ShapeDtypeStruct((n, wide), BF),
        grid=(wide // 256,),
        in_specs=[pl.BlockSpec(memory_space=pltpu.SMEM)]
        + [pl.BlockSpec((512, n), lambda i: (0, 0)) for _ in features]
        + [pl.BlockSpec((c.shape[0], 256), lambda i: (0, i)) for c in contexts],
        out_specs=pl.BlockSpec((n, 256), lambda i: (0, i)),
        scratch_shapes=[pltpu.VMEM((n, 2048), BF), pltpu.VMEM((2048, 256), BF)],
        compiler_params=params(),
        cost_estimate=cost(2 * 2048 * n * wide, 2 * (4096 * n + n * wide)),
    )(t, *features, *contexts)


def proj_kernel(first, last, *refs):
    routed_ref, *refs = refs
    term = None
    tile = refs[0].shape[1]
    for i in range(routed_ref.shape[1] // tile):
        piece = lax.dot_general(
            routed_ref[:, i * tile : (i + 1) * tile],
            refs.pop(0)[...],
            (((1,), (1,)), ((), ())),
            preferred_element_type=F32,
        )
        term = piece if term is None else term + piece
    if not first:
        term = refs[0][...] + term
    if not last:
        refs[-1][...] = term
        return
    h_ref, wt_ref, hid_ref, part_ref = refs[-4:]
    hid_ref[...] = (wt_ref[...] * term).astype(BF)
    part_ref[...] = jnp.sum(term * h_ref[...].astype(F32), axis=1, keepdims=True)


def project(chunk, routed, w, before, hidden, weight):
    rows, width = routed.shape
    hid = w.shape[0]
    first, last = chunk == 0, chunk == len(CHUNKS) - 1
    tile = 256
    across = pl.BlockSpec((tile, hid), lambda i: (i, 0))
    narrow = pl.BlockSpec((tile, 1), lambda i: (i, 0))
    deep = WIDE if CHUNKS[chunk][0] else width
    start, n = CHUNKS[chunk][0] // deep, width // deep
    in_specs = [pl.BlockSpec((tile, width), lambda i: (i, 0))]
    in_specs += [pl.BlockSpec((hid, deep), lambda i, j=j: (0, j)) for j in range(start, start + n)]
    args = [routed] + [w] * n
    if not first:
        in_specs.append(across)
        args.append(before)
    if last:
        in_specs += [across, narrow]
        args += [hidden, weight]
        out_shape = [jax.ShapeDtypeStruct((rows, hid), BF), jax.ShapeDtypeStruct((rows, 1), F32)]
        out_specs = [across, narrow]
    else:
        out_shape, out_specs = jax.ShapeDtypeStruct((rows, hid), F32), across

    def kernel(*refs):
        proj_kernel(first, last, *refs)

    return pl.pallas_call(
        kernel,
        out_shape=out_shape,
        grid=(rows // tile,),
        in_specs=in_specs,
        out_specs=out_specs,
        compiler_params=params(),
        cost_estimate=cost(2 * rows * hid * width, 2 * (rows + hid) * width),
    )(*args)


def down_kernel(routed_ref, ht_ref, wt_ref, *refs):
    weighted = (wt_ref[...] * routed_ref[...].astype(F32)).astype(BF)
    refs[-1][...] = jnp.dot(ht_ref[...], weighted, preferred_element_type=F32).astype(BF)


def weigh(chunk, routed, hidden_t, weight, full, before):
    rows, width = routed.shape
    hid = hidden_t.shape[0]
    steps = width // WIDE
    base = CHUNKS[chunk][0] // WIDE
    in_specs = [
        pl.BlockSpec((rows, WIDE), lambda i: (0, i)),
        pl.BlockSpec((hid, rows), lambda i: (0, 0)),
        pl.BlockSpec((rows, 1), lambda i: (0, 0)),
    ]
    args = [routed, hidden_t, weight]
    if before is not None:
        in_specs.append(pl.BlockSpec(memory_space=pl.ANY))
        args.append(before)
    return pl.pallas_call(
        down_kernel,
        out_shape=jax.ShapeDtypeStruct((hid, full), BF),
        grid=(steps,),
        in_specs=in_specs,
        out_specs=pl.BlockSpec((hid, WIDE), lambda i: (0, base + i)),
        input_output_aliases={} if before is None else {3: 0},
        compiler_params=params(),
        cost_estimate=cost(2 * rows * hid * width, 2 * (rows + hid) * width),
    )(*args)


def ring(x, shift, axis="y", n=4):
    return lax.ppermute(x, axis, [(i, (i + shift) % n) for i in range(n)])


def swap(x, axis):
    return ring(x, 1, axis, 2)


def ring_gather(x):
    return [x, ring(x, 1), ring(x, -1), ring(x, 2)]


def after(x, *others):
    return lax.optimization_barrier((x, *others))[0]


def local(grad_out, expert_ids, route_prob, attn_out, w_down, hidden_saved):
    n_experts = lax.axis_size(ALL)
    slots = hidden_saved.shape[1]
    cap = slots // n_experts
    g = grad_out[0]
    width = g.shape[1]
    y = lax.axis_index("y").reshape(1)
    (at_near, near), (at_far, far) = CHUNKS
    ids = expert_ids[0].T
    label = jnp.pad(ids.astype(BF), ((0, g.shape[0] - ids.shape[0]), (0, 0)))
    low = ring_gather(jnp.concatenate([g[:, at_near : at_near + near], label], axis=1))
    across = swap(g, "zlo")
    spread = place(y, low, slots)
    named = ids[:, None, :] == jnp.arange(n_experts, dtype=jnp.int32)[None, :, None]
    rank = ranks(jnp.any(named, axis=0))
    prob = jnp.sum(jnp.where(named, route_prob[0].T[:, None, :].astype(F32), 0.0), axis=0)
    at = rank[:, None, :] == jnp.arange(cap, dtype=jnp.int32).astype(F32)[None, :, None]
    send_prob = jnp.sum(jnp.where(at, prob[:, None, :], 0.0), axis=2)
    got_prob = lax.all_to_all(
        send_prob.reshape(n_experts, 1, cap), ALL, split_axis=0, concat_axis=0, tiled=True
    )
    high = ring_gather(after(g[:, at_far : at_far + far], send_prob))
    *low, got_prob, across = lax.optimization_barrier((*low, got_prob, across))

    def send(rows):
        return lax.all_to_all(
            rows.reshape(n_experts // 4, 4 * cap, -1), PEERS, split_axis=0, concat_axis=0, tiled=True
        ).reshape(slots, -1)

    rows0 = dispatch(spread, low, near)
    routed0 = send(rows0)
    contexts = after(attn_out, high[3])
    contexts = [contexts, ring(contexts, 1), ring(contexts, -1)]
    parts = quarters(y, across)
    other = [ring(q, shift) if shift else q for q, shift in zip(parts, (0, 1, -1, 2))]
    mine = select(y, low, high, width)
    other = jnp.concatenate(other, axis=0)
    features = [mine, swap(mine, "core"), other, swap(other, "core")]
    rows1 = dispatch(spread, high, far)
    routed1 = send(rows1)
    t = (lax.axis_index("zlo") * 2 + lax.axis_index("core")).reshape(1)
    half = attn_out.shape[0] // 2
    contexts += [ring(contexts[1][:half], 1), ring(contexts[2][half:], -1)]
    partial = outer(t, features, contexts)

    weight = got_prob.reshape(slots, 1)
    hidden = hidden_saved[0]
    hidden_t = hidden.T
    w = w_down[0]
    x = lax.axis_index("x")
    quarter = partial.shape[0] // 4

    def piece(shift):
        return lax.dynamic_slice_in_dim(partial, ((x + shift) & 3) * quarter, quarter, 0)

    pieces = [ring(piece(shift), shift, "x") for shift in (1, -1, 2)]
    proj = project(0, routed0, w, None, hidden, weight)
    down = weigh(0, routed0, hidden_t, weight, width, None)
    grad_hid, part = project(1, routed1, w, proj, hidden, weight)
    part = part.reshape(n_experts, 1, cap)
    *pieces, part = lax.optimization_barrier((*pieces, part))
    sums = piece(0).astype(F32)
    for got in pieces:
        sums = sums + got.astype(F32)
    zhi = lax.axis_index("zhi")
    eighth = quarter // 2
    give = lax.dynamic_slice_in_dim(sums, (1 - zhi) * eighth, eighth, 0).astype(BF)
    keep = lax.dynamic_slice_in_dim(sums, zhi * eighth, eighth, 0)
    grad_oproj = (keep + swap(give, "zhi").astype(F32)).astype(BF)
    down = weigh(1, routed1, hidden_t, weight, width, down)
    returned = lax.all_to_all(
        part, ALL, split_axis=0, concat_axis=0, tiled=True
    ).reshape(n_experts, cap)
    value = jnp.sum(jnp.where(at, returned[:, :, None], 0.0), axis=1)
    grad_prob = jnp.sum(jnp.where(named, value[None], 0.0), axis=1).T[None]
    return (grad_prob, grad_hid[None], down[None], grad_oproj)


def solution(mesh):
    fine = Mesh(mesh.devices.reshape(2, 2, 4, 2, 4), ALL)
    in_specs = (
        P(TP, CP, None),
        P(TP, CP, None),
        P(TP, CP, None),
        P(CP, TP),
        P(ALL, None, None),
        P(ALL, None, None),
    )
    out_specs = (
        P(TP, CP, None),
        P(ALL, None, None),
        P(ALL, None, None),
        P(CP, TP),
    )
    return jax.shard_map(local, mesh=fine, in_specs=in_specs, out_specs=out_specs, check_vma=False)
```

time: 352 us -> 239 us (0.68)
  waiting for transfers between devices: 187 us -> 79.2 us
  starting transfers between devices: 44.8 us -> 63.4 us
  blocking collectives: 17.4 us -> 0 us
  Pallas kernels: 55.6 us -> 70.4 us
  between operations: 13.9 us -> 0.85 us
  matrix products: 10.1 us -> 0.14 us
    all_gather x2 -> x0, waiting for transfers between devices: 78.1 us -> none  [the longest x1 78 us: local(): features = lax.all_gather(features, TP, axis=0, tiled=False)]
    all_to_all x2 -> x3, waiting for transfers between devices: 60.2 us -> 10.2 us  [the longest x2 10.2 us: send(): lax.all_to_all(rows.reshape(n_experts // 4, 4 * cap, -1), PEERS, split_ax...]
    ppermute x11 -> x20, waiting for transfers between devices: 42.7 us -> 67.1 us  [ring(): return lax.ppermute(x, axis, [(i, (i + shift) % n) for i in range(n)])]
    all_to_all x1 -> x0, blocking collectives: 17.4 us -> none  [local(): lax.all_to_all(part.reshape(n_experts, 1, cap), ALL, split_axis=0, concat...]
    ppermute x11 -> x20, starting transfers between devices: 14.9 us -> 28.9 us  [ring(): return lax.ppermute(x, axis, [(i, (i + shift) % n) for i in range(n)])]
    pallas_call x4 -> x7, Pallas kernels: 39.1 us -> 53 us  [the longest x2 19.6 us: project(): pl.pallas_call(kernel, out_shape=out_shape, grid=(rows // tile,), in_spec...]
    all_to_all x2 -> x3, starting transfers between devices: 12.9 us -> 24.1 us  [the longest x2 12.2 us: send(): lax.all_to_all(rows.reshape(n_experts // 4, 4 * cap, -1), PEERS, split_ax...]
    dot_general x1 -> x0, matrix products: 9.98 us -> none  [local(): lax.dot_general(features.reshape(16 * tokens, -1), context, (((0,), (0,))...]
  transfers between devices with their start and end apart: 17 -> 24, of which waited for: 9 -> 11; matrix products, arithmetic and copies ran while one was open for 9% -> 8% of each run, Pallas kernels for 16% -> 27%
where the time goes in v2:
time: 239 us; the launch traced here: 237 us
  waiting for transfers between devices  79.2 us (33%)
  Pallas kernels  70.4 us (29%)
  starting transfers between devices  63.4 us (27%)
  local copies, waits for them, and re-layouts  14.8 us (6%)
  other arithmetic  8.43 us (4%)
    ppermute x20, waiting for transfers between devices, ring(): return lax.ppermute(x, axis, [(i, (i + shift) % n) for i in range(n)])  67.1 us
    ppermute x20, starting transfers between devices, ring(): return lax.ppermute(x, axis, [(i, (i + shift) % n) for i in range(n)])  28.9 us
    pallas_call x2, Pallas kernels, project(): pl.pallas_call(kernel, out_shape=out_shape, grid=(rows // tile,), in_spec...  19.6 us
    pallas_call x2, Pallas kernels, weigh(): pl.pallas_call(down_kernel, out_shape=jax.ShapeDtypeStruct((hid, full), B...  17.3 us
    pallas_call x2, Pallas kernels, dispatch(): pl.pallas_call(dispatch_kernel, out_shape=jax.ShapeDtypeStruct((rows, wid...  14.8 us
    all_to_all x2, starting transfers between devices, send(): lax.all_to_all(rows.reshape(n_experts // 4, 4 * cap, -1), PEERS, split_ax...  12.2 us
    all_to_all x1, starting transfers between devices, local(): lax.all_to_all(part, ALL, split_axis=0, concat_axis=0, tiled=True)  11.9 us
    all_to_all x1, starting transfers between devices, local(): lax.all_to_all(send_prob.reshape(n_experts, 1, cap), ALL, split_axis=0, c...  10.4 us
  transfers between devices with their start and end apart: 24, of which 11 were waited for; matrix products, arithmetic and copies ran while one was open for 8% of the time, Pallas kernels for 27%

profile of v2, /device:TPU:1, one launch (start us, length us, event | category | flops | bytes accessed | tf_op | source)
XLA Modules:
  0.0 237.2 jit_solution(17836507420172776152)
XLA Ops:
  0.6 2.5 %collective-permute-start.3 = (bf16[128,4096]{1,0:T(8,128)(2,1)}, bf16[128,4096]{1,0:T(8,128)(2,1)S(1)}, u32[]{:S(2)}, u32[]{:S(2)}) collective-permute-start(bf16[128,4096]{1,0:T(8,128)(2,1)} %bitcast.40), channel_id=1, source_target_pairs={{0,64},{64,0},{1,65},{65,1},{2,66},{66,2},{3,67},{67,3},{4,68},{68... | collective-permute-start | bytes 3145736 | tf_op jit(solution)/shard_map/ppermute | solution.py:270
  3.2 1.1 slice.16
  5.0 3.0 %collective-permute-start.2 = (bf16[128,1664]{1,0:T(8,128)(2,1)S(1)}, bf16[128,1664]{1,0:T(8,128)(2,1)S(1)}, u32[]{:S(2)}, u32[]{:S(2)}) collective-permute-start(bf16[128,1664]{1,0:T(8,128)(2,1)S(1)} %fusion.4.refs_0_.g0), channel_id=1, source_target_pairs={{0,2},{1,3},{2,0},{3,1},{4,6},{5,7},{6,4},{7,5},{8,10},{9,11},{10,... | collective-permute-start | bytes 1277960 | tf_op jit(solution)/shard_map/ppermute | solution.py:270
  8.0 0.8 collective-permute-start.1
  12.8 10.4 %all-to-all-start = ((f32[128,1,10]{2,1,0:T(1,128)}), f32[128,1,10]{2,1,0:T(1,128)S(1)}, u32[]{:S(2)}, u32[]{:S(2)}) async-start(f32[128,1,10]{2,1,0:T(1,128)} %copy.24), calls=%async_computation | async-start | bytes 131072 | tf_op jit(solution)/shard_map/all_to_all | solution.py:303
  23.3 3.8 %collective-permute-done.1.refs_2_.g2 = bf16[128,1664]{1,0:T(8,128)(2,1)S(1)} collective-permute-done((bf16[128,1664]{1,0:T(8,128)(2,1)S(1)}, bf16[128,1664]{1,0:T(8,128)(2,1)S(1)}, u32[]{:S(2)}, u32[]{:S(2)}) %collective-permute-start.1) | collective-permute-done | bytes 426016 | tf_op jit(solution)/shard_map/ppermute | solution.py:270
  28.3 2.6 %shard_map.96.s_ref = bf16[1280,512]{1,0:T(8,128)(2,1)} custom-call(s32[1]{0:T(128)} %bitcast.3.y_ref, bf16[128,1664]{1,0:T(8,128)(2,1)} %copy-done.1, bf16[128,1664]{1,0:T(8,128)(2,1)} %copy-done.5, bf16[128,1664]{1,0:T(8,128)(2,1)} %copy-done.4, bf16[128,1664]{1,0:T(8,128)(2,1)} %copy-done.3), custom_call_target="tpu_custom_call" | custom-call | flops 100000000 | bytes 2000000 | tf_op jit(solution)/shard_map/pallas_call | solution.py:69
  30.9 1.8 all-to-all-done
  32.7 6.3 %shard_map.98 = bf16[1280,1536]{1,0:T(8,128)(2,1)} custom-call(bf16[1280,512]{1,0:T(8,128)(2,1)} %shard_map.96.s_ref, bf16[128,1664]{1,0:T(8,128)(2,1)} %copy-done.1, bf16[128,1664]{1,0:T(8,128)(2,1)} %copy-done.5, bf16[128,1664]{1,0:T(8,128)(2,1)} %copy-done.4, bf16[128,1664]{1,0:T(8,128)(2,1)} %copy-done.3), custom_call_target="tpu_custom_call" | custom-call | flops 2013265920 | bytes 3932160 | tf_op jit(solution)/shard_map/pallas_call | solution.py:88
  39.0 7.5 %all-to-all-start.2 = ((bf16[32,40,1536]{2,1,0:T(8,128)(2,1)}), bf16[32,40,1536]{2,1,0:T(8,128)(2,1)}, u32[]{:S(2)}, u32[]{:S(2)}) async-start(bf16[32,40,1536]{2,1,0:T(8,128)(2,1)} %bitcast.39), calls=%async_computation.2 | async-start | bytes 7864320 | tf_op jit(solution)/shard_map/all_to_all | solution.py:310
  46.6 2.5 %collective-permute-start.6 = (bf16[128,2560]{1,0:T(8,128)(2,1)S(1)}, bf16[128,2560]{1,0:T(8,128)(2,1)S(1)}, u32[]{:S(2)}, u32[]{:S(2)}) collective-permute-start(bf16[128,2560]{1,0:T(8,128)(2,1)S(1)} %slice.17.refs_4_.g0), channel_id=1, source_target_pairs={{0,2},{1,3},{2,0},{3,1},{4,6},{5,7},{6,4},{7,5},{8,10},{9,11},{10,... | collective-permute-start | bytes 1966088 | tf_op jit(solution)/shard_map/ppermute | solution.py:270
  49.0 0.9 collective-permute-start.5
  50.5 13.8 %collective-permute-done.6.refs_7_.g3 = bf16[128,2560]{1,0:T(8,128)(2,1)S(1)} collective-permute-done((bf16[128,2560]{1,0:T(8,128)(2,1)S(1)}, bf16[128,2560]{1,0:T(8,128)(2,1)S(1)}, u32[]{:S(2)}, u32[]{:S(2)}) %collective-permute-start.6) | collective-permute-done | bytes 655392 | tf_op jit(solution)/shard_map/ppermute | solution.py:270
  64.3 14.0 %collective-permute-done.5.refs_6_.g2 = bf16[128,2560]{1,0:T(8,128)(2,1)S(1)} collective-permute-done((bf16[128,2560]{1,0:T(8,128)(2,1)S(1)}, bf16[128,2560]{1,0:T(8,128)(2,1)S(1)}, u32[]{:S(2)}, u32[]{:S(2)}) %collective-permute-start.5) | collective-permute-done | bytes 655392 | tf_op jit(solution)/shard_map/ppermute | solution.py:270
  79.2 0.8 copy-done.10
  80.0 8.5 %shard_map.97 = bf16[1280,2560]{1,0:T(8,128)(2,1)} custom-call(bf16[1280,512]{1,0:T(8,128)(2,1)} %shard_map.96.s_ref, bf16[128,2560]{1,0:T(8,128)(2,1)} %copy-done.2, bf16[128,2560]{1,0:T(8,128)(2,1)} %copy-done.10, bf16[128,2560]{1,0:T(8,128)(2,1)} %copy-done.9, bf16[128,2560]{1,0:T(8,128)(2,1)} %copy-done.8), custom_call_target="tpu_custom_call" | custom-call | flops 3355443200 | bytes 6553600 | tf_op jit(solution)/shard_map/pallas_call | solution.py:88
  88.5 10.2 %all-to-all-done.2 = bf16[32,40,1536]{2,1,0:T(8,128)(2,1)} async-done(((bf16[32,40,1536]{2,1,0:T(8,128)(2,1)}), bf16[32,40,1536]{2,1,0:T(8,128)(2,1)}, u32[]{:S(2)}, u32[]{:S(2)}) %all-to-all-start.2) | async-done | bytes 3932192 | tf_op jit(solution)/shard_map/all_to_all | solution.py:310
  98.7 4.7 %all-to-all-start.1 = ((bf16[32,40,2560]{2,1,0:T(8,128)(2,1)}), bf16[32,40,2560]{2,1,0:T(8,128)(2,1)}, u32[]{:S(2)}, u32[]{:S(2)}) async-start(bf16[32,40,2560]{2,1,0:T(8,128)(2,1)} %bitcast.38), calls=%async_computation.1 | async-start | bytes 13107200 | tf_op jit(solution)/shard_map/all_to_all | solution.py:310
  103.4 2.5 %shard_map.94 = (bf16[128,1024]{1,0:T(8,128)(2,1)}, bf16[128,1024]{1,0:T(8,128)(2,1)}, bf16[128,1024]{1,0:T(8,128)(2,1)}, bf16[128,1024]{1,0:T(8,128)(2,1)}) custom-call(s32[1]{0:T(128)} %bitcast.3.y_ref, bf16[128,4096]{1,0:T(8,128)(2,1)} %copy-done.7), custom_call_target="tpu_custom_call" | custom-call | bytes 2097152 | tf_op jit(solution)/shard_map/pallas_call | solution.py:133
  105.9 0.9 collective-permute-start.8
  106.8 1.8 collective-permute-start.13
  108.6 2.7 %collective-permute-start.9 = (bf16[128,1024]{1,0:T(8,128)(2,1)}, bf16[128,1024]{1,0:T(8,128)(2,1)S(1)}, u32[]{:S(2)}, u32[]{:S(2)}) collective-permute-start(bf16[128,1024]{1,0:T(8,128)(2,1)} %get-tuple-element.30), channel_id=1, source_target_pairs={{0,3},{1,0},{2,1},{3,2},{4,7},{5,4},{6,5},{7,6},{8,11},{9,8},{10,9... | collective-permute-start | bytes 786440 | tf_op jit(solution)/shard_map/ppermute | solution.py:270
  111.3 1.7 constant_dynamic-update-slice_fusion.3
  112.9 3.6 %shard_map.93.refs_0_ = bf16[512,1024]{1,0:T(8,128)(2,1)} custom-call(s32[1]{0:T(128)} %bitcast.3.y_ref, bf16[128,1664]{1,0:T(8,128)(2,1)} %copy-done.1, bf16[128,1664]{1,0:T(8,128)(2,1)} %copy-done.5, bf16[128,1664]{1,0:T(8,128)(2,1)} %copy-done.4, bf16[128,1664]{1,0:T(8,128)(2,1)} %copy-done.3, bf16[128,2560]{1,0:T(8,128)(2,1)} %copy-done.2, ...), custom_call_target="tpu_custom_call" | custom-call | bytes 4194304 | tf_op jit(solution)/shard_map/pallas_call | solution.py:113
  116.6 1.5 collective-permute-start.7
  118.8 18.2 %collective-permute-done.9 = bf16[128,1024]{1,0:T(8,128)(2,1)S(1)} collective-permute-done((bf16[128,1024]{1,0:T(8,128)(2,1)}, bf16[128,1024]{1,0:T(8,128)(2,1)S(1)}, u32[]{:S(2)}, u32[]{:S(2)}) %collective-permute-start.9) | collective-permute-done | bytes 262176 | tf_op jit(solution)/shard_map/ppermute | solution.py:270
  137.8 6.4 %collective-permute-done.10 = bf16[128,1024]{1,0:T(8,128)(2,1)S(1)} collective-permute-done((bf16[128,1024]{1,0:T(8,128)(2,1)}, bf16[128,1024]{1,0:T(8,128)(2,1)S(1)}, u32[]{:S(2)}, u32[]{:S(2)}) %collective-permute-start.10) | collective-permute-done | bytes 262176 | tf_op jit(solution)/shard_map/ppermute | solution.py:270
  144.9 0.9 collective-permute-start.11
  145.8 2.6 %collective-permute-start.15 = (bf16[256,1024]{1,0:T(8,128)(2,1)S(1)}, bf16[256,1024]{1,0:T(8,128)(2,1)}, u32[]{:S(2)}, u32[]{:S(2)}) collective-permute-start(bf16[256,1024]{1,0:T(8,128)(2,1)S(1)} %slice.19), channel_id=1, source_target_pairs={{0,3},{1,0},{2,1},{3,2},{4,7},{5,4},{6,5},{7,6},{8,11},{9,8},{10,9... | collective-permute-start | bytes 1572872 | tf_op jit(solution)/shard_map/ppermute | solution.py:270
  148.4 1.0 copy-done.12
  149.4 2.3 copy.25
  152.2 0.8 reduce.4
  153.0 1.1 reshape.58.refs_4_.wt_ref
  154.1 5.6 %collective-permute-done.15.refs_8_ = bf16[256,1024]{1,0:T(8,128)(2,1)} collective-permute-done((bf16[256,1024]{1,0:T(8,128)(2,1)S(1)}, bf16[256,1024]{1,0:T(8,128)(2,1)}, u32[]{:S(2)}, u32[]{:S(2)}) %collective-permute-start.15) | collective-permute-done | bytes 524320 | tf_op jit(solution)/shard_map/ppermute | solution.py:270
  159.7 4.2 %collective-permute-done.14.refs_7_ = bf16[256,1024]{1,0:T(8,128)(2,1)} collective-permute-done((bf16[256,1024]{1,0:T(8,128)(2,1)S(1)}, bf16[256,1024]{1,0:T(8,128)(2,1)}, u32[]{:S(2)}, u32[]{:S(2)}) %collective-permute-start.14) | collective-permute-done | bytes 524320 | tf_op jit(solution)/shard_map/ppermute | solution.py:270
  164.0 10.0 %shard_map.95 = bf16[1024,1024]{1,0:T(8,128)(2,1)} custom-call(s32[1]{0:T(128)} %bitcast.2.t_ref, bf16[512,1024]{1,0:T(8,128)(2,1)} %shard_map.93.refs_0_, bf16[512,1024]{1,0:T(8,128)(2,1)} %collective-permute-done.7.refs_1_, bf16[512,1024]{1,0:T(8,128)(2,1)} %constant_dynamic-update-slice_fusion.refs_2_, bf16[512,1024]{1,0:T(8,128)(2,1)} %collective-permute-done.11.refs_3_, ...), custom_call_target="tpu_custom_call" | custom-call | flops 4294967296 | bytes 10485760 | tf_op jit(solution)/shard_map/pallas_call | solution.py:165
  174.0 1.5 constant_dynamic-slice_fusion
  175.5 2.8 %collective-permute-start.18 = (bf16[256,1024]{1,0:T(8,128)(2,1)S(1)}, bf16[256,1024]{1,0:T(8,128)(2,1)S(1)}, u32[]{:S(2)}, u32[]{:S(2)}) collective-permute-start(bf16[256,1024]{1,0:T(8,128)(2,1)S(1)} %get-tuple-element.40), channel_id=1, source_target_pairs={{0,16},{8,24},{16,0},{24,8},{1,17},{9,25},{17,1},{25,9},{2,18},{10... | collective-permute-start | bytes 1572872 | tf_op jit(solution)/shard_map/ppermute | solution.py:270
  178.2 0.9 collective-permute-start.17
  179.7 8.1 %shard_map.99.refs_2_ = f32[1280,768]{1,0:T(8,128)} custom-call(bf16[1280,1536]{1,0:T(8,128)(2,1)} %bitcast.13.refs_0_.routed_ref, bf16[768,4096]{1,0:T(8,128)(2,1)} %bitcast.30, bf16[768,4096]{1,0:T(8,128)(2,1)} %bitcast.31, bf16[768,4096]{1,0:T(8,128)(2,1)} %bitcast.32), custom_call_target="tpu_custom_call" | custom-call | flops 3019898880 | bytes 6291456 | tf_op jit(solution)/shard_map/pallas_call | solution.py:227
  187.8 7.2 %shard_map.101.refs_0_ = bf16[768,4096]{1,0:T(8,128)(2,1)} custom-call(bf16[1280,1536]{1,0:T(8,128)(2,1)} %bitcast.13.refs_0_.routed_ref, bf16[768,1280]{1,0:T(8,128)(2,1)} %bitcast.35, f32[1280,1]{1,0:T(8,128)} %reshape.58.refs_4_.wt_ref), custom_call_target="tpu_custom_call" | custom-call | flops 3019898880 | bytes 6291456 | tf_op jit(solution)/shard_map/pallas_call | solution.py:257
  195.0 11.4 %shard_map.100 = (bf16[1280,768]{1,0:T(8,128)(2,1)}, f32[1280,1]{1,0:T(8,128)}) custom-call(bf16[1280,2560]{1,0:T(8,128)(2,1)} %bitcast.10.refs_0_.routed_ref, bf16[768,4096]{1,0:T(8,128)(2,1)} %bitcast.33, f32[1280,768]{1,0:T(8,128)} %shard_map.99.refs_2_, bf16[1280,768]{1,0:T(8,128)(2,1)} %bitcast.37, f32[1280,1]{1,0:T(8,128)} %reshape.58.refs_4_.wt_ref), custom_call_target="tpu_custom_call" | custom-call | flops 5033164800 | bytes 10485760 | tf_op jit(solution)/shard_map/pallas_call | solution.py:227
  206.5 1.3 reduce.1
  207.8 0.8 reshape.56
  208.6 11.9 %all-to-all-start.3 = ((f32[128,1,10]{2,1,0:T(1,128)}), f32[128,1,10]{2,1,0:T(1,128)S(1)}, u32[]{:S(2)}, u32[]{:S(2)}) async-start(f32[128,1,10]{2,1,0:T(1,128)} %bitcast.16), calls=%async_computation.3 | async-start | bytes 131072 | tf_op jit(solution)/shard_map/all_to_all | solution.py:355
  220.5 1.4 convert_add_fusion
  222.0 3.4 %collective-permute-start.19 = (bf16[128,1024]{1,0:T(8,128)(2,1)S(1)}, bf16[128,1024]{1,0:T(8,128)(2,1)S(1)}, u32[]{:S(2)}, u32[]{:S(2)}) collective-permute-start(bf16[128,1024]{1,0:T(8,128)(2,1)S(1)} %dynamic-slice_convert_fusion), channel_id=1, source_target_pairs={{0,4},{4,0},{1,5},{5,1},{2,6},{6,2},{3,7},{7,3},{8,12},{12,8},{9,1... | collective-permute-start | bytes 786440 | tf_op jit(solution)/shard_map/ppermute | solution.py:270
  225.3 10.1 %shard_map.102 = bf16[768,4096]{1,0:T(8,128)(2,1)} custom-call(bf16[1280,2560]{1,0:T(8,128)(2,1)} %bitcast.10.refs_0_.routed_ref, bf16[768,1280]{1,0:T(8,128)(2,1)} %bitcast.36, f32[1280,1]{1,0:T(8,128)} %reshape.58.refs_4_.wt_ref, bf16[768,4096]{1,0:T(8,128)(2,1)} %shard_map.101.refs_0_), custom_call_target="tpu_custom_call", output_to_operand_aliasing={{}: (3, {})} | custom-call | flops 5033164800 | bytes 10485760 | tf_op jit(solution)/shard_map/pallas_call | solution.py:257
  (68 shorter events, 12.6 us)
Async XLA Ops:
  0.6 32.1 %collective-permute-start.3 = (bf16[128,4096]{1,0:T(8,128)(2,1)}, bf16[128,4096]{1,0:T(8,128)(2,1)S(1)}, u32[]{:S(2)}, u32[]{:S(2)}) collective-permute-start(bf16[128,4096]{1,0:T(8,128)(2,1)} %bitcast.40), channel_id=1, source_target_pairs={{0,64},{64,0},{1,65},{65,1},{2,66},{66,2},{3,67},{67,3},{4,68},{68... | collective-permute-start | bytes 3145736 | tf_op jit(solution)/shard_map/ppermute | solution.py:270
  5.0 22.5 %copy-start.1 = (bf16[128,1664]{1,0:T(8,128)(2,1)}, bf16[128,1664]{1,0:T(8,128)(2,1)S(1)}, u32[]{:S(2)}) copy-start(bf16[128,1664]{1,0:T(8,128)(2,1)S(1)} %fusion.4.refs_0_.g0) | copy-start | bytes 1277956
  5.0 18.3 %collective-permute-start.2 = (bf16[128,1664]{1,0:T(8,128)(2,1)S(1)}, bf16[128,1664]{1,0:T(8,128)(2,1)S(1)}, u32[]{:S(2)}, u32[]{:S(2)}) collective-permute-start(bf16[128,1664]{1,0:T(8,128)(2,1)S(1)} %fusion.4.refs_0_.g0), channel_id=1, source_target_pairs={{0,2},{1,3},{2,0},{3,1},{4,6},{5,7},{6,4},{7,5},{8,10},{9,11},{10,... | collective-permute-start | bytes 1277960 | tf_op jit(solution)/shard_map/ppermute | solution.py:270
  8.0 19.1 %collective-permute-start.1 = (bf16[128,1664]{1,0:T(8,128)(2,1)S(1)}, bf16[128,1664]{1,0:T(8,128)(2,1)S(1)}, u32[]{:S(2)}, u32[]{:S(2)}) collective-permute-start(bf16[128,1664]{1,0:T(8,128)(2,1)S(1)} %fusion.4.refs_0_.g0), channel_id=1, source_target_pairs={{0,3},{1,0},{2,1},{3,2},{4,7},{5,4},{6,5},{7,6},{8,11},{9,8},{10,9... | collective-permute-start | bytes 1277960 | tf_op jit(solution)/shard_map/ppermute | solution.py:270
  8.7 18.7 %collective-permute-start = (bf16[128,1664]{1,0:T(8,128)(2,1)S(1)}, bf16[128,1664]{1,0:T(8,128)(2,1)S(1)}, u32[]{:S(2)}, u32[]{:S(2)}) collective-permute-start(bf16[128,1664]{1,0:T(8,128)(2,1)S(1)} %fusion.4.refs_0_.g0), channel_id=1, source_target_pairs={{0,1},{1,2},{2,3},{3,0},{4,5},{5,6},{6,7},{7,4},{8,9},{9,10},{10,1... | collective-permute-start | bytes 1277960 | tf_op jit(solution)/shard_map/ppermute | solution.py:270
  12.8 19.8 %all-to-all-start = ((f32[128,1,10]{2,1,0:T(1,128)}), f32[128,1,10]{2,1,0:T(1,128)S(1)}, u32[]{:S(2)}, u32[]{:S(2)}) async-start(f32[128,1,10]{2,1,0:T(1,128)} %copy.24), calls=%async_computation | async-start | bytes 131072 | tf_op jit(solution)/shard_map/all_to_all | solution.py:303
  23.3 4.2 %copy-start.3 = (bf16[128,1664]{1,0:T(8,128)(2,1)}, bf16[128,1664]{1,0:T(8,128)(2,1)S(1)}, u32[]{:S(2)}) copy-start(bf16[128,1664]{1,0:T(8,128)(2,1)S(1)} %collective-permute-done.2.refs_3_.g3) | copy-start | bytes 1277956
  27.1 0.8 copy-start.4
  27.5 0.8 copy-start.5
  32.7 6.3 %copy-start.7 = (bf16[128,4096]{1,0:T(8,128)(2,1)}, bf16[128,4096]{1,0:T(8,128)(2,1)S(1)}, u32[]{:S(2)}) copy-start(bf16[128,4096]{1,0:T(8,128)(2,1)S(1)} %collective-permute-done.3.g_ref) | copy-start | bytes 3145732
  39.0 7.5 %copy-start.6 = (bf16[1,128,4096]{2,1,0:T(8,128)(2,1)S(1)}, bf16[1,128,4096]{2,1,0:T(8,128)(2,1)}, u32[]{:S(2)}) copy-start(bf16[1,128,4096]{2,1,0:T(8,128)(2,1)} %param.6) | copy-start | bytes 3145732
  39.0 59.7 %all-to-all-start.2 = ((bf16[32,40,1536]{2,1,0:T(8,128)(2,1)}), bf16[32,40,1536]{2,1,0:T(8,128)(2,1)}, u32[]{:S(2)}, u32[]{:S(2)}) async-start(bf16[32,40,1536]{2,1,0:T(8,128)(2,1)} %bitcast.39), calls=%async_computation.2 | async-start | bytes 7864320 | tf_op jit(solution)/shard_map/all_to_all | solution.py:310
  46.6 32.4 %copy-start.2 = (bf16[128,2560]{1,0:T(8,128)(2,1)}, bf16[128,2560]{1,0:T(8,128)(2,1)S(1)}, u32[]{:S(2)}) copy-start(bf16[128,2560]{1,0:T(8,128)(2,1)S(1)} %slice.17.refs_4_.g0) | copy-start | bytes 1966084
  46.6 17.8 %collective-permute-start.6 = (bf16[128,2560]{1,0:T(8,128)(2,1)S(1)}, bf16[128,2560]{1,0:T(8,128)(2,1)S(1)}, u32[]{:S(2)}, u32[]{:S(2)}) collective-permute-start(bf16[128,2560]{1,0:T(8,128)(2,1)S(1)} %slice.17.refs_4_.g0), channel_id=1, source_target_pairs={{0,2},{1,3},{2,0},{3,1},{4,6},{5,7},{6,4},{7,5},{8,10},{9,11},{10,... | collective-permute-start | bytes 1966088 | tf_op jit(solution)/shard_map/ppermute | solution.py:270
  49.0 29.3 %collective-permute-start.5 = (bf16[128,2560]{1,0:T(8,128)(2,1)S(1)}, bf16[128,2560]{1,0:T(8,128)(2,1)S(1)}, u32[]{:S(2)}, u32[]{:S(2)}) collective-permute-start(bf16[128,2560]{1,0:T(8,128)(2,1)S(1)} %slice.17.refs_4_.g0), channel_id=1, source_target_pairs={{0,3},{1,0},{2,1},{3,2},{4,7},{5,4},{6,5},{7,6},{8,11},{9,8},{10,9... | collective-permute-start | bytes 1966088 | tf_op jit(solution)/shard_map/ppermute | solution.py:270
  50.0 29.0 %collective-permute-start.4 = (bf16[128,2560]{1,0:T(8,128)(2,1)S(1)}, bf16[128,2560]{1,0:T(8,128)(2,1)S(1)}, u32[]{:S(2)}, u32[]{:S(2)}) collective-permute-start(bf16[128,2560]{1,0:T(8,128)(2,1)S(1)} %slice.17.refs_4_.g0), channel_id=1, source_target_pairs={{0,1},{1,2},{2,3},{3,0},{4,5},{5,6},{6,7},{7,4},{8,9},{9,10},{10,1... | collective-permute-start | bytes 1966088 | tf_op jit(solution)/shard_map/ppermute | solution.py:270
  64.3 14.6 %copy-start.8 = (bf16[128,2560]{1,0:T(8,128)(2,1)}, bf16[128,2560]{1,0:T(8,128)(2,1)S(1)}, u32[]{:S(2)}) copy-start(bf16[128,2560]{1,0:T(8,128)(2,1)S(1)} %collective-permute-done.6.refs_7_.g3) | copy-start | bytes 1966084
  78.3 0.8 copy-start.9
  79.2 0.8 copy-start.10
  98.7 96.3 %all-to-all-start.1 = ((bf16[32,40,2560]{2,1,0:T(8,128)(2,1)}), bf16[32,40,2560]{2,1,0:T(8,128)(2,1)}, u32[]{:S(2)}, u32[]{:S(2)}) async-start(bf16[32,40,2560]{2,1,0:T(8,128)(2,1)} %bitcast.38), calls=%async_computation.1 | async-start | bytes 13107200 | tf_op jit(solution)/shard_map/all_to_all | solution.py:310
  105.9 10.6 %collective-permute-start.8 = (bf16[128,1024]{1,0:T(8,128)(2,1)}, bf16[128,1024]{1,0:T(8,128)(2,1)S(1)}, u32[]{:S(2)}, u32[]{:S(2)}) collective-permute-start(bf16[128,1024]{1,0:T(8,128)(2,1)} %get-tuple-element.29), channel_id=1, source_target_pairs={{0,1},{1,2},{2,3},{3,0},{4,5},{5,6},{6,7},{7,4},{8,9},{9,10},{10,1... | collective-permute-start | bytes 786440 | tf_op jit(solution)/shard_map/ppermute | solution.py:270
  106.8 38.9 %collective-permute-start.13 = (bf16[512,1024]{1,0:T(8,128)(2,1)}, bf16[512,1024]{1,0:T(8,128)(2,1)S(1)}, u32[]{:S(2)}, u32[]{:S(2)}) collective-permute-start(bf16[512,1024]{1,0:T(8,128)(2,1)} %refs_4_), channel_id=1, source_target_pairs={{0,3},{1,0},{2,1},{3,2},{4,7},{5,4},{6,5},{7,6},{8,11},{9,8},{10,9... | collective-permute-start | bytes 3145736 | tf_op jit(solution)/shard_map/ppermute | solution.py:270
  108.6 39.8 %collective-permute-start.12 = (bf16[512,1024]{1,0:T(8,128)(2,1)}, bf16[512,1024]{1,0:T(8,128)(2,1)S(1)}, u32[]{:S(2)}, u32[]{:S(2)}) collective-permute-start(bf16[512,1024]{1,0:T(8,128)(2,1)} %refs_4_), channel_id=1, source_target_pairs={{0,1},{1,2},{2,3},{3,0},{4,5},{5,6},{6,7},{7,4},{8,9},{9,10},{10,1... | collective-permute-start | bytes 3145736 | tf_op jit(solution)/shard_map/ppermute | solution.py:270
  108.6 28.5 %collective-permute-start.9 = (bf16[128,1024]{1,0:T(8,128)(2,1)}, bf16[128,1024]{1,0:T(8,128)(2,1)S(1)}, u32[]{:S(2)}, u32[]{:S(2)}) collective-permute-start(bf16[128,1024]{1,0:T(8,128)(2,1)} %get-tuple-element.30), channel_id=1, source_target_pairs={{0,3},{1,0},{2,1},{3,2},{4,7},{5,4},{6,5},{7,6},{8,11},{9,8},{10,9... | collective-permute-start | bytes 786440 | tf_op jit(solution)/shard_map/ppermute | solution.py:270
  111.3 32.9 %collective-permute-start.10 = (bf16[128,1024]{1,0:T(8,128)(2,1)}, bf16[128,1024]{1,0:T(8,128)(2,1)S(1)}, u32[]{:S(2)}, u32[]{:S(2)}) collective-permute-start(bf16[128,1024]{1,0:T(8,128)(2,1)} %get-tuple-element.31), channel_id=1, source_target_pairs={{0,2},{1,3},{2,0},{3,1},{4,6},{5,7},{6,4},{7,5},{8,10},{9,11},{10,... | collective-permute-start | bytes 786440 | tf_op jit(solution)/shard_map/ppermute | solution.py:270
  112.9 36.5 %copy-start = (bf16[1,1280,768]{2,1,0:T(8,128)(2,1)S(1)}, bf16[1,1280,768]{2,1,0:T(8,128)(2,1)}, u32[]{:S(2)}) copy-start(bf16[1,1280,768]{2,1,0:T(8,128)(2,1)} %param.11) | copy-start | bytes 5898244
  116.6 37.5 %collective-permute-start.7 = (bf16[512,1024]{1,0:T(8,128)(2,1)}, bf16[512,1024]{1,0:T(8,128)(2,1)}, u32[]{:S(2)}, u32[]{:S(2)}) collective-permute-start(bf16[512,1024]{1,0:T(8,128)(2,1)} %shard_map.93.refs_0_), channel_id=1, source_target_pairs={{0,32},{32,0},{1,33},{33,1},{2,34},{34,2},{3,35},{35,3},{4,36},{36... | collective-permute-start | bytes 3145736 | tf_op jit(solution)/shard_map/ppermute | solution.py:270
  144.9 19.1 %collective-permute-start.11 = (bf16[512,1024]{1,0:T(8,128)(2,1)}, bf16[512,1024]{1,0:T(8,128)(2,1)}, u32[]{:S(2)}, u32[]{:S(2)}) collective-permute-start(bf16[512,1024]{1,0:T(8,128)(2,1)} %constant_dynamic-update-slice_fusion.refs_2_), channel_id=1, source_target_pairs={{0,32},{32,0},{1,33},{33,1},{2,34},{34,2},{3,35},{35,3},{4,36},{36... | collective-permute-start | bytes 3145736 | tf_op jit(solution)/shard_map/ppermute | solution.py:270
  145.7 2.7 %copy-start.11 = (bf16[512,1024]{1,0:T(8,128)(2,1)}, bf16[512,1024]{1,0:T(8,128)(2,1)S(1)}, u32[]{:S(2)}) copy-start(bf16[512,1024]{1,0:T(8,128)(2,1)S(1)} %collective-permute-done.13.refs_6_) | copy-start | bytes 3145732
  145.8 14.0 %collective-permute-start.15 = (bf16[256,1024]{1,0:T(8,128)(2,1)S(1)}, bf16[256,1024]{1,0:T(8,128)(2,1)}, u32[]{:S(2)}, u32[]{:S(2)}) collective-permute-start(bf16[256,1024]{1,0:T(8,128)(2,1)S(1)} %slice.19), channel_id=1, source_target_pairs={{0,3},{1,0},{2,1},{3,2},{4,7},{5,4},{6,5},{7,6},{8,11},{9,8},{10,9... | collective-permute-start | bytes 1572872 | tf_op jit(solution)/shard_map/ppermute | solution.py:270
  148.4 1.0 copy-start.12
  149.4 14.5 %collective-permute-start.14 = (bf16[256,1024]{1,0:T(8,128)(2,1)S(1)}, bf16[256,1024]{1,0:T(8,128)(2,1)}, u32[]{:S(2)}, u32[]{:S(2)}) collective-permute-start(bf16[256,1024]{1,0:T(8,128)(2,1)S(1)} %slice.18), channel_id=1, source_target_pairs={{0,1},{1,2},{2,3},{3,0},{4,5},{5,6},{6,7},{7,4},{8,9},{9,10},{10,1... | collective-permute-start | bytes 1572872 | tf_op jit(solution)/shard_map/ppermute | solution.py:270
  175.5 33.1 %collective-permute-start.18 = (bf16[256,1024]{1,0:T(8,128)(2,1)S(1)}, bf16[256,1024]{1,0:T(8,128)(2,1)S(1)}, u32[]{:S(2)}, u32[]{:S(2)}) collective-permute-start(bf16[256,1024]{1,0:T(8,128)(2,1)S(1)} %get-tuple-element.40), channel_id=1, source_target_pairs={{0,16},{8,24},{16,0},{24,8},{1,17},{9,25},{17,1},{25,9},{2,18},{10... | collective-permute-start | bytes 1572872 | tf_op jit(solution)/shard_map/ppermute | solution.py:270
  178.2 30.3 %collective-permute-start.17 = (bf16[256,1024]{1,0:T(8,128)(2,1)S(1)}, bf16[256,1024]{1,0:T(8,128)(2,1)S(1)}, u32[]{:S(2)}, u32[]{:S(2)}) collective-permute-start(bf16[256,1024]{1,0:T(8,128)(2,1)S(1)} %get-tuple-element.41), channel_id=1, source_target_pairs={{0,24},{8,0},{16,8},{24,16},{1,25},{9,1},{17,9},{25,17},{2,26},{10... | collective-permute-start | bytes 1572872 | tf_op jit(solution)/shard_map/ppermute | solution.py:270
  179.1 29.5 %collective-permute-start.16 = (bf16[256,1024]{1,0:T(8,128)(2,1)S(1)}, bf16[256,1024]{1,0:T(8,128)(2,1)S(1)}, u32[]{:S(2)}, u32[]{:S(2)}) collective-permute-start(bf16[256,1024]{1,0:T(8,128)(2,1)S(1)} %get-tuple-element.42), channel_id=1, source_target_pairs={{0,8},{8,16},{16,24},{24,0},{1,9},{9,17},{17,25},{25,1},{2,10},{10... | collective-permute-start | bytes 1572872 | tf_op jit(solution)/shard_map/ppermute | solution.py:270
  208.6 26.9 %all-to-all-start.3 = ((f32[128,1,10]{2,1,0:T(1,128)}), f32[128,1,10]{2,1,0:T(1,128)S(1)}, u32[]{:S(2)}, u32[]{:S(2)}) async-start(f32[128,1,10]{2,1,0:T(1,128)} %bitcast.16), calls=%async_computation.3 | async-start | bytes 131072 | tf_op jit(solution)/shard_map/all_to_all | solution.py:355
  222.0 13.9 %copy-start.13 = (s32[1,128,8]{1,2,0:T(8,128)S(1)}, s32[1,128,8]{1,2,0:T(8,128)}, u32[]{:S(2)}) copy-start(s32[1,128,8]{1,2,0:T(8,128)} %param.7) | copy-start | bytes 12292
  222.0 14.5 %collective-permute-start.19 = (bf16[128,1024]{1,0:T(8,128)(2,1)S(1)}, bf16[128,1024]{1,0:T(8,128)(2,1)S(1)}, u32[]{:S(2)}, u32[]{:S(2)}) collective-permute-start(bf16[128,1024]{1,0:T(8,128)(2,1)S(1)} %dynamic-slice_convert_fusion), channel_id=1, source_target_pairs={{0,4},{4,0},{1,5},{5,1},{2,6},{6,2},{3,7},{7,3},{8,12},{12,8},{9,1... | collective-permute-start | bytes 786440 | tf_op jit(solution)/shard_map/ppermute | solution.py:270

commit v3 on v2

--- a/solution.py
+++ b/solution.py
@@ -83,7 +83,7 @@
     o_ref[...] = jnp.dot(s_ref[...], g, preferred_element_type=F32).astype(BF)
 
 
-def dispatch(s, blocks, width):
+def dispatch(s, blocks, width, weight=1):
     rows = s.shape[0]
     return pl.pallas_call(
         dispatch_kernel,
@@ -93,7 +93,7 @@
         + [pl.BlockSpec((128, TILE), lambda i: (0, i)) for _ in blocks],
         out_specs=pl.BlockSpec((rows, TILE), lambda i: (0, i)),
         compiler_params=params(),
-        cost_estimate=cost(2 * rows * 512 * width, 2 * rows * width),
+        cost_estimate=cost(2 * rows * 512 * width * weight, 2 * rows * width),
     )(s, *blocks)
 
 
@@ -146,7 +146,10 @@
     @pl.when(pl.program_id(0) == 0)
     def _():
         for i, f in enumerate(features):
-            ft[:, i * 512 : (i + 1) * 512] = f[...].T
+            turned = f[...].T
+            for j in range(8):
+                to, of = (j % 2 * 4 + j // 2) * 128, j * 128
+                ft[to : to + 128, i * 512 : (i + 1) * 512] = turned[of : of + 128]
 
     for i in range(4):
         who = t_ref[0] ^ i
@@ -195,14 +198,24 @@
         return
     h_ref, wt_ref, hid_ref, part_ref = refs[-4:]
     hid_ref[...] = (wt_ref[...] * term).astype(BF)
-    part_ref[...] = jnp.sum(term * h_ref[...].astype(F32), axis=1, keepdims=True)
+    part = jnp.sum(term * h_ref[...].astype(F32), axis=1, keepdims=True)
+    rows, peers = part.shape[0], part_ref.shape[0]
+    row = lax.broadcasted_iota(jnp.int32, (rows, 128), 0)
+    lane = lax.broadcasted_iota(jnp.int32, (rows, 128), 1)
+    tenth = lax.shift_right_logical(row * 6554, 16)
+    spread = jnp.where(lane == row - tenth * 10, part, 0.0)
+    peer = lax.broadcasted_iota(jnp.int32, (peers, rows), 0)
+    col = lax.shift_right_logical(lax.broadcasted_iota(jnp.int32, (peers, rows), 1) * 6554, 16)
+    part_ref[...] = jnp.dot(
+        (peer == col).astype(F32), spread, precision=lax.Precision.HIGHEST, preferred_element_type=F32
+    )
 
 
 def project(chunk, routed, w, before, hidden, weight):
     rows, width = routed.shape
     hid = w.shape[0]
     first, last = chunk == 0, chunk == len(CHUNKS) - 1
-    tile = 256
+    tile = 320
     across = pl.BlockSpec((tile, hid), lambda i: (i, 0))
     narrow = pl.BlockSpec((tile, 1), lambda i: (i, 0))
     deep = WIDE if CHUNKS[chunk][0] else width
@@ -216,8 +229,8 @@
     if last:
         in_specs += [across, narrow]
         args += [hidden, weight]
-        out_shape = [jax.ShapeDtypeStruct((rows, hid), BF), jax.ShapeDtypeStruct((rows, 1), F32)]
-        out_specs = [across, narrow]
+        out_shape = [jax.ShapeDtypeStruct((rows, hid), BF), jax.ShapeDtypeStruct((rows // 10, 128), F32)]
+        out_specs = [across, pl.BlockSpec((tile // 10, 128), lambda i: (i, 0))]
     else:
         out_shape, out_specs = jax.ShapeDtypeStruct((rows, hid), F32), across
 
@@ -292,8 +305,9 @@
     (at_near, near), (at_far, far) = CHUNKS
     ids = expert_ids[0].T
     label = jnp.pad(ids.astype(BF), ((0, g.shape[0] - ids.shape[0]), (0, 0)))
-    low = ring_gather(jnp.concatenate([g[:, at_near : at_near + near], label], axis=1))
-    across = swap(g, "zlo")
+    low = jnp.concatenate([g[:, at_near : at_near + near], label], axis=1)
+    across = swap(after(g, low), "zlo")
+    low = ring_gather(low)
     spread = place(y, low, slots)
     named = ids[:, None, :] == jnp.arange(n_experts, dtype=jnp.int32)[None, :, None]
     rank = ranks(jnp.any(named, axis=0))
@@ -318,43 +332,41 @@
     parts = quarters(y, across)
     other = [ring(q, shift) if shift else q for q, shift in zip(parts, (0, 1, -1, 2))]
     mine = select(y, low, high, width)
-    other = jnp.concatenate(other, axis=0)
-    features = [mine, swap(mine, "core"), other, swap(other, "core")]
     rows1 = dispatch(spread, high, far)
     routed1 = send(rows1)
-    t = (lax.axis_index("zlo") * 2 + lax.axis_index("core")).reshape(1)
-    half = attn_out.shape[0] // 2
-    contexts += [ring(contexts[1][:half], 1), ring(contexts[2][half:], -1)]
-    partial = outer(t, features, contexts)
-
     weight = got_prob.reshape(slots, 1)
     hidden = hidden_saved[0]
     hidden_t = hidden.T
     w = w_down[0]
-    x = lax.axis_index("x")
-    quarter = partial.shape[0] // 4
-
-    def piece(shift):
-        return lax.dynamic_slice_in_dim(partial, ((x + shift) & 3) * quarter, quarter, 0)
-
-    pieces = [ring(piece(shift), shift, "x") for shift in (1, -1, 2)]
     proj = project(0, routed0, w, None, hidden, weight)
     down = weigh(0, routed0, hidden_t, weight, width, None)
+
+    t = (lax.axis_index("zlo") * 2 + lax.axis_index("core")).reshape(1)
+    half = attn_out.shape[0] // 2
+    contexts += [ring(contexts[1][:half], 1), ring(contexts[2][half:], -1)]
+    *other, proj, down = lax.optimization_barrier((*other, proj, down))
+    other = jnp.concatenate(other, axis=0)
+    features = [mine, swap(mine, "core"), other, swap(other, "core")]
+    partial = outer(t, features, contexts)
+
+    x, zhi = lax.axis_index("x"), lax.axis_index("zhi")
+    half, eighth = partial.shape[0] // 2, partial.shape[0] // 8
+    come = swap(lax.dynamic_slice_in_dim(partial, (1 - zhi) * half, half, 0), "zhi")
     grad_hid, part = project(1, routed1, w, proj, hidden, weight)
-    part = part.reshape(n_experts, 1, cap)
-    *pieces, part = lax.optimization_barrier((*pieces, part))
-    sums = piece(0).astype(F32)
-    for got in pieces:
-        sums = sums + got.astype(F32)
-    zhi = lax.axis_index("zhi")
-    eighth = quarter // 2
-    give = lax.dynamic_slice_in_dim(sums, (1 - zhi) * eighth, eighth, 0).astype(BF)
-    keep = lax.dynamic_slice_in_dim(sums, zhi * eighth, eighth, 0)
-    grad_oproj = (keep + swap(give, "zhi").astype(F32)).astype(BF)
+    come = after(come, part)
+    sums = lax.dynamic_slice_in_dim(partial, zhi * half, half, 0).astype(F32) + come.astype(F32)
+
+    def piece(shift):
+        return lax.dynamic_slice_in_dim(sums, ((x + shift) & 3) * eighth, eighth, 0)
+
+    pieces = [ring(piece(shift).astype(BF), shift, "x") for shift in (1, -1, 2)]
     down = weigh(1, routed1, hidden_t, weight, width, down)
-    returned = lax.all_to_all(
-        part, ALL, split_axis=0, concat_axis=0, tiled=True
-    ).reshape(n_experts, cap)
+    *pieces, _ = lax.optimization_barrier((*pieces, down))
+    total = piece(0)
+    for come in pieces:
+        total = total + come.astype(F32)
+    grad_oproj = total.astype(BF)
+    returned = lax.all_to_all(part[:, None, :], ALL, split_axis=0, concat_axis=0, tiled=True)[:, 0, :cap]
     value = jnp.sum(jnp.where(at, returned[:, :, None], 0.0), axis=1)
     grad_prob = jnp.sum(jnp.where(named, value[None], 0.0), axis=1).T[None]
     return (grad_prob, grad_hid[None], down[None], grad_oproj)

time: 239 us -> 232 us (0.971)
  starting transfers between devices: 63.4 us -> 57.1 us
    all_to_all x2, waiting for transfers between devices: 10.2 us -> 26.4 us  [send(): lax.all_to_all(rows.reshape(n_experts // 4, 4 * cap, -1), PEERS, split_ax...]
    ppermute x20, waiting for transfers between devices: 67.1 us -> 52.5 us  [ring(): return lax.ppermute(x, axis, [(i, (i + shift) % n) for i in range(n)])]
    all_to_all x1, starting transfers between devices: 11.9 us -> 7.22 us  [local(): lax.all_to_all(part[:, None, :], ALL, split_axis=0, concat_axis=0, tiled=...]
    unnamed x32 -> x34, local copies, waits for them, and re-layouts: 8.24 us -> 6.21 us
  transfers between devices with their start and end apart: 24 -> 24, of which waited for: 11 -> 10; matrix products, arithmetic and copies ran while one was open for 8% -> 7% of each run, Pallas kernels for 27% -> 28%
where the time goes in v3:
time: 232 us; the launch traced here: 231 us
  waiting for transfers between devices  81.1 us (35%)
  Pallas kernels  69.9 us (30%)
  starting transfers between devices  57.1 us (25%)
  local copies, waits for them, and re-layouts  12.9 us (6%)
  other arithmetic  8.54 us (4%)
    ppermute x20, waiting for transfers between devices, ring(): return lax.ppermute(x, axis, [(i, (i + shift) % n) for i in range(n)])  52.5 us
    ppermute x20, starting transfers between devices, ring(): return lax.ppermute(x, axis, [(i, (i + shift) % n) for i in range(n)])  27.5 us
    all_to_all x2, waiting for transfers between devices, send(): lax.all_to_all(rows.reshape(n_experts // 4, 4 * cap, -1), PEERS, split_ax...  26.4 us
    pallas_call x2, Pallas kernels, project(): pl.pallas_call(kernel, out_shape=out_shape, grid=(rows // tile,), in_spec...  19.1 us
    pallas_call x2, Pallas kernels, weigh(): pl.pallas_call(down_kernel, out_shape=jax.ShapeDtypeStruct((hid, full), B...  17.4 us
    pallas_call x2, Pallas kernels, dispatch(): pl.pallas_call(dispatch_kernel, out_shape=jax.ShapeDtypeStruct((rows, wid...  14.8 us
    all_to_all x2, starting transfers between devices, send(): lax.all_to_all(rows.reshape(n_experts // 4, 4 * cap, -1), PEERS, split_ax...  12.8 us
    pallas_call x1, Pallas kernels, outer(): pl.pallas_call(outer_kernel, out_shape=jax.ShapeDtypeStruct((n, wide), BF...  9.99 us
  transfers between devices with their start and end apart: 24, of which 10 were waited for; matrix products, arithmetic and copies ran while one was open for 7% of the time, Pallas kernels for 28%

profile of v3, /device:TPU:1, one launch (start us, length us, event | category | flops | bytes accessed | tf_op | source)
XLA Modules:
  0.0 230.6 jit_solution(8032562260719860434)
XLA Ops:
  1.3 1.0 slice.20
  2.4 2.5 %collective-permute-start.6 = (bf16[128,4096]{1,0:T(8,128)(2,1)}, bf16[128,4096]{1,0:T(8,128)(2,1)S(1)}, u32[]{:S(2)}, u32[]{:S(2)}) collective-permute-start(bf16[128,4096]{1,0:T(8,128)(2,1)} %bitcast.44), channel_id=1, source_target_pairs={{0,64},{64,0},{1,65},{65,1},{2,66},{66,2},{3,67},{67,3},{4,68},{68... | collective-permute-start | bytes 3145736 | tf_op jit(solution)/shard_map/ppermute | solution.py:283
  4.9 1.3 collective-permute-start
  6.2 1.4 collective-permute-start.1
  7.7 1.6 collective-permute-start.2
  12.7 9.7 %all-to-all-start.1 = ((f32[128,1,10]{2,1,0:T(1,128)}), f32[128,1,10]{2,1,0:T(1,128)S(1)}, u32[]{:S(2)}, u32[]{:S(2)}) async-start(f32[128,1,10]{2,1,0:T(1,128)} %copy.24), calls=%async_computation.1 | async-start | bytes 131072 | tf_op jit(solution)/shard_map/all_to_all | solution.py:317
  22.5 4.4 %collective-permute-done.2.refs_3_.g3 = bf16[128,1664]{1,0:T(8,128)(2,1)S(1)} collective-permute-done((bf16[128,1664]{1,0:T(8,128)(2,1)S(1)}, bf16[128,1664]{1,0:T(8,128)(2,1)S(1)}, u32[]{:S(2)}, u32[]{:S(2)}) %collective-permute-start.2) | collective-permute-done | bytes 426016 | tf_op jit(solution)/shard_map/ppermute | solution.py:283
  27.7 2.6 %shard_map.93.s_ref = bf16[1280,512]{1,0:T(8,128)(2,1)} custom-call(s32[1]{0:T(128)} %bitcast.2.y_ref, bf16[128,1664]{1,0:T(8,128)(2,1)} %copy-done.1, bf16[128,1664]{1,0:T(8,128)(2,1)} %copy-done.3, bf16[128,1664]{1,0:T(8,128)(2,1)} %copy-done.4, bf16[128,1664]{1,0:T(8,128)(2,1)} %copy-done.5), custom_call_target="tpu_custom_call" | custom-call | flops 100000000 | bytes 2000000 | tf_op jit(solution)/shard_map/pallas_call | solution.py:69
  30.3 2.2 all-to-all-done.1
  32.6 6.3 %shard_map.96 = bf16[1280,1536]{1,0:T(8,128)(2,1)} custom-call(bf16[1280,512]{1,0:T(8,128)(2,1)} %shard_map.93.s_ref, bf16[128,1664]{1,0:T(8,128)(2,1)} %copy-done.1, bf16[128,1664]{1,0:T(8,128)(2,1)} %copy-done.3, bf16[128,1664]{1,0:T(8,128)(2,1)} %copy-done.4, bf16[128,1664]{1,0:T(8,128)(2,1)} %copy-done.5), custom_call_target="tpu_custom_call" | custom-call | flops 2013265920 | bytes 3932160 | tf_op jit(solution)/shard_map/pallas_call | solution.py:88
  38.9 7.9 %all-to-all-start.2 = ((bf16[32,40,1536]{2,1,0:T(8,128)(2,1)}), bf16[32,40,1536]{2,1,0:T(8,128)(2,1)}, u32[]{:S(2)}, u32[]{:S(2)}) async-start(bf16[32,40,1536]{2,1,0:T(8,128)(2,1)} %bitcast.42), calls=%async_computation.2 | async-start | bytes 7864320 | tf_op jit(solution)/shard_map/all_to_all | solution.py:324
  46.9 0.9 collective-permute-start.3
  47.8 1.8 collective-permute-start.4
  49.8 14.5 %collective-permute-done.3.g1.refs_5_ = bf16[128,2560]{1,0:T(8,128)(2,1)S(1)} collective-permute-done((bf16[128,2560]{1,0:T(8,128)(2,1)S(1)}, bf16[128,2560]{1,0:T(8,128)(2,1)S(1)}, u32[]{:S(2)}, u32[]{:S(2)}) %collective-permute-start.3) | collective-permute-done | bytes 655392 | tf_op jit(solution)/shard_map/ppermute | solution.py:283
  64.3 14.2 %collective-permute-done.5.g3.refs_7_ = bf16[128,2560]{1,0:T(8,128)(2,1)S(1)} collective-permute-done((bf16[128,2560]{1,0:T(8,128)(2,1)S(1)}, bf16[128,2560]{1,0:T(8,128)(2,1)S(1)}, u32[]{:S(2)}, u32[]{:S(2)}) %collective-permute-start.5) | collective-permute-done | bytes 655392 | tf_op jit(solution)/shard_map/ppermute | solution.py:283
  78.5 0.9 copy-done.11
  79.4 8.5 %shard_map.94 = bf16[1280,2560]{1,0:T(8,128)(2,1)} custom-call(bf16[1280,512]{1,0:T(8,128)(2,1)} %shard_map.93.s_ref, bf16[128,2560]{1,0:T(8,128)(2,1)} %copy-done.2, bf16[128,2560]{1,0:T(8,128)(2,1)} %copy-done.9, bf16[128,2560]{1,0:T(8,128)(2,1)} %copy-done.10, bf16[128,2560]{1,0:T(8,128)(2,1)} %copy-done.11), custom_call_target="tpu_custom_call" | custom-call | flops 3355443200 | bytes 6553600 | tf_op jit(solution)/shard_map/pallas_call | solution.py:88
  87.9 11.1 %all-to-all-done.2 = bf16[32,40,1536]{2,1,0:T(8,128)(2,1)} async-done(((bf16[32,40,1536]{2,1,0:T(8,128)(2,1)}), bf16[32,40,1536]{2,1,0:T(8,128)(2,1)}, u32[]{:S(2)}, u32[]{:S(2)}) %all-to-all-start.2) | async-done | bytes 3932192 | tf_op jit(solution)/shard_map/all_to_all | solution.py:324
  99.0 4.8 %all-to-all-start = ((bf16[32,40,2560]{2,1,0:T(8,128)(2,1)}), bf16[32,40,2560]{2,1,0:T(8,128)(2,1)}, u32[]{:S(2)}, u32[]{:S(2)}) async-start(bf16[32,40,2560]{2,1,0:T(8,128)(2,1)} %bitcast.41), calls=%async_computation | async-start | bytes 13107200 | tf_op jit(solution)/shard_map/all_to_all | solution.py:324
  103.9 2.3 %copy.25 = bf16[1,1280,768]{1,2,0:T(8,128)(2,1)} copy(bf16[1,1280,768]{2,1,0:T(8,128)(2,1)S(1)} %copy-done) | data formatting | bytes 3932160 | tf_op args[5]
  106.2 0.9 collective-permute-start.12
  107.1 1.8 collective-permute-start.13
  108.9 2.5 %shard_map.95 = (bf16[128,1024]{1,0:T(8,128)(2,1)}, bf16[128,1024]{1,0:T(8,128)(2,1)}, bf16[128,1024]{1,0:T(8,128)(2,1)}, bf16[128,1024]{1,0:T(8,128)(2,1)}) custom-call(s32[1]{0:T(128)} %bitcast.2.y_ref, bf16[128,4096]{1,0:T(8,128)(2,1)} %copy-done.7), custom_call_target="tpu_custom_call" | custom-call | bytes 2097152 | tf_op jit(solution)/shard_map/pallas_call | solution.py:133
  111.4 2.7 %collective-permute-start.8 = (bf16[128,1024]{1,0:T(8,128)(2,1)}, bf16[128,1024]{1,0:T(8,128)(2,1)S(1)}, u32[]{:S(2)}, u32[]{:S(2)}) collective-permute-start(bf16[128,1024]{1,0:T(8,128)(2,1)} %get-tuple-element.34), channel_id=1, source_target_pairs={{0,3},{1,0},{2,1},{3,2},{4,7},{5,4},{6,5},{7,6},{8,11},{9,8},{10,9... | collective-permute-start | bytes 786440 | tf_op jit(solution)/shard_map/ppermute | solution.py:283
  115.4 1.1 reshape.54.wt_ref.refs_4_
  116.4 3.5 %shard_map.101.refs_0_ = bf16[512,1024]{1,0:T(8,128)(2,1)} custom-call(s32[1]{0:T(128)} %bitcast.2.y_ref, bf16[128,1664]{1,0:T(8,128)(2,1)} %copy-done.1, bf16[128,1664]{1,0:T(8,128)(2,1)} %copy-done.3, bf16[128,1664]{1,0:T(8,128)(2,1)} %copy-done.4, bf16[128,1664]{1,0:T(8,128)(2,1)} %copy-done.5, bf16[128,2560]{1,0:T(8,128)(2,1)} %copy-done.2, ...), custom_call_target="tpu_custom_call" | custom-call | bytes 4194304 | tf_op jit(solution)/shard_map/pallas_call | solution.py:113
  119.9 7.4 %shard_map.97.refs_2_ = f32[1280,768]{1,0:T(8,128)} custom-call(bf16[1280,1536]{1,0:T(8,128)(2,1)} %bitcast.12.refs_0_.routed_ref, bf16[768,4096]{1,0:T(8,128)(2,1)} %bitcast.33, bf16[768,4096]{1,0:T(8,128)(2,1)} %bitcast.34, bf16[768,4096]{1,0:T(8,128)(2,1)} %bitcast.35), custom_call_target="tpu_custom_call" | custom-call | flops 3019898880 | bytes 6291456 | tf_op jit(solution)/shard_map/pallas_call | solution.py:240
  127.4 7.3 %shard_map.98.refs_0_ = bf16[768,4096]{1,0:T(8,128)(2,1)} custom-call(bf16[1280,1536]{1,0:T(8,128)(2,1)} %bitcast.12.refs_0_.routed_ref, bf16[768,1280]{1,0:T(8,128)(2,1)} %bitcast.38, f32[1280,1]{1,0:T(8,128)} %reshape.54.wt_ref.refs_4_), custom_call_target="tpu_custom_call" | custom-call | flops 3019898880 | bytes 6291456 | tf_op jit(solution)/shard_map/pallas_call | solution.py:270
  134.7 3.3 %collective-permute-done.7 = bf16[128,1024]{1,0:T(8,128)(2,1)S(1)} collective-permute-done((bf16[128,1024]{1,0:T(8,128)(2,1)}, bf16[128,1024]{1,0:T(8,128)(2,1)S(1)}, u32[]{:S(2)}, u32[]{:S(2)}) %collective-permute-start.7) | collective-permute-done | bytes 262176 | tf_op jit(solution)/shard_map/ppermute | solution.py:283
  138.0 1.2 collective-permute-start.10
  139.2 4.6 %collective-permute-done.9 = bf16[128,1024]{1,0:T(8,128)(2,1)S(1)} collective-permute-done((bf16[128,1024]{1,0:T(8,128)(2,1)}, bf16[128,1024]{1,0:T(8,128)(2,1)S(1)}, u32[]{:S(2)}, u32[]{:S(2)}) %collective-permute-start.9) | collective-permute-done | bytes 262176 | tf_op jit(solution)/shard_map/ppermute | solution.py:283
  146.7 0.9 collective-permute-start.11
  147.6 0.9 collective-permute-start.14
  148.5 1.1 slice.24
  149.6 2.0 collective-permute-start.15
  151.6 11.0 %collective-permute-done.14.refs_7_ = bf16[256,1024]{1,0:T(8,128)(2,1)} collective-permute-done((bf16[256,1024]{1,0:T(8,128)(2,1)S(1)}, bf16[256,1024]{1,0:T(8,128)(2,1)}, u32[]{:S(2)}, u32[]{:S(2)}) %collective-permute-start.14) | collective-permute-done | bytes 524320 | tf_op jit(solution)/shard_map/ppermute | solution.py:283
  163.0 10.0 %shard_map.102 = bf16[1024,1024]{1,0:T(8,128)(2,1)} custom-call(s32[1]{0:T(128)} %bitcast.24.t_ref, bf16[512,1024]{1,0:T(8,128)(2,1)} %shard_map.101.refs_0_, bf16[512,1024]{1,0:T(8,128)(2,1)} %collective-permute-done.10.refs_1_, bf16[512,1024]{1,0:T(8,128)(2,1)} %constant_dynamic-update-slice_fusion.refs_2_, ...), custom_call_target="tpu_custom_call" | custom-call | flops 4294967296 | bytes 10485760 | tf_op jit(solution)/shard_map/pallas_call | solution.py:168
  173.0 1.3 constant_dynamic-slice_fusion
  174.3 2.7 %collective-permute-start.16 = (bf16[512,1024]{1,0:T(8,128)(2,1)S(1)}, bf16[512,1024]{1,0:T(8,128)(2,1)S(1)}, u32[]{:S(2)}, u32[]{:S(2)}) collective-permute-start(bf16[512,1024]{1,0:T(8,128)(2,1)S(1)} %constant_dynamic-slice_fusion), channel_id=1, source_target_pairs={{0,4},{4,0},{1,5},{5,1},{2,6},{6,2},{3,7},{7,3},{8,12},{12,8},{9,1... | collective-permute-start | bytes 3145736 | tf_op jit(solution)/shard_map/ppermute | solution.py:283
  177.0 15.3 %all-to-all-done = bf16[32,40,2560]{2,1,0:T(8,128)(2,1)} async-done(((bf16[32,40,2560]{2,1,0:T(8,128)(2,1)}), bf16[32,40,2560]{2,1,0:T(8,128)(2,1)}, u32[]{:S(2)}, u32[]{:S(2)}) %all-to-all-start) | async-done | bytes 6553632 | tf_op jit(solution)/shard_map/all_to_all | solution.py:324
  192.3 11.7 %shard_map.99 = (bf16[1280,768]{1,0:T(8,128)(2,1)}, f32[128,128]{1,0:T(8,128)}) custom-call(bf16[1280,2560]{1,0:T(8,128)(2,1)} %bitcast.8.refs_0_.routed_ref, bf16[768,4096]{1,0:T(8,128)(2,1)} %bitcast.36, f32[1280,768]{1,0:T(8,128)} %shard_map.97.refs_2_, bf16[1280,768]{1,0:T(8,128)(2,1)} %bitcast.40, f32[1280,1]{1,0:T(8,128)} %reshape.54.wt_ref.refs_4_), custom_call_target="tpu_custom_call" | custom-call | flops 5033164800 | bytes 10485760 | tf_op jit(solution)/shard_map/pallas_call | solution.py:240
  204.0 7.2 %all-to-all-start.3 = ((f32[128,1,128]{2,1,0:T(1,128)}), f32[128,1,128]{2,1,0:T(1,128)S(1)}, u32[]{:S(2)}, u32[]{:S(2)}) async-start(f32[128,1,128]{2,1,0:T(1,128)} %bitcast.50), calls=%async_computation.3 | async-start | bytes 131072 | tf_op jit(solution)/shard_map/all_to_all | solution.py:369
  211.2 1.6 convert_add_fusion
  213.0 1.5 collective-permute-start.17
  214.5 1.2 collective-permute-start.18
  215.8 1.8 collective-permute-start.19
  217.5 10.1 %shard_map.100 = bf16[768,4096]{1,0:T(8,128)(2,1)} custom-call(bf16[1280,2560]{1,0:T(8,128)(2,1)} %bitcast.8.refs_0_.routed_ref, bf16[768,1280]{1,0:T(8,128)(2,1)} %bitcast.39, f32[1280,1]{1,0:T(8,128)} %reshape.54.wt_ref.refs_4_, bf16[768,4096]{1,0:T(8,128)(2,1)} %shard_map.98.refs_0_), custom_call_target="tpu_custom_call", output_to_operand_aliasing={{}: (3, {})} | custom-call | flops 5033164800 | bytes 10485760 | tf_op jit(solution)/shard_map/pallas_call | solution.py:270
  228.6 2.0 add_convert_fusion
  (68 shorter events, 11.0 us)
Async XLA Ops:
  2.4 24.5 %copy-start.1 = (bf16[128,1664]{1,0:T(8,128)(2,1)}, bf16[128,1664]{1,0:T(8,128)(2,1)S(1)}, u32[]{:S(2)}) copy-start(bf16[128,1664]{1,0:T(8,128)(2,1)S(1)} %fusion.4.refs_0_.g0) | copy-start | bytes 1277956
  2.4 30.2 %collective-permute-start.6 = (bf16[128,4096]{1,0:T(8,128)(2,1)}, bf16[128,4096]{1,0:T(8,128)(2,1)S(1)}, u32[]{:S(2)}, u32[]{:S(2)}) collective-permute-start(bf16[128,4096]{1,0:T(8,128)(2,1)} %bitcast.44), channel_id=1, source_target_pairs={{0,64},{64,0},{1,65},{65,1},{2,66},{66,2},{3,67},{67,3},{4,68},{68... | collective-permute-start | bytes 3145736 | tf_op jit(solution)/shard_map/ppermute | solution.py:283
  4.9 17.5 %collective-permute-start = (bf16[128,1664]{1,0:T(8,128)(2,1)S(1)}, bf16[128,1664]{1,0:T(8,128)(2,1)S(1)}, u32[]{:S(2)}, u32[]{:S(2)}) collective-permute-start(bf16[128,1664]{1,0:T(8,128)(2,1)S(1)} %fusion.4.refs_0_.g0), channel_id=1, source_target_pairs={{0,1},{1,2},{2,3},{3,0},{4,5},{5,6},{6,7},{7,4},{8,9},{9,10},{10,1... | collective-permute-start | bytes 1277960 | tf_op jit(solution)/shard_map/ppermute | solution.py:283
  6.2 16.2 %collective-permute-start.1 = (bf16[128,1664]{1,0:T(8,128)(2,1)S(1)}, bf16[128,1664]{1,0:T(8,128)(2,1)S(1)}, u32[]{:S(2)}, u32[]{:S(2)}) collective-permute-start(bf16[128,1664]{1,0:T(8,128)(2,1)S(1)} %fusion.4.refs_0_.g0), channel_id=1, source_target_pairs={{0,3},{1,0},{2,1},{3,2},{4,7},{5,4},{6,5},{7,6},{8,11},{9,8},{10,9... | collective-permute-start | bytes 1277960 | tf_op jit(solution)/shard_map/ppermute | solution.py:283
  7.7 19.2 %collective-permute-start.2 = (bf16[128,1664]{1,0:T(8,128)(2,1)S(1)}, bf16[128,1664]{1,0:T(8,128)(2,1)S(1)}, u32[]{:S(2)}, u32[]{:S(2)}) collective-permute-start(bf16[128,1664]{1,0:T(8,128)(2,1)S(1)} %fusion.4.refs_0_.g0), channel_id=1, source_target_pairs={{0,2},{1,3},{2,0},{3,1},{4,6},{5,7},{6,4},{7,5},{8,10},{9,11},{10,... | collective-permute-start | bytes 1277960 | tf_op jit(solution)/shard_map/ppermute | solution.py:283
  12.7 19.8 %all-to-all-start.1 = ((f32[128,1,10]{2,1,0:T(1,128)}), f32[128,1,10]{2,1,0:T(1,128)S(1)}, u32[]{:S(2)}, u32[]{:S(2)}) async-start(f32[128,1,10]{2,1,0:T(1,128)} %copy.24), calls=%async_computation.1 | async-start | bytes 131072 | tf_op jit(solution)/shard_map/all_to_all | solution.py:317
  22.4 4.5 %copy-start.3 = (bf16[128,1664]{1,0:T(8,128)(2,1)}, bf16[128,1664]{1,0:T(8,128)(2,1)S(1)}, u32[]{:S(2)}) copy-start(bf16[128,1664]{1,0:T(8,128)(2,1)S(1)} %collective-permute-done.refs_1_.g1) | copy-start | bytes 1277956
  22.5 4.5 %copy-start.4 = (bf16[128,1664]{1,0:T(8,128)(2,1)}, bf16[128,1664]{1,0:T(8,128)(2,1)S(1)}, u32[]{:S(2)}) copy-start(bf16[128,1664]{1,0:T(8,128)(2,1)S(1)} %collective-permute-done.1.refs_2_.g2) | copy-start | bytes 1277956
  26.9 0.8 copy-start.5
  32.6 6.3 %copy-start.7 = (bf16[128,4096]{1,0:T(8,128)(2,1)}, bf16[128,4096]{1,0:T(8,128)(2,1)S(1)}, u32[]{:S(2)}) copy-start(bf16[128,4096]{1,0:T(8,128)(2,1)S(1)} %collective-permute-done.6.g_ref) | copy-start | bytes 3145732
  38.9 7.9 %copy-start.6 = (bf16[1,128,4096]{2,1,0:T(8,128)(2,1)S(1)}, bf16[1,128,4096]{2,1,0:T(8,128)(2,1)}, u32[]{:S(2)}) copy-start(bf16[1,128,4096]{2,1,0:T(8,128)(2,1)} %param.6) | copy-start | bytes 3145732
  38.9 60.1 %all-to-all-start.2 = ((bf16[32,40,1536]{2,1,0:T(8,128)(2,1)}), bf16[32,40,1536]{2,1,0:T(8,128)(2,1)}, u32[]{:S(2)}, u32[]{:S(2)}) async-start(bf16[32,40,1536]{2,1,0:T(8,128)(2,1)} %bitcast.42), calls=%async_computation.2 | async-start | bytes 7864320 | tf_op jit(solution)/shard_map/all_to_all | solution.py:324
  46.9 31.7 %copy-start.2 = (bf16[128,2560]{1,0:T(8,128)(2,1)}, bf16[128,2560]{1,0:T(8,128)(2,1)S(1)}, u32[]{:S(2)}) copy-start(bf16[128,2560]{1,0:T(8,128)(2,1)S(1)} %slice.21.g0.refs_4_) | copy-start | bytes 1966084
  46.9 17.4 %collective-permute-start.3 = (bf16[128,2560]{1,0:T(8,128)(2,1)S(1)}, bf16[128,2560]{1,0:T(8,128)(2,1)S(1)}, u32[]{:S(2)}, u32[]{:S(2)}) collective-permute-start(bf16[128,2560]{1,0:T(8,128)(2,1)S(1)} %slice.21.g0.refs_4_), channel_id=1, source_target_pairs={{0,1},{1,2},{2,3},{3,0},{4,5},{5,6},{6,7},{7,4},{8,9},{9,10},{10,1... | collective-permute-start | bytes 1966088 | tf_op jit(solution)/shard_map/ppermute | solution.py:283
  47.8 16.5 %collective-permute-start.4 = (bf16[128,2560]{1,0:T(8,128)(2,1)S(1)}, bf16[128,2560]{1,0:T(8,128)(2,1)S(1)}, u32[]{:S(2)}, u32[]{:S(2)}) collective-permute-start(bf16[128,2560]{1,0:T(8,128)(2,1)S(1)} %slice.21.g0.refs_4_), channel_id=1, source_target_pairs={{0,3},{1,0},{2,1},{3,2},{4,7},{5,4},{6,5},{7,6},{8,11},{9,8},{10,9... | collective-permute-start | bytes 1966088 | tf_op jit(solution)/shard_map/ppermute | solution.py:283
  49.6 28.9 %collective-permute-start.5 = (bf16[128,2560]{1,0:T(8,128)(2,1)S(1)}, bf16[128,2560]{1,0:T(8,128)(2,1)S(1)}, u32[]{:S(2)}, u32[]{:S(2)}) collective-permute-start(bf16[128,2560]{1,0:T(8,128)(2,1)S(1)} %slice.21.g0.refs_4_), channel_id=1, source_target_pairs={{0,2},{1,3},{2,0},{3,1},{4,6},{5,7},{6,4},{7,5},{8,10},{9,11},{10,... | collective-permute-start | bytes 1966088 | tf_op jit(solution)/shard_map/ppermute | solution.py:283
  64.3 14.2 %copy-start.9 = (bf16[128,2560]{1,0:T(8,128)(2,1)}, bf16[128,2560]{1,0:T(8,128)(2,1)S(1)}, u32[]{:S(2)}) copy-start(bf16[128,2560]{1,0:T(8,128)(2,1)S(1)} %collective-permute-done.3.g1.refs_5_) | copy-start | bytes 1966084
  64.3 14.2 %copy-start.10 = (bf16[128,2560]{1,0:T(8,128)(2,1)}, bf16[128,2560]{1,0:T(8,128)(2,1)S(1)}, u32[]{:S(2)}) copy-start(bf16[128,2560]{1,0:T(8,128)(2,1)S(1)} %collective-permute-done.4.g2.refs_6_) | copy-start | bytes 1966084
  78.5 0.9 copy-start.11
  99.0 4.9 %copy-start = (bf16[1,1280,768]{2,1,0:T(8,128)(2,1)S(1)}, bf16[1,1280,768]{2,1,0:T(8,128)(2,1)}, u32[]{:S(2)}) copy-start(bf16[1,1280,768]{2,1,0:T(8,128)(2,1)} %param.11) | copy-start | bytes 5898244
  99.0 93.3 %all-to-all-start = ((bf16[32,40,2560]{2,1,0:T(8,128)(2,1)}), bf16[32,40,2560]{2,1,0:T(8,128)(2,1)}, u32[]{:S(2)}, u32[]{:S(2)}) async-start(bf16[32,40,2560]{2,1,0:T(8,128)(2,1)} %bitcast.41), calls=%async_computation | async-start | bytes 13107200 | tf_op jit(solution)/shard_map/all_to_all | solution.py:324
  106.2 41.3 %collective-permute-start.12 = (bf16[512,1024]{1,0:T(8,128)(2,1)}, bf16[512,1024]{1,0:T(8,128)(2,1)S(1)}, u32[]{:S(2)}, u32[]{:S(2)}) collective-permute-start(bf16[512,1024]{1,0:T(8,128)(2,1)} %refs_4_), channel_id=1, source_target_pairs={{0,1},{1,2},{2,3},{3,0},{4,5},{5,6},{6,7},{7,4},{8,9},{9,10},{10,1... | collective-permute-start | bytes 3145736 | tf_op jit(solution)/shard_map/ppermute | solution.py:283
  107.1 41.4 %collective-permute-start.13 = (bf16[512,1024]{1,0:T(8,128)(2,1)}, bf16[512,1024]{1,0:T(8,128)(2,1)}, u32[]{:S(2)}, u32[]{:S(2)}) collective-permute-start(bf16[512,1024]{1,0:T(8,128)(2,1)} %refs_4_), channel_id=1, source_target_pairs={{0,3},{1,0},{2,1},{3,2},{4,7},{5,4},{6,5},{7,6},{8,11},{9,8},{10,9... | collective-permute-start | bytes 3145736 | tf_op jit(solution)/shard_map/ppermute | solution.py:283
  111.4 26.6 %collective-permute-start.7 = (bf16[128,1024]{1,0:T(8,128)(2,1)}, bf16[128,1024]{1,0:T(8,128)(2,1)S(1)}, u32[]{:S(2)}, u32[]{:S(2)}) collective-permute-start(bf16[128,1024]{1,0:T(8,128)(2,1)} %get-tuple-element.33), channel_id=1, source_target_pairs={{0,1},{1,2},{2,3},{3,0},{4,5},{5,6},{6,7},{7,4},{8,9},{9,10},{10,1... | collective-permute-start | bytes 786440 | tf_op jit(solution)/shard_map/ppermute | solution.py:283
  111.4 27.8 %collective-permute-start.8 = (bf16[128,1024]{1,0:T(8,128)(2,1)}, bf16[128,1024]{1,0:T(8,128)(2,1)S(1)}, u32[]{:S(2)}, u32[]{:S(2)}) collective-permute-start(bf16[128,1024]{1,0:T(8,128)(2,1)} %get-tuple-element.34), channel_id=1, source_target_pairs={{0,3},{1,0},{2,1},{3,2},{4,7},{5,4},{6,5},{7,6},{8,11},{9,8},{10,9... | collective-permute-start | bytes 786440 | tf_op jit(solution)/shard_map/ppermute | solution.py:283
  114.0 29.7 %collective-permute-start.9 = (bf16[128,1024]{1,0:T(8,128)(2,1)}, bf16[128,1024]{1,0:T(8,128)(2,1)S(1)}, u32[]{:S(2)}, u32[]{:S(2)}) collective-permute-start(bf16[128,1024]{1,0:T(8,128)(2,1)} %get-tuple-element.35), channel_id=1, source_target_pairs={{0,2},{1,3},{2,0},{3,1},{4,6},{5,7},{6,4},{7,5},{8,10},{9,11},{10,... | collective-permute-start | bytes 786440 | tf_op jit(solution)/shard_map/ppermute | solution.py:283
  127.3 10.6 %copy-start.8 = (bf16[512,1024]{1,0:T(8,128)(2,1)S(1)}, bf16[512,1024]{1,0:T(8,128)(2,1)}, u32[]{:S(2)}) copy-start(bf16[512,1024]{1,0:T(8,128)(2,1)} %shard_map.101.refs_0_) | copy-start | bytes 3145732
  127.3 16.4 %copy-start.13 = (bf16[128,1024]{1,0:T(8,128)(2,1)S(1)}, bf16[128,1024]{1,0:T(8,128)(2,1)}, u32[]{:S(2)}) copy-start(bf16[128,1024]{1,0:T(8,128)(2,1)} %get-tuple-element.45) | copy-start | bytes 786436
  138.0 13.6 %collective-permute-start.10 = (bf16[512,1024]{1,0:T(8,128)(2,1)S(1)}, bf16[512,1024]{1,0:T(8,128)(2,1)}, u32[]{:S(2)}, u32[]{:S(2)}) collective-permute-start(bf16[512,1024]{1,0:T(8,128)(2,1)S(1)} %copy-done.8), channel_id=1, source_target_pairs={{0,32},{32,0},{1,33},{33,1},{2,34},{34,2},{3,35},{35,3},{4,36},{36... | collective-permute-start | bytes 3145736 | tf_op jit(solution)/shard_map/ppermute | solution.py:283
  146.7 16.3 %collective-permute-start.11 = (bf16[512,1024]{1,0:T(8,128)(2,1)}, bf16[512,1024]{1,0:T(8,128)(2,1)}, u32[]{:S(2)}, u32[]{:S(2)}) collective-permute-start(bf16[512,1024]{1,0:T(8,128)(2,1)} %constant_dynamic-update-slice_fusion.refs_2_), channel_id=1, source_target_pairs={{0,32},{32,0},{1,33},{33,1},{2,34},{34,2},{3,35},{35,3},{4,36},{36... | collective-permute-start | bytes 3145736 | tf_op jit(solution)/shard_map/ppermute | solution.py:283
  147.5 15.5 %copy-start.12 = (bf16[512,1024]{1,0:T(8,128)(2,1)}, bf16[512,1024]{1,0:T(8,128)(2,1)S(1)}, u32[]{:S(2)}) copy-start(bf16[512,1024]{1,0:T(8,128)(2,1)S(1)} %collective-permute-done.12.refs_5_) | copy-start | bytes 3145732
  147.6 14.9 %collective-permute-start.14 = (bf16[256,1024]{1,0:T(8,128)(2,1)S(1)}, bf16[256,1024]{1,0:T(8,128)(2,1)}, u32[]{:S(2)}, u32[]{:S(2)}) collective-permute-start(bf16[256,1024]{1,0:T(8,128)(2,1)S(1)} %slice.23), channel_id=1, source_target_pairs={{0,1},{1,2},{2,3},{3,0},{4,5},{5,6},{6,7},{7,4},{8,9},{9,10},{10,1... | collective-permute-start | bytes 1572872 | tf_op jit(solution)/shard_map/ppermute | solution.py:283
  149.6 13.4 %collective-permute-start.15 = (bf16[256,1024]{1,0:T(8,128)(2,1)S(1)}, bf16[256,1024]{1,0:T(8,128)(2,1)}, u32[]{:S(2)}, u32[]{:S(2)}) collective-permute-start(bf16[256,1024]{1,0:T(8,128)(2,1)S(1)} %slice.24), channel_id=1, source_target_pairs={{0,3},{1,0},{2,1},{3,2},{4,7},{5,4},{6,5},{7,6},{8,11},{9,8},{10,9... | collective-permute-start | bytes 1572872 | tf_op jit(solution)/shard_map/ppermute | solution.py:283
  174.3 36.9 %collective-permute-start.16 = (bf16[512,1024]{1,0:T(8,128)(2,1)S(1)}, bf16[512,1024]{1,0:T(8,128)(2,1)S(1)}, u32[]{:S(2)}, u32[]{:S(2)}) collective-permute-start(bf16[512,1024]{1,0:T(8,128)(2,1)S(1)} %constant_dynamic-slice_fusion), channel_id=1, source_target_pairs={{0,4},{4,0},{1,5},{5,1},{2,6},{6,2},{3,7},{7,3},{8,12},{12,8},{9,1... | collective-permute-start | bytes 3145736 | tf_op jit(solution)/shard_map/ppermute | solution.py:283
  204.0 23.6 %all-to-all-start.3 = ((f32[128,1,128]{2,1,0:T(1,128)}), f32[128,1,128]{2,1,0:T(1,128)S(1)}, u32[]{:S(2)}, u32[]{:S(2)}) async-start(f32[128,1,128]{2,1,0:T(1,128)} %bitcast.50), calls=%async_computation.3 | async-start | bytes 131072 | tf_op jit(solution)/shard_map/all_to_all | solution.py:369
  213.0 15.6 %collective-permute-start.17 = (bf16[128,1024]{1,0:T(8,128)(2,1)S(1)}, bf16[128,1024]{1,0:T(8,128)(2,1)}, u32[]{:S(2)}, u32[]{:S(2)}) collective-permute-start(bf16[128,1024]{1,0:T(8,128)(2,1)S(1)} %get-tuple-element.56), channel_id=1, source_target_pairs={{0,8},{8,16},{16,24},{24,0},{1,9},{9,17},{17,25},{25,1},{2,10},{10... | collective-permute-start | bytes 786440 | tf_op jit(solution)/shard_map/ppermute | solution.py:283
  214.5 14.1 %collective-permute-start.18 = (bf16[128,1024]{1,0:T(8,128)(2,1)S(1)}, bf16[128,1024]{1,0:T(8,128)(2,1)}, u32[]{:S(2)}, u32[]{:S(2)}) collective-permute-start(bf16[128,1024]{1,0:T(8,128)(2,1)S(1)} %get-tuple-element.55), channel_id=1, source_target_pairs={{0,24},{8,0},{16,8},{24,16},{1,25},{9,1},{17,9},{25,17},{2,26},{10... | collective-permute-start | bytes 786440 | tf_op jit(solution)/shard_map/ppermute | solution.py:283
  215.7 12.2 %copy-start.14 = (s32[1,128,8]{1,2,0:T(8,128)S(1)}, s32[1,128,8]{1,2,0:T(8,128)}, u32[]{:S(2)}) copy-start(s32[1,128,8]{1,2,0:T(8,128)} %param.7) | copy-start | bytes 12292
  215.8 12.9 %collective-permute-start.19 = (bf16[128,1024]{1,0:T(8,128)(2,1)S(1)}, bf16[128,1024]{1,0:T(8,128)(2,1)}, u32[]{:S(2)}, u32[]{:S(2)}) collective-permute-start(bf16[128,1024]{1,0:T(8,128)(2,1)S(1)} %get-tuple-element.54), channel_id=1, source_target_pairs={{0,16},{8,24},{16,0},{24,8},{1,17},{9,25},{17,1},{25,9},{2,18},{10... | collective-permute-start | bytes 786440 | tf_op jit(solution)/shard_map/ppermute | solution.py:283

commit v4 on v3

--- a/solution.py
+++ b/solution.py
@@ -215,7 +215,7 @@
     rows, width = routed.shape
     hid = w.shape[0]
     first, last = chunk == 0, chunk == len(CHUNKS) - 1
-    tile = 320
+    tile = 640
     across = pl.BlockSpec((tile, hid), lambda i: (i, 0))
     narrow = pl.BlockSpec((tile, 1), lambda i: (i, 0))
     deep = WIDE if CHUNKS[chunk][0] else width
@@ -256,10 +256,11 @@
 def weigh(chunk, routed, hidden_t, weight, full, before):
     rows, width = routed.shape
     hid = hidden_t.shape[0]
-    steps = width // WIDE
-    base = CHUNKS[chunk][0] // WIDE
+    tile = width // 2 if width % 256 == 0 and CHUNKS[chunk][0] == 0 else WIDE
+    steps = width // tile
+    base = CHUNKS[chunk][0] // tile
     in_specs = [
-        pl.BlockSpec((rows, WIDE), lambda i: (0, i)),
+        pl.BlockSpec((rows, tile), lambda i: (0, i)),
         pl.BlockSpec((hid, rows), lambda i: (0, 0)),
         pl.BlockSpec((rows, 1), lambda i: (0, 0)),
     ]
@@ -272,7 +273,7 @@
         out_shape=jax.ShapeDtypeStruct((hid, full), BF),
         grid=(steps,),
         in_specs=in_specs,
-        out_specs=pl.BlockSpec((hid, WIDE), lambda i: (0, base + i)),
+        out_specs=pl.BlockSpec((hid, tile), lambda i: (0, base + i)),
         input_output_aliases={} if before is None else {3: 0},
         compiler_params=params(),
         cost_estimate=cost(2 * rows * hid * width, 2 * (rows + hid) * width),

time: 232 us -> 232 us (level)
  transfers between devices with their start and end apart: 24 -> 24, of which waited for: 10 -> 11; matrix products, arithmetic and copies ran while one was open for 7% -> 7% of each run, Pallas kernels for 28% -> 27%
where the time goes in v4:
time: 232 us; the launch traced here: 231 us
  waiting for transfers between devices  82 us (35%)
  Pallas kernels  69.5 us (30%)
  starting transfers between devices  57.1 us (25%)
  local copies, waits for them, and re-layouts  12.9 us (6%)
  other arithmetic  8.53 us (4%)
    ppermute x20, waiting for transfers between devices, ring(): return lax.ppermute(x, axis, [(i, (i + shift) % n) for i in range(n)])  53.5 us
    ppermute x20, starting transfers between devices, ring(): return lax.ppermute(x, axis, [(i, (i + shift) % n) for i in range(n)])  27.4 us
    all_to_all x2, waiting for transfers between devices, send(): lax.all_to_all(rows.reshape(n_experts // 4, 4 * cap, -1), PEERS, split_ax...  26.4 us
    pallas_call x2, Pallas kernels, project(): pl.pallas_call(kernel, out_shape=out_shape, grid=(rows // tile,), in_spec...  19.2 us
    pallas_call x2, Pallas kernels, weigh(): pl.pallas_call(down_kernel, out_shape=jax.ShapeDtypeStruct((hid, full), B...  17 us
    pallas_call x2, Pallas kernels, dispatch(): pl.pallas_call(dispatch_kernel, out_shape=jax.ShapeDtypeStruct((rows, wid...  14.8 us
    all_to_all x2, starting transfers between devices, send(): lax.all_to_all(rows.reshape(n_experts // 4, 4 * cap, -1), PEERS, split_ax...  12.8 us
    pallas_call x1, Pallas kernels, outer(): pl.pallas_call(outer_kernel, out_shape=jax.ShapeDtypeStruct((n, wide), BF...  10 us
  transfers between devices with their start and end apart: 24, of which 11 were waited for; matrix products, arithmetic and copies ran while one was open for 7% of the time, Pallas kernels for 27%

profile of v4, /device:TPU:1, one launch (start us, length us, event | category | flops | bytes accessed | tf_op | source)
XLA Modules:
  0.0 231.1 jit_solution(18419717853656476732)
XLA Ops:
  1.3 1.0 slice.20
  2.4 2.5 %collective-permute-start.6 = (bf16[128,4096]{1,0:T(8,128)(2,1)}, bf16[128,4096]{1,0:T(8,128)(2,1)S(1)}, u32[]{:S(2)}, u32[]{:S(2)}) collective-permute-start(bf16[128,4096]{1,0:T(8,128)(2,1)} %bitcast.44), channel_id=1, source_target_pairs={{0,64},{64,0},{1,65},{65,1},{2,66},{66,2},{3,67},{67,3},{4,68},{68... | collective-permute-start | bytes 3145736 | tf_op jit(solution)/shard_map/ppermute | solution.py:284
  4.9 1.3 collective-permute-start
  6.2 1.4 collective-permute-start.1
  7.7 1.6 collective-permute-start.2
  12.7 9.7 %all-to-all-start.1 = ((f32[128,1,10]{2,1,0:T(1,128)}), f32[128,1,10]{2,1,0:T(1,128)S(1)}, u32[]{:S(2)}, u32[]{:S(2)}) async-start(f32[128,1,10]{2,1,0:T(1,128)} %copy.24), calls=%async_computation.1 | async-start | bytes 131072 | tf_op jit(solution)/shard_map/all_to_all | solution.py:318
  22.5 4.4 %collective-permute-done.2.refs_3_.g3 = bf16[128,1664]{1,0:T(8,128)(2,1)S(1)} collective-permute-done((bf16[128,1664]{1,0:T(8,128)(2,1)S(1)}, bf16[128,1664]{1,0:T(8,128)(2,1)S(1)}, u32[]{:S(2)}, u32[]{:S(2)}) %collective-permute-start.2) | collective-permute-done | bytes 426016 | tf_op jit(solution)/shard_map/ppermute | solution.py:284
  27.7 2.6 %shard_map.93.s_ref = bf16[1280,512]{1,0:T(8,128)(2,1)} custom-call(s32[1]{0:T(128)} %bitcast.2.y_ref, bf16[128,1664]{1,0:T(8,128)(2,1)} %copy-done.1, bf16[128,1664]{1,0:T(8,128)(2,1)} %copy-done.3, bf16[128,1664]{1,0:T(8,128)(2,1)} %copy-done.4, bf16[128,1664]{1,0:T(8,128)(2,1)} %copy-done.5), custom_call_target="tpu_custom_call" | custom-call | flops 100000000 | bytes 2000000 | tf_op jit(solution)/shard_map/pallas_call | solution.py:69
  30.3 2.2 all-to-all-done.1
  32.6 6.3 %shard_map.96 = bf16[1280,1536]{1,0:T(8,128)(2,1)} custom-call(bf16[1280,512]{1,0:T(8,128)(2,1)} %shard_map.93.s_ref, bf16[128,1664]{1,0:T(8,128)(2,1)} %copy-done.1, bf16[128,1664]{1,0:T(8,128)(2,1)} %copy-done.3, bf16[128,1664]{1,0:T(8,128)(2,1)} %copy-done.4, bf16[128,1664]{1,0:T(8,128)(2,1)} %copy-done.5), custom_call_target="tpu_custom_call" | custom-call | flops 2013265920 | bytes 3932160 | tf_op jit(solution)/shard_map/pallas_call | solution.py:88
  38.9 7.9 %all-to-all-start.2 = ((bf16[32,40,1536]{2,1,0:T(8,128)(2,1)}), bf16[32,40,1536]{2,1,0:T(8,128)(2,1)}, u32[]{:S(2)}, u32[]{:S(2)}) async-start(bf16[32,40,1536]{2,1,0:T(8,128)(2,1)} %bitcast.42), calls=%async_computation.2 | async-start | bytes 7864320 | tf_op jit(solution)/shard_map/all_to_all | solution.py:325
  46.9 0.9 collective-permute-start.3
  47.8 1.8 collective-permute-start.4
  49.8 14.5 %collective-permute-done.3.g1.refs_5_ = bf16[128,2560]{1,0:T(8,128)(2,1)S(1)} collective-permute-done((bf16[128,2560]{1,0:T(8,128)(2,1)S(1)}, bf16[128,2560]{1,0:T(8,128)(2,1)S(1)}, u32[]{:S(2)}, u32[]{:S(2)}) %collective-permute-start.3) | collective-permute-done | bytes 655392 | tf_op jit(solution)/shard_map/ppermute | solution.py:284
  64.3 14.2 %collective-permute-done.5.g3.refs_7_ = bf16[128,2560]{1,0:T(8,128)(2,1)S(1)} collective-permute-done((bf16[128,2560]{1,0:T(8,128)(2,1)S(1)}, bf16[128,2560]{1,0:T(8,128)(2,1)S(1)}, u32[]{:S(2)}, u32[]{:S(2)}) %collective-permute-start.5) | collective-permute-done | bytes 655392 | tf_op jit(solution)/shard_map/ppermute | solution.py:284
  78.5 0.9 copy-done.11
  79.4 8.5 %shard_map.94 = bf16[1280,2560]{1,0:T(8,128)(2,1)} custom-call(bf16[1280,512]{1,0:T(8,128)(2,1)} %shard_map.93.s_ref, bf16[128,2560]{1,0:T(8,128)(2,1)} %copy-done.2, bf16[128,2560]{1,0:T(8,128)(2,1)} %copy-done.9, bf16[128,2560]{1,0:T(8,128)(2,1)} %copy-done.10, bf16[128,2560]{1,0:T(8,128)(2,1)} %copy-done.11), custom_call_target="tpu_custom_call" | custom-call | flops 3355443200 | bytes 6553600 | tf_op jit(solution)/shard_map/pallas_call | solution.py:88
  87.9 11.1 %all-to-all-done.2 = bf16[32,40,1536]{2,1,0:T(8,128)(2,1)} async-done(((bf16[32,40,1536]{2,1,0:T(8,128)(2,1)}), bf16[32,40,1536]{2,1,0:T(8,128)(2,1)}, u32[]{:S(2)}, u32[]{:S(2)}) %all-to-all-start.2) | async-done | bytes 3932192 | tf_op jit(solution)/shard_map/all_to_all | solution.py:325
  99.0 4.8 %all-to-all-start = ((bf16[32,40,2560]{2,1,0:T(8,128)(2,1)}), bf16[32,40,2560]{2,1,0:T(8,128)(2,1)}, u32[]{:S(2)}, u32[]{:S(2)}) async-start(bf16[32,40,2560]{2,1,0:T(8,128)(2,1)} %bitcast.41), calls=%async_computation | async-start | bytes 13107200 | tf_op jit(solution)/shard_map/all_to_all | solution.py:325
  103.9 2.3 %copy.25 = bf16[1,1280,768]{1,2,0:T(8,128)(2,1)} copy(bf16[1,1280,768]{2,1,0:T(8,128)(2,1)S(1)} %copy-done) | data formatting | bytes 3932160 | tf_op args[5]
  106.2 0.9 collective-permute-start.12
  107.1 1.8 collective-permute-start.13
  108.9 2.5 %shard_map.95 = (bf16[128,1024]{1,0:T(8,128)(2,1)}, bf16[128,1024]{1,0:T(8,128)(2,1)}, bf16[128,1024]{1,0:T(8,128)(2,1)}, bf16[128,1024]{1,0:T(8,128)(2,1)}) custom-call(s32[1]{0:T(128)} %bitcast.2.y_ref, bf16[128,4096]{1,0:T(8,128)(2,1)} %copy-done.7), custom_call_target="tpu_custom_call" | custom-call | bytes 2097152 | tf_op jit(solution)/shard_map/pallas_call | solution.py:133
  111.4 2.7 %collective-permute-start.8 = (bf16[128,1024]{1,0:T(8,128)(2,1)}, bf16[128,1024]{1,0:T(8,128)(2,1)S(1)}, u32[]{:S(2)}, u32[]{:S(2)}) collective-permute-start(bf16[128,1024]{1,0:T(8,128)(2,1)} %get-tuple-element.34), channel_id=1, source_target_pairs={{0,3},{1,0},{2,1},{3,2},{4,7},{5,4},{6,5},{7,6},{8,11},{9,8},{10,9... | collective-permute-start | bytes 786440 | tf_op jit(solution)/shard_map/ppermute | solution.py:284
  115.4 1.1 reshape.54.wt_ref.refs_4_
  116.4 3.5 %shard_map.101.refs_0_ = bf16[512,1024]{1,0:T(8,128)(2,1)} custom-call(s32[1]{0:T(128)} %bitcast.2.y_ref, bf16[128,1664]{1,0:T(8,128)(2,1)} %copy-done.1, bf16[128,1664]{1,0:T(8,128)(2,1)} %copy-done.3, bf16[128,1664]{1,0:T(8,128)(2,1)} %copy-done.4, bf16[128,1664]{1,0:T(8,128)(2,1)} %copy-done.5, bf16[128,2560]{1,0:T(8,128)(2,1)} %copy-done.2, ...), custom_call_target="tpu_custom_call" | custom-call | bytes 4194304 | tf_op jit(solution)/shard_map/pallas_call | solution.py:113
  119.9 7.0 %shard_map.97.refs_2_ = f32[1280,768]{1,0:T(8,128)} custom-call(bf16[1280,1536]{1,0:T(8,128)(2,1)} %bitcast.12.refs_0_.routed_ref, bf16[768,4096]{1,0:T(8,128)(2,1)} %bitcast.33, bf16[768,4096]{1,0:T(8,128)(2,1)} %bitcast.34, bf16[768,4096]{1,0:T(8,128)(2,1)} %bitcast.35), custom_call_target="tpu_custom_call" | custom-call | flops 3019898880 | bytes 6291456 | tf_op jit(solution)/shard_map/pallas_call | solution.py:240
  126.9 7.3 %shard_map.98.refs_0_ = bf16[768,4096]{1,0:T(8,128)(2,1)} custom-call(bf16[1280,1536]{1,0:T(8,128)(2,1)} %bitcast.12.refs_0_.routed_ref, bf16[768,1280]{1,0:T(8,128)(2,1)} %bitcast.38, f32[1280,1]{1,0:T(8,128)} %reshape.54.wt_ref.refs_4_), custom_call_target="tpu_custom_call" | custom-call | flops 3019898880 | bytes 6291456 | tf_op jit(solution)/shard_map/pallas_call | solution.py:271
  134.2 3.8 %collective-permute-done.7 = bf16[128,1024]{1,0:T(8,128)(2,1)S(1)} collective-permute-done((bf16[128,1024]{1,0:T(8,128)(2,1)}, bf16[128,1024]{1,0:T(8,128)(2,1)S(1)}, u32[]{:S(2)}, u32[]{:S(2)}) %collective-permute-start.7) | collective-permute-done | bytes 262176 | tf_op jit(solution)/shard_map/ppermute | solution.py:284
  138.0 1.2 collective-permute-start.10
  139.2 4.6 %collective-permute-done.9 = bf16[128,1024]{1,0:T(8,128)(2,1)S(1)} collective-permute-done((bf16[128,1024]{1,0:T(8,128)(2,1)}, bf16[128,1024]{1,0:T(8,128)(2,1)S(1)}, u32[]{:S(2)}, u32[]{:S(2)}) %collective-permute-start.9) | collective-permute-done | bytes 262176 | tf_op jit(solution)/shard_map/ppermute | solution.py:284
  146.7 0.9 collective-permute-start.11
  147.6 0.9 collective-permute-start.14
  148.5 1.1 slice.24
  149.6 2.0 collective-permute-start.15
  151.6 11.0 %collective-permute-done.14.refs_7_ = bf16[256,1024]{1,0:T(8,128)(2,1)} collective-permute-done((bf16[256,1024]{1,0:T(8,128)(2,1)S(1)}, bf16[256,1024]{1,0:T(8,128)(2,1)}, u32[]{:S(2)}, u32[]{:S(2)}) %collective-permute-start.14) | collective-permute-done | bytes 524320 | tf_op jit(solution)/shard_map/ppermute | solution.py:284
  163.0 10.0 %shard_map.102 = bf16[1024,1024]{1,0:T(8,128)(2,1)} custom-call(s32[1]{0:T(128)} %bitcast.24.t_ref, bf16[512,1024]{1,0:T(8,128)(2,1)} %shard_map.101.refs_0_, bf16[512,1024]{1,0:T(8,128)(2,1)} %collective-permute-done.10.refs_1_, bf16[512,1024]{1,0:T(8,128)(2,1)} %constant_dynamic-update-slice_fusion.refs_2_, ...), custom_call_target="tpu_custom_call" | custom-call | flops 4294967296 | bytes 10485760 | tf_op jit(solution)/shard_map/pallas_call | solution.py:168
  173.0 1.3 constant_dynamic-slice_fusion
  174.3 2.7 %collective-permute-start.16 = (bf16[512,1024]{1,0:T(8,128)(2,1)S(1)}, bf16[512,1024]{1,0:T(8,128)(2,1)S(1)}, u32[]{:S(2)}, u32[]{:S(2)}) collective-permute-start(bf16[512,1024]{1,0:T(8,128)(2,1)S(1)} %constant_dynamic-slice_fusion), channel_id=1, source_target_pairs={{0,4},{4,0},{1,5},{5,1},{2,6},{6,2},{3,7},{7,3},{8,12},{12,8},{9,1... | collective-permute-start | bytes 3145736 | tf_op jit(solution)/shard_map/ppermute | solution.py:284
  177.1 15.2 %all-to-all-done = bf16[32,40,2560]{2,1,0:T(8,128)(2,1)} async-done(((bf16[32,40,2560]{2,1,0:T(8,128)(2,1)}), bf16[32,40,2560]{2,1,0:T(8,128)(2,1)}, u32[]{:S(2)}, u32[]{:S(2)}) %all-to-all-start) | async-done | bytes 6553632 | tf_op jit(solution)/shard_map/all_to_all | solution.py:325
  192.3 12.2 %shard_map.99 = (bf16[1280,768]{1,0:T(8,128)(2,1)}, f32[128,128]{1,0:T(8,128)}) custom-call(bf16[1280,2560]{1,0:T(8,128)(2,1)} %bitcast.8.refs_0_.routed_ref, bf16[768,4096]{1,0:T(8,128)(2,1)} %bitcast.36, f32[1280,768]{1,0:T(8,128)} %shard_map.97.refs_2_, bf16[1280,768]{1,0:T(8,128)(2,1)} %bitcast.40, f32[1280,1]{1,0:T(8,128)} %reshape.54.wt_ref.refs_4_), custom_call_target="tpu_custom_call" | custom-call | flops 5033164800 | bytes 10485760 | tf_op jit(solution)/shard_map/pallas_call | solution.py:240
  204.5 7.2 %all-to-all-start.3 = ((f32[128,1,128]{2,1,0:T(1,128)}), f32[128,1,128]{2,1,0:T(1,128)S(1)}, u32[]{:S(2)}, u32[]{:S(2)}) async-start(f32[128,1,128]{2,1,0:T(1,128)} %bitcast.50), calls=%async_computation.3 | async-start | bytes 131072 | tf_op jit(solution)/shard_map/all_to_all | solution.py:370
  211.7 1.6 convert_add_fusion
  213.5 1.5 collective-permute-start.17
  214.9 1.3 collective-permute-start.18
  216.2 1.7 collective-permute-start.19
  217.9 9.7 %shard_map.100 = bf16[768,4096]{1,0:T(8,128)(2,1)} custom-call(bf16[1280,2560]{1,0:T(8,128)(2,1)} %bitcast.8.refs_0_.routed_ref, bf16[768,1280]{1,0:T(8,128)(2,1)} %bitcast.39, f32[1280,1]{1,0:T(8,128)} %reshape.54.wt_ref.refs_4_, bf16[768,4096]{1,0:T(8,128)(2,1)} %shard_map.98.refs_0_), custom_call_target="tpu_custom_call", output_to_operand_aliasing={{}: (3, {})} | custom-call | flops 5033164800 | bytes 10485760 | tf_op jit(solution)/shard_map/pallas_call | solution.py:271
  229.1 2.0 add_convert_fusion
  (68 shorter events, 11.6 us)
Async XLA Ops:
  2.4 24.5 %copy-start.1 = (bf16[128,1664]{1,0:T(8,128)(2,1)}, bf16[128,1664]{1,0:T(8,128)(2,1)S(1)}, u32[]{:S(2)}) copy-start(bf16[128,1664]{1,0:T(8,128)(2,1)S(1)} %fusion.4.refs_0_.g0) | copy-start | bytes 1277956
  2.4 30.2 %collective-permute-start.6 = (bf16[128,4096]{1,0:T(8,128)(2,1)}, bf16[128,4096]{1,0:T(8,128)(2,1)S(1)}, u32[]{:S(2)}, u32[]{:S(2)}) collective-permute-start(bf16[128,4096]{1,0:T(8,128)(2,1)} %bitcast.44), channel_id=1, source_target_pairs={{0,64},{64,0},{1,65},{65,1},{2,66},{66,2},{3,67},{67,3},{4,68},{68... | collective-permute-start | bytes 3145736 | tf_op jit(solution)/shard_map/ppermute | solution.py:284
  4.9 17.5 %collective-permute-start = (bf16[128,1664]{1,0:T(8,128)(2,1)S(1)}, bf16[128,1664]{1,0:T(8,128)(2,1)S(1)}, u32[]{:S(2)}, u32[]{:S(2)}) collective-permute-start(bf16[128,1664]{1,0:T(8,128)(2,1)S(1)} %fusion.4.refs_0_.g0), channel_id=1, source_target_pairs={{0,1},{1,2},{2,3},{3,0},{4,5},{5,6},{6,7},{7,4},{8,9},{9,10},{10,1... | collective-permute-start | bytes 1277960 | tf_op jit(solution)/shard_map/ppermute | solution.py:284
  6.2 16.2 %collective-permute-start.1 = (bf16[128,1664]{1,0:T(8,128)(2,1)S(1)}, bf16[128,1664]{1,0:T(8,128)(2,1)S(1)}, u32[]{:S(2)}, u32[]{:S(2)}) collective-permute-start(bf16[128,1664]{1,0:T(8,128)(2,1)S(1)} %fusion.4.refs_0_.g0), channel_id=1, source_target_pairs={{0,3},{1,0},{2,1},{3,2},{4,7},{5,4},{6,5},{7,6},{8,11},{9,8},{10,9... | collective-permute-start | bytes 1277960 | tf_op jit(solution)/shard_map/ppermute | solution.py:284
  7.7 19.2 %collective-permute-start.2 = (bf16[128,1664]{1,0:T(8,128)(2,1)S(1)}, bf16[128,1664]{1,0:T(8,128)(2,1)S(1)}, u32[]{:S(2)}, u32[]{:S(2)}) collective-permute-start(bf16[128,1664]{1,0:T(8,128)(2,1)S(1)} %fusion.4.refs_0_.g0), channel_id=1, source_target_pairs={{0,2},{1,3},{2,0},{3,1},{4,6},{5,7},{6,4},{7,5},{8,10},{9,11},{10,... | collective-permute-start | bytes 1277960 | tf_op jit(solution)/shard_map/ppermute | solution.py:284
  12.7 19.8 %all-to-all-start.1 = ((f32[128,1,10]{2,1,0:T(1,128)}), f32[128,1,10]{2,1,0:T(1,128)S(1)}, u32[]{:S(2)}, u32[]{:S(2)}) async-start(f32[128,1,10]{2,1,0:T(1,128)} %copy.24), calls=%async_computation.1 | async-start | bytes 131072 | tf_op jit(solution)/shard_map/all_to_all | solution.py:318
  22.4 4.5 %copy-start.3 = (bf16[128,1664]{1,0:T(8,128)(2,1)}, bf16[128,1664]{1,0:T(8,128)(2,1)S(1)}, u32[]{:S(2)}) copy-start(bf16[128,1664]{1,0:T(8,128)(2,1)S(1)} %collective-permute-done.refs_1_.g1) | copy-start | bytes 1277956
  22.5 4.5 %copy-start.4 = (bf16[128,1664]{1,0:T(8,128)(2,1)}, bf16[128,1664]{1,0:T(8,128)(2,1)S(1)}, u32[]{:S(2)}) copy-start(bf16[128,1664]{1,0:T(8,128)(2,1)S(1)} %collective-permute-done.1.refs_2_.g2) | copy-start | bytes 1277956
  26.9 0.8 copy-start.5
  32.6 6.3 %copy-start.7 = (bf16[128,4096]{1,0:T(8,128)(2,1)}, bf16[128,4096]{1,0:T(8,128)(2,1)S(1)}, u32[]{:S(2)}) copy-start(bf16[128,4096]{1,0:T(8,128)(2,1)S(1)} %collective-permute-done.6.g_ref) | copy-start | bytes 3145732
  38.9 7.9 %copy-start.6 = (bf16[1,128,4096]{2,1,0:T(8,128)(2,1)S(1)}, bf16[1,128,4096]{2,1,0:T(8,128)(2,1)}, u32[]{:S(2)}) copy-start(bf16[1,128,4096]{2,1,0:T(8,128)(2,1)} %param.6) | copy-start | bytes 3145732
  38.9 60.1 %all-to-all-start.2 = ((bf16[32,40,1536]{2,1,0:T(8,128)(2,1)}), bf16[32,40,1536]{2,1,0:T(8,128)(2,1)}, u32[]{:S(2)}, u32[]{:S(2)}) async-start(bf16[32,40,1536]{2,1,0:T(8,128)(2,1)} %bitcast.42), calls=%async_computation.2 | async-start | bytes 7864320 | tf_op jit(solution)/shard_map/all_to_all | solution.py:325
  46.9 31.7 %copy-start.2 = (bf16[128,2560]{1,0:T(8,128)(2,1)}, bf16[128,2560]{1,0:T(8,128)(2,1)S(1)}, u32[]{:S(2)}) copy-start(bf16[128,2560]{1,0:T(8,128)(2,1)S(1)} %slice.21.g0.refs_4_) | copy-start | bytes 1966084
  46.9 17.4 %collective-permute-start.3 = (bf16[128,2560]{1,0:T(8,128)(2,1)S(1)}, bf16[128,2560]{1,0:T(8,128)(2,1)S(1)}, u32[]{:S(2)}, u32[]{:S(2)}) collective-permute-start(bf16[128,2560]{1,0:T(8,128)(2,1)S(1)} %slice.21.g0.refs_4_), channel_id=1, source_target_pairs={{0,1},{1,2},{2,3},{3,0},{4,5},{5,6},{6,7},{7,4},{8,9},{9,10},{10,1... | collective-permute-start | bytes 1966088 | tf_op jit(solution)/shard_map/ppermute | solution.py:284
  47.8 16.5 %collective-permute-start.4 = (bf16[128,2560]{1,0:T(8,128)(2,1)S(1)}, bf16[128,2560]{1,0:T(8,128)(2,1)S(1)}, u32[]{:S(2)}, u32[]{:S(2)}) collective-permute-start(bf16[128,2560]{1,0:T(8,128)(2,1)S(1)} %slice.21.g0.refs_4_), channel_id=1, source_target_pairs={{0,3},{1,0},{2,1},{3,2},{4,7},{5,4},{6,5},{7,6},{8,11},{9,8},{10,9... | collective-permute-start | bytes 1966088 | tf_op jit(solution)/shard_map/ppermute | solution.py:284
  49.6 28.9 %collective-permute-start.5 = (bf16[128,2560]{1,0:T(8,128)(2,1)S(1)}, bf16[128,2560]{1,0:T(8,128)(2,1)S(1)}, u32[]{:S(2)}, u32[]{:S(2)}) collective-permute-start(bf16[128,2560]{1,0:T(8,128)(2,1)S(1)} %slice.21.g0.refs_4_), channel_id=1, source_target_pairs={{0,2},{1,3},{2,0},{3,1},{4,6},{5,7},{6,4},{7,5},{8,10},{9,11},{10,... | collective-permute-start | bytes 1966088 | tf_op jit(solution)/shard_map/ppermute | solution.py:284
  64.3 14.2 %copy-start.9 = (bf16[128,2560]{1,0:T(8,128)(2,1)}, bf16[128,2560]{1,0:T(8,128)(2,1)S(1)}, u32[]{:S(2)}) copy-start(bf16[128,2560]{1,0:T(8,128)(2,1)S(1)} %collective-permute-done.3.g1.refs_5_) | copy-start | bytes 1966084
  64.3 14.2 %copy-start.10 = (bf16[128,2560]{1,0:T(8,128)(2,1)}, bf16[128,2560]{1,0:T(8,128)(2,1)S(1)}, u32[]{:S(2)}) copy-start(bf16[128,2560]{1,0:T(8,128)(2,1)S(1)} %collective-permute-done.4.g2.refs_6_) | copy-start | bytes 1966084
  78.5 0.9 copy-start.11
  99.0 4.9 %copy-start = (bf16[1,1280,768]{2,1,0:T(8,128)(2,1)S(1)}, bf16[1,1280,768]{2,1,0:T(8,128)(2,1)}, u32[]{:S(2)}) copy-start(bf16[1,1280,768]{2,1,0:T(8,128)(2,1)} %param.11) | copy-start | bytes 5898244
  99.0 93.3 %all-to-all-start = ((bf16[32,40,2560]{2,1,0:T(8,128)(2,1)}), bf16[32,40,2560]{2,1,0:T(8,128)(2,1)}, u32[]{:S(2)}, u32[]{:S(2)}) async-start(bf16[32,40,2560]{2,1,0:T(8,128)(2,1)} %bitcast.41), calls=%async_computation | async-start | bytes 13107200 | tf_op jit(solution)/shard_map/all_to_all | solution.py:325
  106.2 41.3 %collective-permute-start.12 = (bf16[512,1024]{1,0:T(8,128)(2,1)}, bf16[512,1024]{1,0:T(8,128)(2,1)S(1)}, u32[]{:S(2)}, u32[]{:S(2)}) collective-permute-start(bf16[512,1024]{1,0:T(8,128)(2,1)} %refs_4_), channel_id=1, source_target_pairs={{0,1},{1,2},{2,3},{3,0},{4,5},{5,6},{6,7},{7,4},{8,9},{9,10},{10,1... | collective-permute-start | bytes 3145736 | tf_op jit(solution)/shard_map/ppermute | solution.py:284
  107.1 41.4 %collective-permute-start.13 = (bf16[512,1024]{1,0:T(8,128)(2,1)}, bf16[512,1024]{1,0:T(8,128)(2,1)}, u32[]{:S(2)}, u32[]{:S(2)}) collective-permute-start(bf16[512,1024]{1,0:T(8,128)(2,1)} %refs_4_), channel_id=1, source_target_pairs={{0,3},{1,0},{2,1},{3,2},{4,7},{5,4},{6,5},{7,6},{8,11},{9,8},{10,9... | collective-permute-start | bytes 3145736 | tf_op jit(solution)/shard_map/ppermute | solution.py:284
  111.4 26.6 %collective-permute-start.7 = (bf16[128,1024]{1,0:T(8,128)(2,1)}, bf16[128,1024]{1,0:T(8,128)(2,1)S(1)}, u32[]{:S(2)}, u32[]{:S(2)}) collective-permute-start(bf16[128,1024]{1,0:T(8,128)(2,1)} %get-tuple-element.33), channel_id=1, source_target_pairs={{0,1},{1,2},{2,3},{3,0},{4,5},{5,6},{6,7},{7,4},{8,9},{9,10},{10,1... | collective-permute-start | bytes 786440 | tf_op jit(solution)/shard_map/ppermute | solution.py:284
  111.4 27.8 %collective-permute-start.8 = (bf16[128,1024]{1,0:T(8,128)(2,1)}, bf16[128,1024]{1,0:T(8,128)(2,1)S(1)}, u32[]{:S(2)}, u32[]{:S(2)}) collective-permute-start(bf16[128,1024]{1,0:T(8,128)(2,1)} %get-tuple-element.34), channel_id=1, source_target_pairs={{0,3},{1,0},{2,1},{3,2},{4,7},{5,4},{6,5},{7,6},{8,11},{9,8},{10,9... | collective-permute-start | bytes 786440 | tf_op jit(solution)/shard_map/ppermute | solution.py:284
  114.0 29.7 %collective-permute-start.9 = (bf16[128,1024]{1,0:T(8,128)(2,1)}, bf16[128,1024]{1,0:T(8,128)(2,1)S(1)}, u32[]{:S(2)}, u32[]{:S(2)}) collective-permute-start(bf16[128,1024]{1,0:T(8,128)(2,1)} %get-tuple-element.35), channel_id=1, source_target_pairs={{0,2},{1,3},{2,0},{3,1},{4,6},{5,7},{6,4},{7,5},{8,10},{9,11},{10,... | collective-permute-start | bytes 786440 | tf_op jit(solution)/shard_map/ppermute | solution.py:284
  126.9 11.1 %copy-start.8 = (bf16[512,1024]{1,0:T(8,128)(2,1)S(1)}, bf16[512,1024]{1,0:T(8,128)(2,1)}, u32[]{:S(2)}) copy-start(bf16[512,1024]{1,0:T(8,128)(2,1)} %shard_map.101.refs_0_) | copy-start | bytes 3145732
  126.9 16.9 %copy-start.13 = (bf16[128,1024]{1,0:T(8,128)(2,1)S(1)}, bf16[128,1024]{1,0:T(8,128)(2,1)}, u32[]{:S(2)}) copy-start(bf16[128,1024]{1,0:T(8,128)(2,1)} %get-tuple-element.45) | copy-start | bytes 786436
  138.0 13.6 %collective-permute-start.10 = (bf16[512,1024]{1,0:T(8,128)(2,1)S(1)}, bf16[512,1024]{1,0:T(8,128)(2,1)}, u32[]{:S(2)}, u32[]{:S(2)}) collective-permute-start(bf16[512,1024]{1,0:T(8,128)(2,1)S(1)} %copy-done.8), channel_id=1, source_target_pairs={{0,32},{32,0},{1,33},{33,1},{2,34},{34,2},{3,35},{35,3},{4,36},{36... | collective-permute-start | bytes 3145736 | tf_op jit(solution)/shard_map/ppermute | solution.py:284
  146.7 16.3 %collective-permute-start.11 = (bf16[512,1024]{1,0:T(8,128)(2,1)}, bf16[512,1024]{1,0:T(8,128)(2,1)}, u32[]{:S(2)}, u32[]{:S(2)}) collective-permute-start(bf16[512,1024]{1,0:T(8,128)(2,1)} %constant_dynamic-update-slice_fusion.refs_2_), channel_id=1, source_target_pairs={{0,32},{32,0},{1,33},{33,1},{2,34},{34,2},{3,35},{35,3},{4,36},{36... | collective-permute-start | bytes 3145736 | tf_op jit(solution)/shard_map/ppermute | solution.py:284
  147.5 15.5 %copy-start.12 = (bf16[512,1024]{1,0:T(8,128)(2,1)}, bf16[512,1024]{1,0:T(8,128)(2,1)S(1)}, u32[]{:S(2)}) copy-start(bf16[512,1024]{1,0:T(8,128)(2,1)S(1)} %collective-permute-done.12.refs_5_) | copy-start | bytes 3145732
  147.6 14.9 %collective-permute-start.14 = (bf16[256,1024]{1,0:T(8,128)(2,1)S(1)}, bf16[256,1024]{1,0:T(8,128)(2,1)}, u32[]{:S(2)}, u32[]{:S(2)}) collective-permute-start(bf16[256,1024]{1,0:T(8,128)(2,1)S(1)} %slice.23), channel_id=1, source_target_pairs={{0,1},{1,2},{2,3},{3,0},{4,5},{5,6},{6,7},{7,4},{8,9},{9,10},{10,1... | collective-permute-start | bytes 1572872 | tf_op jit(solution)/shard_map/ppermute | solution.py:284
  149.6 13.4 %collective-permute-start.15 = (bf16[256,1024]{1,0:T(8,128)(2,1)S(1)}, bf16[256,1024]{1,0:T(8,128)(2,1)}, u32[]{:S(2)}, u32[]{:S(2)}) collective-permute-start(bf16[256,1024]{1,0:T(8,128)(2,1)S(1)} %slice.24), channel_id=1, source_target_pairs={{0,3},{1,0},{2,1},{3,2},{4,7},{5,4},{6,5},{7,6},{8,11},{9,8},{10,9... | collective-permute-start | bytes 1572872 | tf_op jit(solution)/shard_map/ppermute | solution.py:284
  174.3 37.4 %collective-permute-start.16 = (bf16[512,1024]{1,0:T(8,128)(2,1)S(1)}, bf16[512,1024]{1,0:T(8,128)(2,1)S(1)}, u32[]{:S(2)}, u32[]{:S(2)}) collective-permute-start(bf16[512,1024]{1,0:T(8,128)(2,1)S(1)} %constant_dynamic-slice_fusion), channel_id=1, source_target_pairs={{0,4},{4,0},{1,5},{5,1},{2,6},{6,2},{3,7},{7,3},{8,12},{12,8},{9,1... | collective-permute-start | bytes 3145736 | tf_op jit(solution)/shard_map/ppermute | solution.py:284
  204.5 23.1 %all-to-all-start.3 = ((f32[128,1,128]{2,1,0:T(1,128)}), f32[128,1,128]{2,1,0:T(1,128)S(1)}, u32[]{:S(2)}, u32[]{:S(2)}) async-start(f32[128,1,128]{2,1,0:T(1,128)} %bitcast.50), calls=%async_computation.3 | async-start | bytes 131072 | tf_op jit(solution)/shard_map/all_to_all | solution.py:370
  213.5 15.1 %collective-permute-start.17 = (bf16[128,1024]{1,0:T(8,128)(2,1)S(1)}, bf16[128,1024]{1,0:T(8,128)(2,1)}, u32[]{:S(2)}, u32[]{:S(2)}) collective-permute-start(bf16[128,1024]{1,0:T(8,128)(2,1)S(1)} %get-tuple-element.56), channel_id=1, source_target_pairs={{0,8},{8,16},{16,24},{24,0},{1,9},{9,17},{17,25},{25,1},{2,10},{10... | collective-permute-start | bytes 786440 | tf_op jit(solution)/shard_map/ppermute | solution.py:284
  214.9 13.7 %collective-permute-start.18 = (bf16[128,1024]{1,0:T(8,128)(2,1)S(1)}, bf16[128,1024]{1,0:T(8,128)(2,1)}, u32[]{:S(2)}, u32[]{:S(2)}) collective-permute-start(bf16[128,1024]{1,0:T(8,128)(2,1)S(1)} %get-tuple-element.55), channel_id=1, source_target_pairs={{0,24},{8,0},{16,8},{24,16},{1,25},{9,1},{17,9},{25,17},{2,26},{10... | collective-permute-start | bytes 786440 | tf_op jit(solution)/shard_map/ppermute | solution.py:284
  216.2 11.7 %copy-start.14 = (s32[1,128,8]{1,2,0:T(8,128)S(1)}, s32[1,128,8]{1,2,0:T(8,128)}, u32[]{:S(2)}) copy-start(s32[1,128,8]{1,2,0:T(8,128)} %param.7) | copy-start | bytes 12292
  216.2 12.9 %collective-permute-start.19 = (bf16[128,1024]{1,0:T(8,128)(2,1)S(1)}, bf16[128,1024]{1,0:T(8,128)(2,1)}, u32[]{:S(2)}, u32[]{:S(2)}) collective-permute-start(bf16[128,1024]{1,0:T(8,128)(2,1)S(1)} %get-tuple-element.54), channel_id=1, source_target_pairs={{0,16},{8,24},{16,0},{24,8},{1,17},{9,25},{17,1},{25,9},{2,18},{10... | collective-permute-start | bytes 786440 | tf_op jit(solution)/shard_map/ppermute | solution.py:284
